TPU v7x, 512 devices: a whole 4x8x8 slice. The times are simulated.
512 devices in a mesh: grp: 8 (over z_hi, core), blk: 64 (over y, x, z_lo).
Axes of the slice: x: 4, y: 8, z: 8 (z_hi: 4, z_lo: 2; z = z_hi * 2 + z_lo), core: 2. Of those that a mesh axis runs over, the one named last changes fastest.
Arguments:
- ints: bfloat16 [64, 1536, 4096], P('blk', 'grp'), may hold values from -1 to 1
- occ_energy: float32 [400], replicated, may hold values from -2 to -0.3
- occ_window: int32 [64], replicated, may hold values from 0 to 399, as said below
- virt_energy: float32 [1536], replicated, may hold values from 0.3 to 3
Outputs:
- virt_density: float32 [1536, 192], P(('grp', 'blk'))
- pair_energy: float32 [64, 4], P('blk')
Inputs may be any that keep to these rules, and one draw needn't show every extreme that they name: `occ_window`: distinct indices into occ_energy.
All inputs are finite; a program needn't handle non-finite values.
Results may differ from a plain program's by a relative error of at most 0.0003.
Values may be sent and summed in bfloat16 or wider, within the bound.
No kernel may reach another device: no remote copies, remote signals or barrier semaphores. Data moves between devices by JAX's collectives and lax.ppermute only.
A program may use at most 64 MiB of HBM per device.

v0:
```python
import functools

import jax
import jax.numpy as jnp
from jax import lax
from jax.sharding import Mesh
from jax.sharding import PartitionSpec as P

STEPS = 4
GRP = ("grp_0", "grp_1")
GRP_BLK = ("grp_0", "grp_1", "blk")


def from_partner(block, axis, stride):
    count = lax.axis_size(axis)
    route = []
    for low in range(count):
        high = low | 1 << stride
        if high != low and high < count:
            route += [(low, high), (high, low)]
    return lax.ppermute(block, axis, route)


def shifted(shard, axis, by):
    peers = lax.axis_size(axis)
    return lax.ppermute(shard, axis, [(i, (i + by) % peers) for i in range(peers)])


def cut_along(shard, dim, peers):
    before, after = (shard.shape[:dim], shard.shape[dim + 1 :])
    return jnp.moveaxis(shard.reshape(*before, peers, -1, *after), dim, 0)


def sent_and_summed(shard, axis, dim):
    tiles = cut_along(shard, dim, lax.axis_size(axis))
    arrived = lax.all_to_all(tiles, axis, split_axis=0, concat_axis=0, tiled=True)
    return arrived.sum(axis=0)


def by_axis(shard, axes):
    return functools.reduce(lax.psum, axes, shard)


def lookup_many(values_in, where_at):
    positions = jnp.arange(values_in.shape[0], dtype=jnp.int32)
    matches = positions[None, :] == where_at[:, None]
    return jnp.sum(
        jnp.where(matches, values_in[None, :], jnp.zeros_like(values_in)[None, :]), axis=1
    )


def local(ints, occ_energy, occ_window, virt_energy):
    occ_dev = ints.shape[0]
    virt_width = ints.shape[1]
    occ_count = occ_window.shape[0]
    block_count = occ_count // occ_dev
    group_index = lax.axis_index(GRP)
    block_index = lax.axis_index("blk")
    mirror_index = group_index + 1 - 2 * (group_index % 2)
    virt_own = lax.dynamic_slice_in_dim(virt_energy, group_index * virt_width, virt_width)
    virt_mirror = lax.dynamic_slice_in_dim(virt_energy, mirror_index * virt_width, virt_width)
    virt_cols = jnp.concatenate([virt_own, virt_mirror])
    local_rows = jnp.arange(occ_dev, dtype=jnp.int32)
    occ_own = lookup_many(occ_energy, lookup_many(occ_window, block_index * occ_dev + local_rows))

    def accumulate(cycle_step, current, density, energies):
        partner_block = (block_index - cycle_step) % block_count
        partner_ids = partner_block * occ_dev + local_rows
        occ_pair = lookup_many(occ_energy, lookup_many(occ_window, partner_ids))
        diag_tile = jnp.einsum("rap,tbp->rtab", ints, current, preferred_element_type=jnp.float32)
        far_rows = from_partner(current, GRP, 0)
        off_tile = jnp.einsum("rap,tbp->rtab", ints, far_rows, preferred_element_type=jnp.float32)
        coupling = jnp.concatenate([diag_tile, off_tile], axis=3)
        denominator = (
            virt_own[None, None, :, None]
            + virt_cols[None, None, None, :]
            - occ_own[:, None, None, None]
            - occ_pair[None, :, None, None]
        )
        amplitude = coupling / denominator
        density = density + jnp.einsum(
            "rtab,rtcb->ac",
            amplitude,
            amplitude,
            precision=lax.Precision.HIGHEST,
            preferred_element_type=jnp.float32,
        )
        pair_value = -jnp.sum(amplitude * coupling, axis=(2, 3)) / (virt_width * virt_width)
        start = jnp.asarray(cycle_step, jnp.int32) * occ_dev
        energies = lax.dynamic_update_slice(
            energies, pair_value, (jnp.asarray(0, jnp.int32), start)
        )
        return (density, energies)

    density, energies = accumulate(
        0,
        ints,
        jnp.zeros((virt_width, virt_width), jnp.float32),
        jnp.zeros((occ_dev, STEPS * occ_dev), jnp.float32),
    )

    def advance(cycle_step, state_tuple):
        current, density_sum, energy_list = state_tuple
        current = shifted(current, "blk", 1)
        density_sum, energy_list = accumulate(cycle_step, current, density_sum, energy_list)
        return (current, density_sum, energy_list)

    state_tuple = lax.fori_loop(1, STEPS, advance, (ints, density, energies))
    shares = sent_and_summed(state_tuple[1], "blk", 0) / (occ_count * STEPS * occ_dev)
    totals = by_axis(state_tuple[2], GRP)
    return (shares, totals)


def solution(mesh):
    finer = Mesh(mesh.devices.reshape(4, 2, mesh.shape["blk"]), ("grp_0", "grp_1", "blk"))
    placed = (P("blk", GRP, None), P(), P(), P())
    return jax.shard_map(
        local,
        mesh=finer,
        in_specs=placed,
        out_specs=(P(GRP_BLK, None), P("blk", None)),
        check_vma=False,
    )
```

profile of v0, /device:TPU:1, one launch (start us, length us, event | category | flops | bytes accessed | tf_op | source)
XLA Modules:
  0.0 214.7 jit_solution(9921922154497954648)
XLA Ops:
  0.6 8.8 %collective-permute-start.2 = (bf16[1,192,4096]{2,1,0:T(8,128)(2,1)}, bf16[1,192,4096]{2,1,0:T(8,128)(2,1)S(1)}, u32[]{:S(2)}, u32[]{:S(2)}) collective-permute-start(bf16[1,192,4096]{2,1,0:T(8,128)(2,1)} %param.6), channel_id=1, source_target_pairs={{0,64},{64,0},{128,192},{192,128},{256,320},{320,256},{384,448},{4... | collective-permute-start | bytes 4718600 | tf_op jit(solution)/shard_map/ppermute | solution.py:21
  9.5 2.8 %copy.8 = bf16[1,192,4096]{2,1,0:T(8,128)(2,1)} copy(bf16[1,192,4096]{2,1,0:T(8,128)(2,1)} %param.6) | data formatting | bytes 3145728
  12.3 0.8 fusion.41
  13.2 0.7 fusion.38
  13.9 1.9 select_reduce_fusion.2
  16.4 0.6 fusion.20
  17.0 2.0 fusion.33
  19.7 0.6 dynamic_update_slice.16
  20.3 1.8 fusion.26
  22.1 168.0 %while.21 = (s32[]{:T(128)}, bf16[1,192,4096]{2,1,0:T(8,128)(2,1)}, f32[192,192]{1,0:T(8,128)S(1)}, f32[1,4]{1,0:T(1,128)}, bf16[1,192,4096]{2,1,0:T(8,128)(2,1)...) while((s32[]{:T(128)}, bf16[1,192,4096]{2,1,0:T(8,128)(2,1)}, ...), condition=%wide.region_9.10_spmd, body=%wide.region_5.9_spmd.sunk | while | flops 774772096 | bytes 23206852 | solution.py:108
  22.1 1.9 collective-permute-start
  24.0 40.4 %collective-permute-done = bf16[1,192,4096]{2,1,0:T(8,128)(2,1)S(1)} collective-permute-done((bf16[1,192,4096]{2,1,0:T(8,128)(2,1)}, bf16[1,192,4096]{2,1,0:T(8,128)(2,1)S(1)}, u32[]{:S(2)}, u32[]{:S(2)}) %collective-permute-start) | collective-permute-done | bytes 1572896 | tf_op jit(solution)/shard_map/while/body/eval_jaxpr/ppermute | solution.py:26
  64.4 2.7 %collective-permute-start.1 = (bf16[1,192,4096]{2,1,0:T(8,128)(2,1)S(1)}, bf16[1,192,4096]{2,1,0:T(8,128)(2,1)}, u32[]{:S(2)}, u32[]{:S(2)}) collective-permute-start(bf16[1,192,4096]{2,1,0:T(8,128)(2,1)S(1)} %collective-permute-done), channel_id=1, source_target_pairs={{0,64},{64,0},{128,192},{192,128},{256,320},{320,256},{384,448},{4... | collective-permute-start | bytes 4718600 | tf_op jit(solution)/shard_map/while/body/eval_jaxpr/ppermute | solution.py:21
  67.1 0.7 fusion.58
  67.8 1.3 select_reduce_fusion.4
  69.1 1.2 copy.16
  70.3 0.6 fusion.57
  70.9 2.0 fusion.56
  72.9 2.0 fusion.59
  75.5 1.9 convolution_add_fusion.2
  77.5 0.6 copy-done.4
  78.1 1.9 collective-permute-start
  80.0 40.4 %collective-permute-done = bf16[1,192,4096]{2,1,0:T(8,128)(2,1)S(1)} collective-permute-done((bf16[1,192,4096]{2,1,0:T(8,128)(2,1)}, bf16[1,192,4096]{2,1,0:T(8,128)(2,1)S(1)}, u32[]{:S(2)}, u32[]{:S(2)}) %collective-permute-start) | collective-permute-done | bytes 1572896 | tf_op jit(solution)/shard_map/while/body/eval_jaxpr/ppermute | solution.py:26
  120.4 2.7 %collective-permute-start.1 = (bf16[1,192,4096]{2,1,0:T(8,128)(2,1)S(1)}, bf16[1,192,4096]{2,1,0:T(8,128)(2,1)}, u32[]{:S(2)}, u32[]{:S(2)}) collective-permute-start(bf16[1,192,4096]{2,1,0:T(8,128)(2,1)S(1)} %collective-permute-done), channel_id=1, source_target_pairs={{0,64},{64,0},{128,192},{192,128},{256,320},{320,256},{384,448},{4... | collective-permute-start | bytes 4718600 | tf_op jit(solution)/shard_map/while/body/eval_jaxpr/ppermute | solution.py:21
  123.1 0.7 fusion.58
  123.8 1.3 select_reduce_fusion.4
  125.1 1.2 copy.16
  126.3 0.6 fusion.57
  126.9 2.0 fusion.56
  128.9 2.0 fusion.59
  131.5 1.9 convolution_add_fusion.2
  133.5 0.6 copy-done.4
  134.1 1.9 collective-permute-start
  136.0 40.4 %collective-permute-done = bf16[1,192,4096]{2,1,0:T(8,128)(2,1)S(1)} collective-permute-done((bf16[1,192,4096]{2,1,0:T(8,128)(2,1)}, bf16[1,192,4096]{2,1,0:T(8,128)(2,1)S(1)}, u32[]{:S(2)}, u32[]{:S(2)}) %collective-permute-start) | collective-permute-done | bytes 1572896 | tf_op jit(solution)/shard_map/while/body/eval_jaxpr/ppermute | solution.py:26
  176.4 2.7 %collective-permute-start.1 = (bf16[1,192,4096]{2,1,0:T(8,128)(2,1)S(1)}, bf16[1,192,4096]{2,1,0:T(8,128)(2,1)}, u32[]{:S(2)}, u32[]{:S(2)}) collective-permute-start(bf16[1,192,4096]{2,1,0:T(8,128)(2,1)S(1)} %collective-permute-done), channel_id=1, source_target_pairs={{0,64},{64,0},{128,192},{192,128},{256,320},{320,256},{384,448},{4... | collective-permute-start | bytes 4718600 | tf_op jit(solution)/shard_map/while/body/eval_jaxpr/ppermute | solution.py:21
  179.1 0.7 fusion.58
  179.8 1.3 select_reduce_fusion.4
  181.1 1.2 copy.16
  182.3 0.6 fusion.57
  182.9 2.0 fusion.56
  184.9 2.0 fusion.59
  187.5 1.9 convolution_add_fusion.2
  189.5 0.6 copy-done.4
  190.1 0.8 reshape.756
  190.8 4.6 %all-to-all-start = ((f32[64,3,192]{2,1,0:T(4,128)}), f32[64,3,192]{2,1,0:T(4,128)S(1)}, u32[]{:S(2)}, u32[]{:S(2)}) async-start(f32[64,3,192]{2,1,0:T(4,128)} %reshape.756), calls=%async_computation | async-start | bytes 524288 | tf_op jit(solution)/shard_map/all_to_all | solution.py:36
  195.4 13.5 %psum.14 = f32[1,4]{1,0:T(1,128)S(1)} all-reduce(f32[1,4]{1,0:T(1,128)} %get-tuple-element.349), channel_id=1, replica_groups=mesh['grp_0'=4,'grp_1'=2,'blk'=64] {'grp_0'}, use_global_device_ids=true, to_apply=%region_11.12 | all-reduce | flops 4 | bytes 32 | tf_op jit(solution)/shard_map/psum | solution.py:41
  208.9 5.1 %psum.15 = f32[1,4]{1,0:T(1,128)} all-reduce(f32[1,4]{1,0:T(1,128)S(1)} %psum.14), channel_id=1, replica_groups=mesh['grp_0'=4,'grp_1'=2,'blk'=64] {'grp_1'}, use_global_device_ids=true, to_apply=%region_12.13 | all-reduce | flops 4 | bytes 32 | tf_op jit(solution)/shard_map/psum | solution.py:41
  214.1 0.6 broadcast_multiply_fusion
  (26 shorter events, 1.1 us)
Async XLA Ops:
  0.6 15.8 %collective-permute-start.2 = (bf16[1,192,4096]{2,1,0:T(8,128)(2,1)}, bf16[1,192,4096]{2,1,0:T(8,128)(2,1)S(1)}, u32[]{:S(2)}, u32[]{:S(2)}) collective-permute-start(bf16[1,192,4096]{2,1,0:T(8,128)(2,1)} %param.6), channel_id=1, source_target_pairs={{0,64},{64,0},{128,192},{192,128},{256,320},{320,256},{384,448},{4... | collective-permute-start | bytes 4718600 | tf_op jit(solution)/shard_map/ppermute | solution.py:21
  9.4 3.8 %copy-start.2 = (s32[64]{0:T(128)S(1)}, s32[64]{0:T(128)}, u32[]{:S(2)}) copy-start(s32[64]{0:T(128)} %param.8) | copy-start | bytes 772
  9.5 4.5 %copy-start.1 = (f32[400]{0:T(512)S(1)}, f32[400]{0:T(512)}, u32[]{:S(2)}) copy-start(f32[400]{0:T(512)} %param.7) | copy-start | bytes 4804
  9.5 6.4 %copy-start = (bf16[1,192,4096]{2,1,0:T(8,128)(2,1)S(1)}, bf16[1,192,4096]{2,1,0:T(8,128)(2,1)}, u32[]{:S(2)}) copy-start(bf16[1,192,4096]{2,1,0:T(8,128)(2,1)} %param.6) | copy-start | bytes 4718596
  22.1 42.3 %collective-permute-start = (bf16[1,192,4096]{2,1,0:T(8,128)(2,1)}, bf16[1,192,4096]{2,1,0:T(8,128)(2,1)S(1)}, u32[]{:S(2)}, u32[]{:S(2)}) collective-permute-start(bf16[1,192,4096]{2,1,0:T(8,128)(2,1)} %get-tuple-element.463), channel_id=1, source_target_pairs={{0,1},{1,2},{2,3},{3,4},{4,5},{5,6},{6,7},{7,8},{8,9},{9,10},{10,1... | collective-permute-start | bytes 4718600 | tf_op jit(solution)/shard_map/while/body/eval_jaxpr/ppermute | solution.py:26
  64.4 6.5 %collective-permute-start.1 = (bf16[1,192,4096]{2,1,0:T(8,128)(2,1)S(1)}, bf16[1,192,4096]{2,1,0:T(8,128)(2,1)}, u32[]{:S(2)}, u32[]{:S(2)}) collective-permute-start(bf16[1,192,4096]{2,1,0:T(8,128)(2,1)S(1)} %collective-permute-done), channel_id=1, source_target_pairs={{0,64},{64,0},{128,192},{192,128},{256,320},{320,256},{384,448},{4... | collective-permute-start | bytes 4718600 | tf_op jit(solution)/shard_map/while/body/eval_jaxpr/ppermute | solution.py:21
  72.9 4.4 %copy-start.3 = (f32[1,4]{1,0:T(1,128)S(1)}, f32[1,4]{1,0:T(1,128)}, u32[]{:S(2)}) copy-start(f32[1,4]{1,0:T(1,128)} %get-tuple-element.465) | copy-start | bytes 52 | tf_op jit(solution)/shard_map/while
  77.5 0.6 copy-start.4
  78.1 42.3 %collective-permute-start = (bf16[1,192,4096]{2,1,0:T(8,128)(2,1)}, bf16[1,192,4096]{2,1,0:T(8,128)(2,1)S(1)}, u32[]{:S(2)}, u32[]{:S(2)}) collective-permute-start(bf16[1,192,4096]{2,1,0:T(8,128)(2,1)} %get-tuple-element.463), channel_id=1, source_target_pairs={{0,1},{1,2},{2,3},{3,4},{4,5},{5,6},{6,7},{7,8},{8,9},{9,10},{10,1... | collective-permute-start | bytes 4718600 | tf_op jit(solution)/shard_map/while/body/eval_jaxpr/ppermute | solution.py:26
  120.4 6.5 %collective-permute-start.1 = (bf16[1,192,4096]{2,1,0:T(8,128)(2,1)S(1)}, bf16[1,192,4096]{2,1,0:T(8,128)(2,1)}, u32[]{:S(2)}, u32[]{:S(2)}) collective-permute-start(bf16[1,192,4096]{2,1,0:T(8,128)(2,1)S(1)} %collective-permute-done), channel_id=1, source_target_pairs={{0,64},{64,0},{128,192},{192,128},{256,320},{320,256},{384,448},{4... | collective-permute-start | bytes 4718600 | tf_op jit(solution)/shard_map/while/body/eval_jaxpr/ppermute | solution.py:21
  128.9 4.4 %copy-start.3 = (f32[1,4]{1,0:T(1,128)S(1)}, f32[1,4]{1,0:T(1,128)}, u32[]{:S(2)}) copy-start(f32[1,4]{1,0:T(1,128)} %get-tuple-element.465) | copy-start | bytes 52 | tf_op jit(solution)/shard_map/while
  133.5 0.6 copy-start.4
  134.1 42.3 %collective-permute-start = (bf16[1,192,4096]{2,1,0:T(8,128)(2,1)}, bf16[1,192,4096]{2,1,0:T(8,128)(2,1)S(1)}, u32[]{:S(2)}, u32[]{:S(2)}) collective-permute-start(bf16[1,192,4096]{2,1,0:T(8,128)(2,1)} %get-tuple-element.463), channel_id=1, source_target_pairs={{0,1},{1,2},{2,3},{3,4},{4,5},{5,6},{6,7},{7,8},{8,9},{9,10},{10,1... | collective-permute-start | bytes 4718600 | tf_op jit(solution)/shard_map/while/body/eval_jaxpr/ppermute | solution.py:26
  176.4 6.5 %collective-permute-start.1 = (bf16[1,192,4096]{2,1,0:T(8,128)(2,1)S(1)}, bf16[1,192,4096]{2,1,0:T(8,128)(2,1)}, u32[]{:S(2)}, u32[]{:S(2)}) collective-permute-start(bf16[1,192,4096]{2,1,0:T(8,128)(2,1)S(1)} %collective-permute-done), channel_id=1, source_target_pairs={{0,64},{64,0},{128,192},{192,128},{256,320},{320,256},{384,448},{4... | collective-permute-start | bytes 4718600 | tf_op jit(solution)/shard_map/while/body/eval_jaxpr/ppermute | solution.py:21
  184.9 4.4 %copy-start.3 = (f32[1,4]{1,0:T(1,128)S(1)}, f32[1,4]{1,0:T(1,128)}, u32[]{:S(2)}) copy-start(f32[1,4]{1,0:T(1,128)} %get-tuple-element.465) | copy-start | bytes 52 | tf_op jit(solution)/shard_map/while
  189.5 0.6 copy-start.4
  190.8 23.2 %all-to-all-start = ((f32[64,3,192]{2,1,0:T(4,128)}), f32[64,3,192]{2,1,0:T(4,128)S(1)}, u32[]{:S(2)}, u32[]{:S(2)}) async-start(f32[64,3,192]{2,1,0:T(4,128)} %reshape.756), calls=%async_computation | async-start | bytes 524288 | tf_op jit(solution)/shard_map/all_to_all | solution.py:36
where the time goes:
time: 215 us
  waiting for transfers between devices  121 us (56%)
  starting transfers between devices  27.2 us (13%)
  blocking collectives  18.6 us (9%)
  other arithmetic  17.3 us (8%)
  matrix products  16.3 us (8%)
  local copies, waits for them, and re-layouts  10.7 us (5%)
    ppermute x3, waiting for transfers between devices, shifted(): lax.ppermute(shard, axis, [(i, (i + by) % peers) for i in range(peers)])  121 us
    psum x2, blocking collectives, by_axis(): return functools.reduce(lax.psum, axes, shard)  18.6 us
    ppermute x4, starting transfers between devices, from_partner(): return lax.ppermute(block, axis, route)  16.9 us
    reduce_sum x8, other arithmetic, lookup_many(): jnp.sum(jnp.where(matches, values_in[None, :], jnp.zeros_like(values_in)[...  8.63 us
    reduce_sum x4, other arithmetic, accumulate(): jnp.sum(amplitude * coupling, axis=(2, 3))  7.87 us
    dot_general x4, matrix products, accumulate(): jnp.einsum('rtab,rtcb->ac', amplitude, amplitude, precision=lax.Precision...  7.34 us
    dot_general x4, matrix products, accumulate(): jnp.einsum('rap,tbp->rtab', ints, far_rows, preferred_element_type=jnp.fl...  6.57 us
    ppermute x3, starting transfers between devices, shifted(): lax.ppermute(shard, axis, [(i, (i + by) % peers) for i in range(peers)])  5.74 us
  transfers between devices with their start and end apart: 8, of which 3 were waited for; matrix products, arithmetic and copies ran while one was open for 8% of the time, Pallas kernels for 0%

commit v1 on v0

v1 whole, which is shorter than its diff:
```python
import functools

import jax
import jax.numpy as jnp
from jax import lax
from jax.experimental import pallas as pl
from jax.experimental.pallas import tpu as pltpu
from jax.sharding import Mesh
from jax.sharding import PartitionSpec as P

STEPS = 4
CHUNKS = 4
GRP = ("z_hi", "core")
VMEM_BYTES = 24 * 1024 * 1024


def shifted(shard, axis, by):
    peers = lax.axis_size(axis)
    return lax.ppermute(shard, axis, [(i, (i + by) % peers) for i in range(peers)])


def nt_dot(left, right):
    return lax.dot_general(
        left, right, (((1,), (1,)), ((), ())), preferred_element_type=jnp.float32
    )


def self_product(amps):
    head = amps.astype(jnp.bfloat16)
    rest = (amps - head.astype(jnp.float32)).astype(jnp.bfloat16)
    return nt_dot(head, head) + nt_dot(head, rest) + nt_dot(rest, head)


def amplitude_of(coupling, virt_col, virt_row, occ_row, occ_partner):
    return coupling / (virt_col + virt_row - occ_row - occ_partner)


def own_kernel(levels, own, own_mirror, virt_col, virt_rows, density, energy):
    total = jnp.zeros(density.shape, jnp.float32)
    value = jnp.zeros((1, 1), jnp.float32)
    for half, cols in enumerate((own, own_mirror)):
        coupling = nt_dot(own[...], cols[...])
        amp = amplitude_of(
            coupling, virt_col[...], virt_rows[half : half + 1, :], levels[0], levels[0]
        )
        value = value + jnp.sum(amp * coupling, keepdims=True)
        total = total + self_product(amp)
    density[...] = total
    energy[...] = jnp.broadcast_to(value, energy.shape)


def pair_list(own, own_mirror, near, far, far_mirror):
    return (
        (own, far),
        (own, far_mirror),
        (near, own),
        (near, own_mirror),
        (near, far),
        (near, far_mirror),
    )


def chunk_kernel(first, own, own_mirror, near, far, far_mirror, *rest):
    sums = rest[-1]
    for at, (rows, cols) in enumerate(pair_list(own, own_mirror, near, far, far_mirror)):
        part = nt_dot(rows[...], cols[...])
        sums[at] = part if first else rest[0][at] + part


def last_kernel(
    levels,
    own,
    own_mirror,
    near,
    far,
    far_mirror,
    sums,
    virt_col,
    virt_rows,
    density_in,
    energy_in,
    density_out,
    energy_out,
    held,
):
    pairs = pair_list(own, own_mirror, near, far, far_mirror)
    total = density_in[...]
    values = []
    for at, (rows, cols) in enumerate(pairs):
        coupling = sums[at] + nt_dot(rows[...], cols[...])
        left = levels[0] if at < 2 else levels[1]
        right = levels[0] if at in (2, 3) else levels[2]
        amp = amplitude_of(
            coupling, virt_col[...], virt_rows[at % 2 : at % 2 + 1, :], left, right
        )
        values.append(jnp.sum(amp * coupling, keepdims=True))
        total = total + self_product(amp)
    own_two = values[0] + values[1]
    next_one = values[2] + values[3]
    next_three = values[4] + values[5]
    lane = lax.broadcasted_iota(jnp.int32, energy_out.shape, 1)
    picked = jnp.where(lane == 0, energy_in[...], 0.0)
    picked = jnp.where(lane == 1, own_two, picked)
    picked = jnp.where(lane == 2, next_one, picked)
    picked = jnp.where(lane == 3, next_three, picked)
    energy_out[...] = picked
    lanes = held.shape[2]
    panels = held.shape[0]
    width = total.shape[1]
    for panel in range(panels):
        part = total[:, panel * lanes : min(width, (panel + 1) * lanes)]
        if part.shape[1] < lanes:
            held[panel] = jnp.zeros(held.shape[1:], jnp.float32)
        held[panel, :, : part.shape[1]] = part
    peers, span = density_out.shape
    rows_each = width // peers
    for row in range(rows_each):
        for panel in range(panels):
            at = (row * panels + panel) * lanes
            density_out[:, at : at + lanes] = held[panel, pl.Slice(row, peers, rows_each), :]


def lookup_many(values_in, where_at):
    positions = jnp.arange(values_in.shape[0], dtype=jnp.int32)
    matches = positions[None, :] == where_at[:, None]
    return jnp.sum(
        jnp.where(matches, values_in[None, :], jnp.zeros_like(values_in)[None, :]), axis=1
    )


def call(kernel, out_shape, operands, smem=0, scratch=(), flops=0, moved=0):
    vmem = pl.BlockSpec(memory_space=pltpu.VMEM)
    specs = [pl.BlockSpec(memory_space=pltpu.SMEM)] * smem
    specs += [vmem] * (len(operands) - smem)
    outs = jax.tree.map(lambda _: vmem, out_shape)
    return pl.pallas_call(
        kernel,
        out_shape=out_shape,
        in_specs=specs,
        out_specs=outs,
        scratch_shapes=list(scratch),
        compiler_params=pltpu.CompilerParams(vmem_limit_bytes=VMEM_BYTES),
        cost_estimate=pl.CostEstimate(flops=flops, bytes_accessed=moved, transcendentals=0),
    )(*operands)


def local(ints, occ_energy, occ_window, virt_energy):
    own = ints[0]
    width, depth = own.shape
    piece = depth // CHUNKS
    occ_count = occ_window.shape[0]
    peers = lax.axis_size("blk")
    group_index = lax.axis_index(GRP)
    block_index = lax.axis_index("blk")
    mirror_index = group_index + 1 - 2 * (group_index % 2)

    cut = [own[:, c * piece : (c + 1) * piece] for c in range(CHUNKS)]
    far = [shifted(part, "blk", 2) for part in cut]
    near = [shifted(part, "blk", -1) for part in cut]
    own_mirror = shifted(own, "core", 1)
    far_mirror = [shifted(part, "core", 1) for part in far]

    virt_own = lax.dynamic_slice_in_dim(virt_energy, group_index * width, width)
    virt_mirror = lax.dynamic_slice_in_dim(virt_energy, mirror_index * width, width)
    virt_rows = jnp.stack([virt_own, virt_mirror])
    virt_col = virt_own[:, None]
    wanted = (block_index + jnp.array([0, 1, -2], jnp.int32)) % peers
    levels = lookup_many(occ_energy, lookup_many(occ_window, wanted))

    square = jax.ShapeDtypeStruct((width, width), jnp.float32)
    line = jax.ShapeDtypeStruct((1, 128), jnp.float32)
    density, energy = call(
        own_kernel,
        (square, line),
        (levels, own, own_mirror, virt_col, virt_rows),
        smem=1,
        flops=4 * width * width * depth,
        moved=4 * width * depth,
    )
    sums = None
    six = jax.ShapeDtypeStruct((6, width, width), jnp.float32)
    for c in range(CHUNKS):
        blocks = (
            cut[c],
            own_mirror[:, c * piece : (c + 1) * piece],
            near[c],
            far[c],
            far_mirror[c],
        )
        if c < CHUNKS - 1:
            sums = call(
                functools.partial(chunk_kernel, sums is None),
                six,
                blocks + (() if sums is None else (sums,)),
                flops=12 * width * width * piece,
                moved=10 * width * piece,
            )
    rows_each = width // peers
    stride = -(-width // 128) * 128
    spread, energies = call(
        last_kernel,
        (jax.ShapeDtypeStruct((peers, rows_each * stride), jnp.float32), line),
        (levels,) + blocks + (sums, virt_col, virt_rows, density, energy),
        smem=1,
        scratch=(pltpu.VMEM((stride // 128, width, 128), jnp.float32),),
        flops=12 * width * width * piece,
        moved=10 * width * piece,
    )
    arrived = lax.all_to_all(spread, "blk", 0, 0, tiled=True)
    passed = shifted(energies[:, 2:4], "blk", 1)
    pair = jnp.stack([energies[:, 0], passed[:, 0], energies[:, 1], passed[:, 1]], axis=1)
    totals = lax.psum(lax.psum(pair, "core"), "z_hi") * (-1.0 / (width * width))
    share = arrived.sum(axis=0).reshape(rows_each, stride)[:, :width]
    return share * (1.0 / (occ_count * STEPS)), totals


def solution(mesh):
    peers = mesh.shape["blk"]
    finer = Mesh(mesh.devices.reshape(-1, 2, peers), ("z_hi", "core", "blk"))
    placed = (P("blk", GRP, None), P(), P(), P())
    return jax.shard_map(
        local,
        mesh=finer,
        in_specs=placed,
        out_specs=(P(GRP + ("blk",), None), P("blk", None)),
        check_vma=False,
    )
```

time: 215 us -> 106 us (0.49)
  waiting for transfers between devices: 121 us -> 12.7 us
  starting transfers between devices: 27.2 us -> 52.4 us
  matrix products: 16.3 us -> 0 us
  other arithmetic: 17.3 us -> 4.26 us
  Pallas kernels: 0 us -> 10.7 us
  local copies, waits for them, and re-layouts: 10.7 us -> 5.59 us
    ppermute x3 -> x14, waiting for transfers between devices: 121 us -> 12.7 us  [shifted(): lax.ppermute(shard, axis, [(i, (i + by) % peers) for i in range(peers)])]
    ppermute x3 -> x14, starting transfers between devices: 5.74 us -> 45.7 us  [shifted(): lax.ppermute(shard, axis, [(i, (i + by) % peers) for i in range(peers)])]
    ppermute x4 -> x0, starting transfers between devices: 16.9 us -> none  [from_partner(): return lax.ppermute(block, axis, route)]
    dot_general x12 -> x0, matrix products: 16.3 us -> none  [the longest x4 7.34 us: accumulate(): jnp.einsum('rtab,rtcb->ac', amplitude, amplitude, precision=lax.Precision...]
    pallas_call x0 -> x5, Pallas kernels: none -> 10.7 us  [call(): pl.pallas_call(kernel, out_shape=out_shape, in_specs=specs, out_specs=out...]
    reduce_sum x8 -> x2, other arithmetic: 8.63 us -> 0.37 us  [lookup_many(): jnp.sum(jnp.where(matches, values_in[None, :], jnp.zeros_like(values_in)[...]
    reduce_sum x5 -> x1, other arithmetic: 7.96 us -> 0.15 us  [local(): share = arrived.sum(axis=0).reshape(rows_each, stride)[:, :width]]
    while x15 -> x0, local copies, waits for them, and re-layouts: 5.27 us -> none
  transfers between devices with their start and end apart: 8 -> 15, of which waited for: 3 -> 5; matrix products, arithmetic and copies ran while one was open for 8% -> 7% of each run, Pallas kernels for 0% -> 8%
where the time goes in v1:
time: 106 us; the launch traced here: 105 us
  starting transfers between devices  52.4 us (49%)
  blocking collectives  18.1 us (17%)
  waiting for transfers between devices  12.7 us (12%)
  Pallas kernels  10.7 us (10%)
  local copies, waits for them, and re-layouts  5.59 us (5%)
  other arithmetic  4.26 us (4%)
    ppermute x14, starting transfers between devices, shifted(): lax.ppermute(shard, axis, [(i, (i + by) % peers) for i in range(peers)])  45.7 us
    psum x2, blocking collectives, local(): totals = lax.psum(lax.psum(pair, 'core'), 'z_hi') * (-1.0 / (width * width))  18.1 us
    ppermute x14, waiting for transfers between devices, shifted(): lax.ppermute(shard, axis, [(i, (i + by) % peers) for i in range(peers)])  12.7 us
    pallas_call x5, Pallas kernels, call(): pl.pallas_call(kernel, out_shape=out_shape, in_specs=specs, out_specs=out...  10.7 us
    all_to_all x1, starting transfers between devices, local(): arrived = lax.all_to_all(spread, 'blk', 0, 0, tiled=True)  6.72 us
    another operation x1, other arithmetic, local(): jnp.stack([energies[:, 0], passed[:, 0], energies[:, 1], passed[:, 1]], a...  2.61 us
  transfers between devices with their start and end apart: 15, of which 5 were waited for; matrix products, arithmetic and copies ran while one was open for 7% of the time, Pallas kernels for 8%

profile of v1, /device:TPU:1, one launch (start us, length us, event | category | flops | bytes accessed | tf_op | source)
XLA Modules:
  0.0 104.7 jit_solution(18011590063379409844)
XLA Ops:
  0.6 0.0 copy-start.5
  0.7 8.9 %collective-permute-start = (bf16[192,4096]{1,0:T(8,128)(2,1)}, bf16[192,4096]{1,0:T(8,128)(2,1)S(1)}, u32[]{:S(2)}, u32[]{:S(2)}) collective-permute-start(bf16[192,4096]{1,0:T(8,128)(2,1)} %bitcast.5), channel_id=1, source_target_pairs={{0,64},{64,0},{1,65},{65,1},{2,66},{66,2},{3,67},{67,3},{4,68},{68... | collective-permute-start | bytes 4718600 | tf_op jit(solution)/shard_map/ppermute | solution.py:19
  9.6 1.5 %fusion.2 = (bf16[192,1024]{1,0:T(8,128)(2,1)S(1)}, bf16[192,1024]{1,0:T(8,128)(2,1)S(1)}, bf16[192,1024]{1,0:T(8,128)(2,1)S(1)}, bf16[192,1024]{1,0:T(8,128)(2,1)S(1)}) fusion(bf16[192,4096]{1,0:T(8,128)(2,1)} %bitcast.6), kind=kLoop, calls=%fused_computation.13 | loop fusion | bytes 3145728 | tf_op jit(solution)/shard_map/slice | solution.py:157
  11.1 1.9 %collective-permute-start.11 = (bf16[192,1024]{1,0:T(8,128)(2,1)S(1)}, bf16[192,1024]{1,0:T(8,128)(2,1)}, u32[]{:S(2)}, u32[]{:S(2)}) collective-permute-start(bf16[192,1024]{1,0:T(8,128)(2,1)S(1)} %get-tuple-element.14.own), channel_id=1, source_target_pairs={{0,2},{1,3},{2,4},{3,5},{4,6},{5,7},{6,8},{7,9},{8,10},{9,11},{10,... | collective-permute-start | bytes 1179656 | tf_op jit(solution)/shard_map/ppermute | solution.py:19
  13.0 3.7 %collective-permute-start.10 = (bf16[192,1024]{1,0:T(8,128)(2,1)S(1)}, bf16[192,1024]{1,0:T(8,128)(2,1)}, u32[]{:S(2)}, u32[]{:S(2)}) collective-permute-start(bf16[192,1024]{1,0:T(8,128)(2,1)S(1)} %get-tuple-element.14.own), channel_id=1, source_target_pairs={{0,63},{1,0},{2,1},{3,2},{4,3},{5,4},{6,5},{7,6},{8,7},{9,8},{10,9... | collective-permute-start | bytes 1179656 | tf_op jit(solution)/shard_map/ppermute | solution.py:19
  16.7 1.9 %collective-permute-start.8 = (bf16[192,1024]{1,0:T(8,128)(2,1)S(1)}, bf16[192,1024]{1,0:T(8,128)(2,1)}, u32[]{:S(2)}, u32[]{:S(2)}) collective-permute-start(bf16[192,1024]{1,0:T(8,128)(2,1)S(1)} %get-tuple-element.15.own), channel_id=1, source_target_pairs={{0,2},{1,3},{2,4},{3,5},{4,6},{5,7},{6,8},{7,9},{8,10},{9,11},{10,... | collective-permute-start | bytes 1179656 | tf_op jit(solution)/shard_map/ppermute | solution.py:19
  18.7 6.0 %collective-permute-start.7 = (bf16[192,1024]{1,0:T(8,128)(2,1)S(1)}, bf16[192,1024]{1,0:T(8,128)(2,1)S(1)}, u32[]{:S(2)}, u32[]{:S(2)}) collective-permute-start(bf16[192,1024]{1,0:T(8,128)(2,1)S(1)} %get-tuple-element.15.own), channel_id=1, source_target_pairs={{0,63},{1,0},{2,1},{3,2},{4,3},{5,4},{6,5},{7,6},{8,7},{9,8},{10,9... | collective-permute-start | bytes 1179656 | tf_op jit(solution)/shard_map/ppermute | solution.py:19
  24.7 2.4 %collective-permute-done.11.far = bf16[192,1024]{1,0:T(8,128)(2,1)} collective-permute-done((bf16[192,1024]{1,0:T(8,128)(2,1)S(1)}, bf16[192,1024]{1,0:T(8,128)(2,1)}, u32[]{:S(2)}, u32[]{:S(2)}) %collective-permute-start.11) | collective-permute-done | bytes 393248 | tf_op jit(solution)/shard_map/ppermute | solution.py:19
  27.1 1.9 %collective-permute-start.5 = (bf16[192,1024]{1,0:T(8,128)(2,1)S(1)}, bf16[192,1024]{1,0:T(8,128)(2,1)}, u32[]{:S(2)}, u32[]{:S(2)}) collective-permute-start(bf16[192,1024]{1,0:T(8,128)(2,1)S(1)} %get-tuple-element.16.own), channel_id=1, source_target_pairs={{0,2},{1,3},{2,4},{3,5},{4,6},{5,7},{6,8},{7,9},{8,10},{9,11},{10,... | collective-permute-start | bytes 1179656 | tf_op jit(solution)/shard_map/ppermute | solution.py:19
  29.1 1.9 %collective-permute-start.2 = (bf16[192,1024]{1,0:T(8,128)(2,1)S(1)}, bf16[192,1024]{1,0:T(8,128)(2,1)}, u32[]{:S(2)}, u32[]{:S(2)}) collective-permute-start(bf16[192,1024]{1,0:T(8,128)(2,1)S(1)} %get-tuple-element.17.own), channel_id=1, source_target_pairs={{0,2},{1,3},{2,4},{3,5},{4,6},{5,7},{6,8},{7,9},{8,10},{9,11},{10,... | collective-permute-start | bytes 1179656 | tf_op jit(solution)/shard_map/ppermute | solution.py:19
  31.0 4.5 %collective-permute-done.8.far = bf16[192,1024]{1,0:T(8,128)(2,1)} collective-permute-done((bf16[192,1024]{1,0:T(8,128)(2,1)S(1)}, bf16[192,1024]{1,0:T(8,128)(2,1)}, u32[]{:S(2)}, u32[]{:S(2)}) %collective-permute-start.8) | collective-permute-done | bytes 393248 | tf_op jit(solution)/shard_map/ppermute | solution.py:19
  35.6 3.1 %collective-permute-start.12 = (bf16[192,1024]{1,0:T(8,128)(2,1)}, bf16[192,1024]{1,0:T(8,128)(2,1)}, u32[]{:S(2)}, u32[]{:S(2)}) collective-permute-start(bf16[192,1024]{1,0:T(8,128)(2,1)} %collective-permute-done.11.far), channel_id=1, source_target_pairs={{0,64},{64,0},{1,65},{65,1},{2,66},{66,2},{3,67},{67,3},{4,68},{68... | collective-permute-start | bytes 1179656 | tf_op jit(solution)/shard_map/ppermute | solution.py:19
  38.7 0.9 fusion.3
  39.5 0.2 select_reduce_fusion.1
  39.7 0.2 select_reduce_fusion.levels
  39.9 0.0 collective-permute-done.7.near
  39.9 0.8 copy-done.1
  40.7 1.9 %collective-permute-start.4 = (bf16[192,1024]{1,0:T(8,128)(2,1)S(1)}, bf16[192,1024]{1,0:T(8,128)(2,1)}, u32[]{:S(2)}, u32[]{:S(2)}) collective-permute-start(bf16[192,1024]{1,0:T(8,128)(2,1)S(1)} %get-tuple-element.16.own), channel_id=1, source_target_pairs={{0,63},{1,0},{2,1},{3,2},{4,3},{5,4},{6,5},{7,6},{8,7},{9,8},{10,9... | collective-permute-start | bytes 1179656 | tf_op jit(solution)/shard_map/ppermute | solution.py:19
  42.6 0.9 collective-permute-done.5.far
  43.5 4.1 %collective-permute-start.9 = (bf16[192,1024]{1,0:T(8,128)(2,1)}, bf16[192,1024]{1,0:T(8,128)(2,1)}, u32[]{:S(2)}, u32[]{:S(2)}) collective-permute-start(bf16[192,1024]{1,0:T(8,128)(2,1)} %collective-permute-done.8.far), channel_id=1, source_target_pairs={{0,64},{64,0},{1,65},{65,1},{2,66},{66,2},{3,67},{67,3},{4,68},{68... | collective-permute-start | bytes 1179656 | tf_op jit(solution)/shard_map/ppermute | solution.py:19
  47.6 4.3 %collective-permute-done.2.far = bf16[192,1024]{1,0:T(8,128)(2,1)} collective-permute-done((bf16[192,1024]{1,0:T(8,128)(2,1)S(1)}, bf16[192,1024]{1,0:T(8,128)(2,1)}, u32[]{:S(2)}, u32[]{:S(2)}) %collective-permute-start.2) | collective-permute-done | bytes 393248 | tf_op jit(solution)/shard_map/ppermute | solution.py:19
  51.9 3.2 %collective-permute-start.6 = (bf16[192,1024]{1,0:T(8,128)(2,1)}, bf16[192,1024]{1,0:T(8,128)(2,1)}, u32[]{:S(2)}, u32[]{:S(2)}) collective-permute-start(bf16[192,1024]{1,0:T(8,128)(2,1)} %collective-permute-done.5.far), channel_id=1, source_target_pairs={{0,64},{64,0},{1,65},{65,1},{2,66},{66,2},{3,67},{67,3},{4,68},{68... | collective-permute-start | bytes 1179656 | tf_op jit(solution)/shard_map/ppermute | solution.py:19
  55.1 0.1 copy.13.virt_col
  55.3 1.9 %collective-permute-start.1 = (bf16[192,1024]{1,0:T(8,128)(2,1)S(1)}, bf16[192,1024]{1,0:T(8,128)(2,1)S(1)}, u32[]{:S(2)}, u32[]{:S(2)}) collective-permute-start(bf16[192,1024]{1,0:T(8,128)(2,1)S(1)} %get-tuple-element.17.own), channel_id=1, source_target_pairs={{0,63},{1,0},{2,1},{3,2},{4,3},{5,4},{6,5},{7,6},{8,7},{9,8},{10,9... | collective-permute-start | bytes 1179656 | tf_op jit(solution)/shard_map/ppermute | solution.py:19
  57.2 0.0 collective-permute-done.own_mirror
  57.2 1.9 %collective-permute-start.3 = (bf16[192,1024]{1,0:T(8,128)(2,1)}, bf16[192,1024]{1,0:T(8,128)(2,1)S(1)}, u32[]{:S(2)}, u32[]{:S(2)}) collective-permute-start(bf16[192,1024]{1,0:T(8,128)(2,1)} %collective-permute-done.2.far), channel_id=1, source_target_pairs={{0,64},{64,0},{1,65},{65,1},{2,66},{66,2},{3,67},{67,3},{4,68},{68... | collective-permute-start | bytes 1179656 | tf_op jit(solution)/shard_map/ppermute | solution.py:19
  59.1 0.1 fusion.1
  59.3 2.1 %shard_map.68.rest_0_ = f32[6,192,192]{2,1,0:T(8,128)S(1)} custom-call(bf16[192,1024]{1,0:T(8,128)(2,1)S(1)} %get-tuple-element.14.own, bf16[192,1024]{1,0:T(8,128)(2,1)S(1)} %get-tuple-element.10.own_mirror, bf16[192,1024]{1,0:T(8,128)(2,1)} %collective-permute-done.10.near, bf16[192,1024]{1,0:T(8,128)(2,1)} %collective-permute-done.11.far, ...), custom_call_target="tpu_custom_call" | custom-call | flops 452984832 | bytes 1966080 | tf_op jit(solution)/shard_map/pallas_call | solution.py:136
  61.4 0.0 collective-permute-done.9.far_mirror
  61.4 1.9 %shard_map.69.rest_0_ = f32[6,192,192]{2,1,0:T(8,128)S(1)} custom-call(bf16[192,1024]{1,0:T(8,128)(2,1)S(1)} %get-tuple-element.15.own, bf16[192,1024]{1,0:T(8,128)(2,1)S(1)} %get-tuple-element.11.own_mirror, bf16[192,1024]{1,0:T(8,128)(2,1)S(1)} %copy-done.2, bf16[192,1024]{1,0:T(8,128)(2,1)} %collective-permute-done.8.far, ...), custom_call_target="tpu_custom_call" | custom-call | flops 452984832 | bytes 1966080 | tf_op jit(solution)/shard_map/pallas_call | solution.py:136
  63.3 0.0 collective-permute-done.4.near
  63.3 0.0 copy-start
  63.3 2.1 %shard_map.70.sums = f32[6,192,192]{2,1,0:T(8,128)S(1)} custom-call(bf16[192,1024]{1,0:T(8,128)(2,1)S(1)} %get-tuple-element.16.own, bf16[192,1024]{1,0:T(8,128)(2,1)S(1)} %get-tuple-element.12.own_mirror, bf16[192,1024]{1,0:T(8,128)(2,1)} %collective-permute-done.4.near, bf16[192,1024]{1,0:T(8,128)(2,1)} %collective-permute-done.5.far, ...), custom_call_target="tpu_custom_call" | custom-call | flops 452984832 | bytes 1966080 | tf_op jit(solution)/shard_map/pallas_call | solution.py:136
  65.5 1.9 %shard_map.71 = (f32[192,192]{1,0:T(8,128)S(1)}, f32[1,128]{1,0:T(1,128)S(1)}) custom-call(f32[3]{0:T(128)S(1)} %select_reduce_fusion.levels, bf16[192,4096]{1,0:T(8,128)(2,1)S(1)} %bitcast.7, bf16[192,4096]{1,0:T(8,128)(2,1)S(1)} %collective-permute-done.own_mirror, f32[192,1]{1,0:T(8,128)S(1)} %copy.13.virt_col, f32[2,192]{1,0:T(2,128)S(1)} %pad_maximum_fusion.virt_rows), custom_call_target="tpu_custom_call" | custom-call | flops 603979776 | bytes 3145728 | tf_op jit(solution)/shard_map/pallas_call | solution.py:136
  67.4 0.5 collective-permute-done.1.near
  67.9 2.8 %shard_map.72 = (f32[64,768]{1,0:T(8,128)S(1)}, f32[1,128]{1,0:T(1,128)S(1)}) custom-call(f32[3]{0:T(128)S(1)} %select_reduce_fusion.levels, bf16[192,1024]{1,0:T(8,128)(2,1)S(1)} %get-tuple-element.17.own, bf16[192,1024]{1,0:T(8,128)(2,1)S(1)} %get-tuple-element.13.own_mirror, bf16[192,1024]{1,0:T(8,128)(2,1)S(1)} %collective-permute-done.1.near, ...), custom_call_target="tpu_custom_call" | custom-call | flops 452984832 | bytes 1966080 | tf_op jit(solution)/shard_map/pallas_call | solution.py:136
  70.6 0.1 slice.52
  70.7 0.6 fusion.4
  71.4 3.1 %collective-permute-start.13 = (f32[1,2]{1,0:T(1,128)S(1)}, f32[1,2]{1,0:T(1,128)S(1)}, u32[]{:S(2)}, u32[]{:S(2)}) collective-permute-start(f32[1,2]{1,0:T(1,128)S(1)} %slice.52), channel_id=1, source_target_pairs={{0,1},{1,2},{2,3},{3,4},{4,5},{5,6},{6,7},{7,8},{8,9},{9,10},{10,1... | collective-permute-start | bytes 32 | tf_op jit(solution)/shard_map/ppermute | solution.py:19
  74.5 0.9 copy.14
  75.4 6.7 %all-to-all-start = ((f32[64,1,768]{2,1,0:T(1,128)}), f32[64,1,768]{2,1,0:T(1,128)S(1)}, u32[]{:S(2)}, u32[]{:S(2)}) async-start(f32[64,1,768]{2,1,0:T(1,128)} %copy.14), calls=%async_computation | async-start | bytes 393216 | tf_op jit(solution)/shard_map/all_to_all | solution.py:209
  82.2 0.6 fusion.5
  82.7 2.6 %pad_maximum_fusion.1 = f32[1,4]{1,0:T(1,128)S(1)} fusion(f32[1,1]{1,0:T(1,128)} %get-tuple-element.23, f32[1,1]{1,0:T(1,128)} %get-tuple-element.21, f32[1,1]{1,0:T(1,128)} %get-tuple-element.22, f32[1,1]{1,0:T(1,128)} %get-tuple-element.20), kind=kLoop, calls=%fused_computation.10 | loop fusion | flops 12 | bytes 32 | tf_op jit(solution)/shard_map/stack | solution.py:211
  85.3 3.5 %psum.14 = f32[1,4]{1,0:T(1,128)S(1)} all-reduce(f32[1,4]{1,0:T(1,128)S(1)} %pad_maximum_fusion.1), channel_id=1, replica_groups=mesh['z_hi'=4,'core'=2,'blk'=64] {'core'}, use_global_device_ids=true, to_apply=%region_3.4 | all-reduce | flops 4 | bytes 32 | tf_op jit(solution)/shard_map/psum | solution.py:212
  88.8 14.6 %psum.15 = f32[1,4]{1,0:T(1,128)S(1)} all-reduce(f32[1,4]{1,0:T(1,128)S(1)} %psum.14), channel_id=1, replica_groups=mesh['z_hi'=4,'core'=2,'blk'=64] {'z_hi'}, use_global_device_ids=true, to_apply=%region_4.5 | all-reduce | flops 4 | bytes 32 | tf_op jit(solution)/shard_map/psum | solution.py:212
  103.4 0.5 broadcast_multiply_fusion
  103.9 0.1 reduce_sum.29
  104.1 0.6 slice_multiply_fusion
  (18 shorter events, 0.1 us)
Async XLA Ops:
  0.6 30.4 %copy-start.5 = (s32[3]{0:T(128)S(1)}, s32[3]{0:T(128)}, u32[]{:S(2)}) copy-start(s32[3]{0:T(128)} %constant.58.clone) | copy-start | bytes 40
  0.6 38.9 %copy-start.4 = (s32[64]{0:T(128)S(1)}, s32[64]{0:T(128)}, u32[]{:S(2)}) copy-start(s32[64]{0:T(128)} %param.7) | copy-start | bytes 772
  0.7 39.0 %copy-start.3 = (f32[400]{0:T(512)S(1)}, f32[400]{0:T(512)}, u32[]{:S(2)}) copy-start(f32[400]{0:T(512)} %param.6) | copy-start | bytes 4804
  0.7 56.5 %collective-permute-start = (bf16[192,4096]{1,0:T(8,128)(2,1)}, bf16[192,4096]{1,0:T(8,128)(2,1)S(1)}, u32[]{:S(2)}, u32[]{:S(2)}) collective-permute-start(bf16[192,4096]{1,0:T(8,128)(2,1)} %bitcast.5), channel_id=1, source_target_pairs={{0,64},{64,0},{1,65},{65,1},{2,66},{66,2},{3,67},{67,3},{4,68},{68... | collective-permute-start | bytes 4718600 | tf_op jit(solution)/shard_map/ppermute | solution.py:19
  11.1 16.1 %collective-permute-start.11 = (bf16[192,1024]{1,0:T(8,128)(2,1)S(1)}, bf16[192,1024]{1,0:T(8,128)(2,1)}, u32[]{:S(2)}, u32[]{:S(2)}) collective-permute-start(bf16[192,1024]{1,0:T(8,128)(2,1)S(1)} %get-tuple-element.14.own), channel_id=1, source_target_pairs={{0,2},{1,3},{2,4},{3,5},{4,6},{5,7},{6,8},{7,9},{8,10},{9,11},{10,... | collective-permute-start | bytes 1179656 | tf_op jit(solution)/shard_map/ppermute | solution.py:19
  13.0 16.0 %collective-permute-start.10 = (bf16[192,1024]{1,0:T(8,128)(2,1)S(1)}, bf16[192,1024]{1,0:T(8,128)(2,1)}, u32[]{:S(2)}, u32[]{:S(2)}) collective-permute-start(bf16[192,1024]{1,0:T(8,128)(2,1)S(1)} %get-tuple-element.14.own), channel_id=1, source_target_pairs={{0,63},{1,0},{2,1},{3,2},{4,3},{5,4},{6,5},{7,6},{8,7},{9,8},{10,9... | collective-permute-start | bytes 1179656 | tf_op jit(solution)/shard_map/ppermute | solution.py:19
  16.7 18.8 %collective-permute-start.8 = (bf16[192,1024]{1,0:T(8,128)(2,1)S(1)}, bf16[192,1024]{1,0:T(8,128)(2,1)}, u32[]{:S(2)}, u32[]{:S(2)}) collective-permute-start(bf16[192,1024]{1,0:T(8,128)(2,1)S(1)} %get-tuple-element.15.own), channel_id=1, source_target_pairs={{0,2},{1,3},{2,4},{3,5},{4,6},{5,7},{6,8},{7,9},{8,10},{9,11},{10,... | collective-permute-start | bytes 1179656 | tf_op jit(solution)/shard_map/ppermute | solution.py:19
  18.7 21.2 %collective-permute-start.7 = (bf16[192,1024]{1,0:T(8,128)(2,1)S(1)}, bf16[192,1024]{1,0:T(8,128)(2,1)S(1)}, u32[]{:S(2)}, u32[]{:S(2)}) collective-permute-start(bf16[192,1024]{1,0:T(8,128)(2,1)S(1)} %get-tuple-element.15.own), channel_id=1, source_target_pairs={{0,63},{1,0},{2,1},{3,2},{4,3},{5,4},{6,5},{7,6},{8,7},{9,8},{10,9... | collective-permute-start | bytes 1179656 | tf_op jit(solution)/shard_map/ppermute | solution.py:19
  27.1 16.3 %collective-permute-start.5 = (bf16[192,1024]{1,0:T(8,128)(2,1)S(1)}, bf16[192,1024]{1,0:T(8,128)(2,1)}, u32[]{:S(2)}, u32[]{:S(2)}) collective-permute-start(bf16[192,1024]{1,0:T(8,128)(2,1)S(1)} %get-tuple-element.16.own), channel_id=1, source_target_pairs={{0,2},{1,3},{2,4},{3,5},{4,6},{5,7},{6,8},{7,9},{8,10},{9,11},{10,... | collective-permute-start | bytes 1179656 | tf_op jit(solution)/shard_map/ppermute | solution.py:19
  29.1 22.8 %collective-permute-start.2 = (bf16[192,1024]{1,0:T(8,128)(2,1)S(1)}, bf16[192,1024]{1,0:T(8,128)(2,1)}, u32[]{:S(2)}, u32[]{:S(2)}) collective-permute-start(bf16[192,1024]{1,0:T(8,128)(2,1)S(1)} %get-tuple-element.17.own), channel_id=1, source_target_pairs={{0,2},{1,3},{2,4},{3,5},{4,6},{5,7},{6,8},{7,9},{8,10},{9,11},{10,... | collective-permute-start | bytes 1179656 | tf_op jit(solution)/shard_map/ppermute | solution.py:19
  35.6 19.7 %collective-permute-start.12 = (bf16[192,1024]{1,0:T(8,128)(2,1)}, bf16[192,1024]{1,0:T(8,128)(2,1)}, u32[]{:S(2)}, u32[]{:S(2)}) collective-permute-start(bf16[192,1024]{1,0:T(8,128)(2,1)} %collective-permute-done.11.far), channel_id=1, source_target_pairs={{0,64},{64,0},{1,65},{65,1},{2,66},{66,2},{3,67},{67,3},{4,68},{68... | collective-permute-start | bytes 1179656 | tf_op jit(solution)/shard_map/ppermute | solution.py:19
  39.9 0.8 copy-start.1
  40.7 22.7 %collective-permute-start.4 = (bf16[192,1024]{1,0:T(8,128)(2,1)S(1)}, bf16[192,1024]{1,0:T(8,128)(2,1)}, u32[]{:S(2)}, u32[]{:S(2)}) collective-permute-start(bf16[192,1024]{1,0:T(8,128)(2,1)S(1)} %get-tuple-element.16.own), channel_id=1, source_target_pairs={{0,63},{1,0},{2,1},{3,2},{4,3},{5,4},{6,5},{7,6},{8,7},{9,8},{10,9... | collective-permute-start | bytes 1179656 | tf_op jit(solution)/shard_map/ppermute | solution.py:19
  43.5 17.9 %collective-permute-start.9 = (bf16[192,1024]{1,0:T(8,128)(2,1)}, bf16[192,1024]{1,0:T(8,128)(2,1)}, u32[]{:S(2)}, u32[]{:S(2)}) collective-permute-start(bf16[192,1024]{1,0:T(8,128)(2,1)} %collective-permute-done.8.far), channel_id=1, source_target_pairs={{0,64},{64,0},{1,65},{65,1},{2,66},{66,2},{3,67},{67,3},{4,68},{68... | collective-permute-start | bytes 1179656 | tf_op jit(solution)/shard_map/ppermute | solution.py:19
  51.9 11.4 %collective-permute-start.6 = (bf16[192,1024]{1,0:T(8,128)(2,1)}, bf16[192,1024]{1,0:T(8,128)(2,1)}, u32[]{:S(2)}, u32[]{:S(2)}) collective-permute-start(bf16[192,1024]{1,0:T(8,128)(2,1)} %collective-permute-done.5.far), channel_id=1, source_target_pairs={{0,64},{64,0},{1,65},{65,1},{2,66},{66,2},{3,67},{67,3},{4,68},{68... | collective-permute-start | bytes 1179656 | tf_op jit(solution)/shard_map/ppermute | solution.py:19
  55.3 12.6 %collective-permute-start.1 = (bf16[192,1024]{1,0:T(8,128)(2,1)S(1)}, bf16[192,1024]{1,0:T(8,128)(2,1)S(1)}, u32[]{:S(2)}, u32[]{:S(2)}) collective-permute-start(bf16[192,1024]{1,0:T(8,128)(2,1)S(1)} %get-tuple-element.17.own), channel_id=1, source_target_pairs={{0,63},{1,0},{2,1},{3,2},{4,3},{5,4},{6,5},{7,6},{8,7},{9,8},{10,9... | collective-permute-start | bytes 1179656 | tf_op jit(solution)/shard_map/ppermute | solution.py:19
  57.2 10.7 %collective-permute-start.3 = (bf16[192,1024]{1,0:T(8,128)(2,1)}, bf16[192,1024]{1,0:T(8,128)(2,1)S(1)}, u32[]{:S(2)}, u32[]{:S(2)}) collective-permute-start(bf16[192,1024]{1,0:T(8,128)(2,1)} %collective-permute-done.2.far), channel_id=1, source_target_pairs={{0,64},{64,0},{1,65},{65,1},{2,66},{66,2},{3,67},{67,3},{4,68},{68... | collective-permute-start | bytes 1179656 | tf_op jit(solution)/shard_map/ppermute | solution.py:19
  59.3 2.1 %copy-start.2 = (bf16[192,1024]{1,0:T(8,128)(2,1)S(1)}, bf16[192,1024]{1,0:T(8,128)(2,1)}, u32[]{:S(2)}) copy-start(bf16[192,1024]{1,0:T(8,128)(2,1)} %copy-done.1) | copy-start | bytes 1179652
  63.3 2.2 %copy-start = (bf16[1,192,4096]{2,1,0:T(8,128)(2,1)S(1)}, bf16[1,192,4096]{2,1,0:T(8,128)(2,1)}, u32[]{:S(2)}) copy-start(bf16[1,192,4096]{2,1,0:T(8,128)(2,1)} %param.5) | copy-start | bytes 4718596
  71.4 10.8 %collective-permute-start.13 = (f32[1,2]{1,0:T(1,128)S(1)}, f32[1,2]{1,0:T(1,128)S(1)}, u32[]{:S(2)}, u32[]{:S(2)}) collective-permute-start(f32[1,2]{1,0:T(1,128)S(1)} %slice.52), channel_id=1, source_target_pairs={{0,1},{1,2},{2,3},{3,4},{4,5},{5,6},{6,7},{7,8},{8,9},{9,10},{10,1... | collective-permute-start | bytes 32 | tf_op jit(solution)/shard_map/ppermute | solution.py:19
  75.4 28.5 %all-to-all-start = ((f32[64,1,768]{2,1,0:T(1,128)}), f32[64,1,768]{2,1,0:T(1,128)S(1)}, u32[]{:S(2)}, u32[]{:S(2)}) async-start(f32[64,1,768]{2,1,0:T(1,128)} %copy.14), calls=%async_computation | async-start | bytes 393216 | tf_op jit(solution)/shard_map/all_to_all | solution.py:209

commit v2 on v1

v2 whole, which is shorter than its diff:
```python
import functools

import jax
import jax.numpy as jnp
from jax import lax
from jax.experimental import pallas as pl
from jax.experimental.pallas import tpu as pltpu
from jax.sharding import Mesh
from jax.sharding import PartitionSpec as P

STEPS = 4
LANES = 128
GRP = ("z_hi", "core")
VMEM_BYTES = 8 * 1024 * 1024
OWN_PAIRS = ((0, 0, 0),)
FAR_PAIRS = ((0, 1, 0), (0, 2, 2))
NEAR_PAIRS = ((1, 0, 1), (1, 1, 1), (1, 2, 3))
LAST_PAIRS = ((0, 3, 2), (1, 3, 3))


def shifted(shard, axis, by):
    peers = lax.axis_size(axis)
    return lax.ppermute(shard, axis, [(i, (i + by) % peers) for i in range(peers)])


def nt_dot(left, right):
    return lax.dot_general(
        left, right, (((1,), (1,)), ((), ())), preferred_element_type=jnp.float32
    )


def self_product(amps):
    head = amps.astype(jnp.bfloat16)
    rest = (amps - head.astype(jnp.float32)).astype(jnp.bfloat16)
    return nt_dot(head, head) + nt_dot(head, rest) + nt_dot(rest, head)


def add_pairs(pairs, rows, cols, levels, virt_col, virt_rows, density, energy):
    lane = lax.broadcasted_iota(jnp.int32, energy.shape, 1)
    for row, col, slot in pairs:
        coupling = nt_dot(rows[row][...], cols[col][...])
        half = col % 2
        denominator = (
            virt_col[...]
            + virt_rows[half : half + 1, :]
            - levels[row]
            - levels[0 if col < 2 else 2]
        )
        amp = coupling / denominator
        value = jnp.sum(amp * coupling, keepdims=True)
        energy = energy + jnp.where(lane == slot, value, 0.0)
        density = density + self_product(amp)
    return density, energy


def own_kernel(levels, own, virt_col, virt_rows, density, energy):
    density[...], energy[...] = add_pairs(
        OWN_PAIRS,
        (own,),
        (own,),
        levels,
        virt_col,
        virt_rows,
        jnp.zeros(density.shape, jnp.float32),
        jnp.zeros(energy.shape, jnp.float32),
    )


def far_kernel(
    levels, own, own_mirror, far, virt_col, virt_rows, density_in, energy_in, density, energy
):
    density[...], energy[...] = add_pairs(
        FAR_PAIRS,
        (own,),
        (None, own_mirror, far),
        levels,
        virt_col,
        virt_rows,
        density_in[...],
        energy_in[...],
    )


def near_kernel(
    levels, own, own_mirror, near, far, virt_col, virt_rows, density_in, energy_in, density, energy
):
    density[...], energy[...] = add_pairs(
        NEAR_PAIRS,
        (None, near),
        (own, own_mirror, far),
        levels,
        virt_col,
        virt_rows,
        density_in[...],
        energy_in[...],
    )


def last_kernel(
    levels,
    block,
    own,
    near,
    far_mirror,
    virt_col,
    virt_rows,
    density_in,
    energy_in,
    spread,
    held,
):
    density, energy = add_pairs(
        LAST_PAIRS,
        (own, near),
        (None, None, None, far_mirror),
        levels,
        virt_col,
        virt_rows,
        density_in[...],
        energy_in[...],
    )
    width = density.shape[0]
    peers, rows, stride = spread.shape
    panels = stride // LANES
    for panel in range(panels):
        part = density[:, panel * LANES : min(width, (panel + 1) * LANES)]
        if part.shape[1] < LANES:
            held[panel] = jnp.zeros(held.shape[1:], jnp.float32)
        held[panel, :, : part.shape[1]] = part
    each = width // peers
    for row in range(each):
        for panel in range(panels):
            spread[:, row, panel * LANES : (panel + 1) * LANES] = held[
                panel, pl.Slice(row, peers, each), :
            ]
    owner = lax.broadcasted_iota(jnp.int32, (peers, LANES), 0)
    slot = lax.broadcasted_iota(jnp.int32, (peers, LANES), 1)
    target = jnp.where(slot % 2 == 0, block[0], block[1])
    scaled = energy * (-1.0 / (width * width))
    spread[:, each, :LANES] = jnp.where(owner == target, scaled, 0.0)
    spread[:, each, LANES:] = jnp.zeros((peers, stride - LANES), jnp.float32)


def lookup_many(values_in, where_at):
    positions = jnp.arange(values_in.shape[0], dtype=jnp.int32)
    matches = positions[None, :] == where_at[:, None]
    return jnp.sum(
        jnp.where(matches, values_in[None, :], jnp.zeros_like(values_in)[None, :]), axis=1
    )


def call(kernel, out_shape, operands, smem, pairs, block, scratch=()):
    vmem = pl.BlockSpec(memory_space=pltpu.VMEM)
    specs = [pl.BlockSpec(memory_space=pltpu.SMEM)] * smem
    specs += [vmem] * (len(operands) - smem)
    width, depth = block.shape
    return pl.pallas_call(
        kernel,
        out_shape=out_shape,
        in_specs=specs,
        out_specs=jax.tree.map(lambda _: vmem, out_shape),
        scratch_shapes=list(scratch),
        compiler_params=pltpu.CompilerParams(vmem_limit_bytes=VMEM_BYTES),
        cost_estimate=pl.CostEstimate(
            flops=2 * pairs * width * width * depth,
            bytes_accessed=2 * pairs * width * depth,
            transcendentals=0,
        ),
    )(*operands)


def local(ints, occ_energy, occ_window, virt_energy):
    far = shifted(ints, "blk", 2)[0]
    near = shifted(ints, "blk", -1)[0]
    own_mirror = shifted(ints, "core", 1)[0]
    own = ints[0]
    width, depth = own.shape
    occ_count = occ_window.shape[0]
    peers = lax.axis_size("blk")
    group_index = lax.axis_index(GRP)
    block_index = lax.axis_index("blk")
    mirror_index = group_index + 1 - 2 * (group_index % 2)

    virt_own = lax.dynamic_slice_in_dim(virt_energy, group_index * width, width)
    virt_mirror = lax.dynamic_slice_in_dim(virt_energy, mirror_index * width, width)
    virt = (virt_own[:, None], jnp.stack([virt_own, virt_mirror]))
    wanted = (block_index + jnp.array([0, 1, -2], jnp.int32)) % peers
    levels = lookup_many(occ_energy, lookup_many(occ_window, wanted))

    sums = (
        jax.ShapeDtypeStruct((width, width), jnp.float32),
        jax.ShapeDtypeStruct((1, LANES), jnp.float32),
    )
    state = call(own_kernel, sums, (levels, own) + virt, 1, 1, own)
    far, density, energy = lax.optimization_barrier((far, *state))
    far_mirror = shifted(far, "core", 1)
    state = call(
        far_kernel, sums, (levels, own, own_mirror, far) + virt + (density, energy), 1, 2, own
    )
    state = call(
        near_kernel, sums, (levels, own, own_mirror, near, far) + virt + tuple(state), 1, 3, own
    )
    each = width // peers
    panels = -(-width // LANES)
    spread = call(
        last_kernel,
        jax.ShapeDtypeStruct((peers, each + 1, panels * LANES), jnp.float32),
        (levels, wanted, own, near, far_mirror) + virt + tuple(state),
        2,
        2,
        own,
        scratch=(pltpu.VMEM((panels, width, LANES), jnp.float32),),
    )
    arrived = lax.all_to_all(spread, "blk", 0, 0, tiled=True)
    total = arrived.sum(axis=0)
    pair = lax.psum(lax.psum(total[each:, :STEPS], "core"), "z_hi")
    return total[:each, :width] * (1.0 / (occ_count * STEPS)), pair


def solution(mesh):
    peers = mesh.shape["blk"]
    finer = Mesh(mesh.devices.reshape(-1, 2, peers), ("z_hi", "core", "blk"))
    placed = (P("blk", GRP, None), P(), P(), P())
    return jax.shard_map(
        local,
        mesh=finer,
        in_specs=placed,
        out_specs=(P(GRP + ("blk",), None), P("blk", None)),
        check_vma=False,
    )
```

time: 106 us -> 96.3 us (0.908)
  starting transfers between devices: 52.4 us -> 23 us
  blocking collectives: 18.1 us -> 40.4 us
  waiting for transfers between devices: 12.7 us -> 16.3 us
  local copies, waits for them, and re-layouts: 5.59 us -> 2.37 us
  other arithmetic: 4.26 us -> 3.06 us
    ppermute x14 -> x4, starting transfers between devices: 45.7 us -> 23 us  [shifted(): lax.ppermute(shard, axis, [(i, (i + by) % peers) for i in range(peers)])]
    all_to_all x0 -> x1, blocking collectives: none -> 19.4 us  [local(): arrived = lax.all_to_all(spread, 'blk', 0, 0, tiled=True)]
    all_to_all x1 -> x0, starting transfers between devices: 6.72 us -> none  [local(): arrived = lax.all_to_all(spread, 'blk', 0, 0, tiled=True)]
    ppermute x14 -> x4, waiting for transfers between devices: 12.7 us -> 16.3 us  [shifted(): lax.ppermute(shard, axis, [(i, (i + by) % peers) for i in range(peers)])]
    slice x5 -> x1, local copies, waits for them, and re-layouts: 2.93 us -> 0.01 us  [local(): pair = lax.psum(lax.psum(total[each:, :STEPS], 'core'), 'z_hi')]
    psum x2, blocking collectives: 18.1 us -> 21 us  [local(): pair = lax.psum(lax.psum(total[each:, :STEPS], 'core'), 'z_hi')]
    another operation x2 -> x1, other arithmetic: 2.62 us -> 0.01 us  [local(): virt = (virt_own[:, None], jnp.stack([virt_own, virt_mirror]))]
    reduce_sum x2, other arithmetic: 0.37 us -> 1.7 us  [lookup_many(): jnp.sum(jnp.where(matches, values_in[None, :], jnp.zeros_like(values_in)[...]
  transfers between devices with their start and end apart: 15 -> 4, of which waited for: 5 -> 1; matrix products, arithmetic and copies ran while one was open for 7% -> 3% of each run, Pallas kernels for 8% -> 7%
where the time goes in v2:
time: 96.3 us; the launch traced here: 95.9 us
  blocking collectives  40.4 us (42%)
  starting transfers between devices  23 us (24%)
  waiting for transfers between devices  16.3 us (17%)
  Pallas kernels  10 us (10%)
  other arithmetic  3.06 us (3%)
  local copies, waits for them, and re-layouts  2.37 us (2%)
    ppermute x4, starting transfers between devices, shifted(): lax.ppermute(shard, axis, [(i, (i + by) % peers) for i in range(peers)])  23 us
    psum x2, blocking collectives, local(): pair = lax.psum(lax.psum(total[each:, :STEPS], 'core'), 'z_hi')  21 us
    all_to_all x1, blocking collectives, local(): arrived = lax.all_to_all(spread, 'blk', 0, 0, tiled=True)  19.4 us
    ppermute x4, waiting for transfers between devices, shifted(): lax.ppermute(shard, axis, [(i, (i + by) % peers) for i in range(peers)])  16.3 us
    pallas_call x4, Pallas kernels, call(): pl.pallas_call(kernel, out_shape=out_shape, in_specs=specs, out_specs=jax...  10 us
  transfers between devices with their start and end apart: 4, of which 1 were waited for; matrix products, arithmetic and copies ran while one was open for 3% of the time, Pallas kernels for 7%

profile of v2, /device:TPU:1, one launch (start us, length us, event | category | flops | bytes accessed | tf_op | source)
XLA Modules:
  0.0 95.9 jit_solution(8603369430728019490)
XLA Ops:
  0.6 4.0 %collective-permute-start.1 = (bf16[1,192,4096]{2,1,0:T(8,128)(2,1)}, bf16[1,192,4096]{2,1,0:T(8,128)(2,1)S(1)}, u32[]{:S(2)}, u32[]{:S(2)}) collective-permute-start(bf16[1,192,4096]{2,1,0:T(8,128)(2,1)} %param.5), channel_id=1, source_target_pairs={{0,2},{1,3},{2,4},{3,5},{4,6},{5,7},{6,8},{7,9},{8,10},{9,11},{10,... | collective-permute-start | bytes 4718600 | tf_op jit(solution)/shard_map/ppermute | solution.py:23
  4.6 7.9 %collective-permute-start = (bf16[1,192,4096]{2,1,0:T(8,128)(2,1)}, bf16[1,192,4096]{2,1,0:T(8,128)(2,1)}, u32[]{:S(2)}, u32[]{:S(2)}) collective-permute-start(bf16[1,192,4096]{2,1,0:T(8,128)(2,1)} %param.5), channel_id=1, source_target_pairs={{0,63},{1,0},{2,1},{3,2},{4,3},{5,4},{6,5},{7,6},{8,7},{9,8},{10,9... | collective-permute-start | bytes 4718600 | tf_op jit(solution)/shard_map/ppermute | solution.py:23
  12.5 2.9 %collective-permute-start.3 = (bf16[1,192,4096]{2,1,0:T(8,128)(2,1)}, bf16[1,192,4096]{2,1,0:T(8,128)(2,1)S(1)}, u32[]{:S(2)}, u32[]{:S(2)}) collective-permute-start(bf16[1,192,4096]{2,1,0:T(8,128)(2,1)} %param.5), channel_id=1, source_target_pairs={{0,64},{64,0},{1,65},{65,1},{2,66},{66,2},{3,67},{67,3},{4,68},{68... | collective-permute-start | bytes 4718600 | tf_op jit(solution)/shard_map/ppermute | solution.py:23
  15.4 0.7 and_select_fusion.block
  16.1 0.8 select_reduce_fusion.1
  16.9 0.9 select_reduce_fusion.levels
  17.8 0.8 fusion.1
  18.6 0.1 copy.11.virt_col
  18.8 0.0 copy-start
  18.8 1.4 %copy-done = bf16[1,192,4096]{2,1,0:T(8,128)(2,1)S(1)} copy-done((bf16[1,192,4096]{2,1,0:T(8,128)(2,1)S(1)}, bf16[1,192,4096]{2,1,0:T(8,128)(2,1)}, u32[]{:S(2)}) %copy-start) | copy-done | bytes 1572888
  20.2 1.5 %shard_map.68 = (f32[192,192]{1,0:T(8,128)S(1)}, f32[1,128]{1,0:T(1,128)S(1)}) custom-call(f32[3]{0:T(128)S(1)} %select_reduce_fusion.levels, bf16[192,4096]{1,0:T(8,128)(2,1)S(1)} %bitcast.7, f32[192,1]{1,0:T(8,128)S(1)} %copy.11.virt_col, f32[2,192]{1,0:T(2,128)S(1)} %pad_maximum_fusion.virt_rows), custom_call_target="tpu_custom_call" | custom-call | flops 301989888 | bytes 1572864 | tf_op jit(solution)/shard_map/pallas_call | solution.py:157
  21.7 16.3 %collective-permute-done.1 = bf16[1,192,4096]{2,1,0:T(8,128)(2,1)S(1)} collective-permute-done((bf16[1,192,4096]{2,1,0:T(8,128)(2,1)}, bf16[1,192,4096]{2,1,0:T(8,128)(2,1)S(1)}, u32[]{:S(2)}, u32[]{:S(2)}) %collective-permute-start.1) | collective-permute-done | bytes 1572896 | tf_op jit(solution)/shard_map/ppermute | solution.py:23
  37.9 8.3 %collective-permute-start.2 = (bf16[192,4096]{1,0:T(8,128)(2,1)S(1)}, bf16[192,4096]{1,0:T(8,128)(2,1)S(1)}, u32[]{:S(2)}, u32[]{:S(2)}) collective-permute-start(bf16[192,4096]{1,0:T(8,128)(2,1)S(1)} %bitcast.11), channel_id=1, source_target_pairs={{0,64},{64,0},{1,65},{65,1},{2,66},{66,2},{3,67},{67,3},{4,68},{68... | collective-permute-start | bytes 4718600 | tf_op jit(solution)/shard_map/ppermute | solution.py:23
  46.2 0.0 collective-permute-done.3
  46.2 1.9 %shard_map.69 = (f32[192,192]{1,0:T(8,128)S(1)}, f32[1,128]{1,0:T(1,128)S(1)}) custom-call(f32[3]{0:T(128)S(1)} %select_reduce_fusion.levels, bf16[192,4096]{1,0:T(8,128)(2,1)S(1)} %bitcast.8, bf16[192,4096]{1,0:T(8,128)(2,1)S(1)} %bitcast.14, bf16[192,4096]{1,0:T(8,128)(2,1)S(1)} %bitcast.12, f32[192,1]{1,0:T(8,128)S(1)} %copy.11.virt_col, ...), custom_call_target="tpu_custom_call" | custom-call | flops 603979776 | bytes 3145728 | tf_op jit(solution)/shard_map/pallas_call | solution.py:157
  48.1 0.0 collective-permute-done
  48.1 3.8 %shard_map.70 = (f32[192,192]{1,0:T(8,128)S(1)}, f32[1,128]{1,0:T(1,128)S(1)}) custom-call(f32[3]{0:T(128)S(1)} %select_reduce_fusion.levels, bf16[192,4096]{1,0:T(8,128)(2,1)S(1)} %bitcast.9, bf16[192,4096]{1,0:T(8,128)(2,1)S(1)} %bitcast.15, bf16[192,4096]{1,0:T(8,128)(2,1)} %bitcast.1.near, bf16[192,4096]{1,0:T(8,128)(2,1)S(1)} %bitcast.13, ...), custom_call_target="tpu_custom_call" | custom-call | flops 905969664 | bytes 4718592 | tf_op jit(solution)/shard_map/pallas_call | solution.py:157
  51.9 0.0 collective-permute-done.2.far_mirror
  51.9 2.9 %shard_map.71 = f32[64,4,256]{2,1,0:T(4,128)S(1)} custom-call(f32[3]{0:T(128)S(1)} %select_reduce_fusion.levels, s32[3]{0:T(128)S(1)} %and_select_fusion.block, bf16[192,4096]{1,0:T(8,128)(2,1)S(1)} %bitcast.10, bf16[192,4096]{1,0:T(8,128)(2,1)} %bitcast.1.near, bf16[192,4096]{1,0:T(8,128)(2,1)S(1)} %collective-permute-done.2.far_mirror, ...), custom_call_target="tpu_custom_call" | custom-call | flops 603979776 | bytes 3145728 | tf_op jit(solution)/shard_map/pallas_call | solution.py:157
  54.8 19.4 %all_to_all.5 = f32[64,4,256]{2,1,0:T(4,128)S(1)} all-to-all(f32[64,4,256]{2,1,0:T(4,128)S(1)} %shard_map.71), channel_id=1, replica_groups=mesh['z_hi'=4,'core'=2,'blk'=64] {'blk'}, dimensions={0} | all-to-all | bytes 524288 | tf_op jit(solution)/shard_map/all_to_all | solution.py:214
  74.2 0.1 reduce_sum.29
  74.3 5.8 %psum.14 = f32[1,4]{1,0:T(1,128)S(1)} all-reduce(f32[1,4]{1,0:T(1,128)S(1)} %slice.9), channel_id=1, replica_groups=mesh['z_hi'=4,'core'=2,'blk'=64] {'core'}, use_global_device_ids=true, to_apply=%region_3.4 | all-reduce | flops 4 | bytes 32 | tf_op jit(solution)/shard_map/psum | solution.py:216
  80.1 0.6 slice_multiply_fusion
  80.7 15.2 %psum.15 = f32[1,4]{1,0:T(1,128)} all-reduce(f32[1,4]{1,0:T(1,128)S(1)} %psum.14), channel_id=1, replica_groups=mesh['z_hi'=4,'core'=2,'blk'=64] {'z_hi'}, use_global_device_ids=true, to_apply=%region_4.5 | all-reduce | flops 4 | bytes 32 | tf_op jit(solution)/shard_map/psum | solution.py:216
  (2 shorter events, 0.0 us)
Async XLA Ops:
  0.6 37.3 %collective-permute-start.1 = (bf16[1,192,4096]{2,1,0:T(8,128)(2,1)}, bf16[1,192,4096]{2,1,0:T(8,128)(2,1)S(1)}, u32[]{:S(2)}, u32[]{:S(2)}) collective-permute-start(bf16[1,192,4096]{2,1,0:T(8,128)(2,1)} %param.5), channel_id=1, source_target_pairs={{0,2},{1,3},{2,4},{3,5},{4,6},{5,7},{6,8},{7,9},{8,10},{9,11},{10,... | collective-permute-start | bytes 4718600 | tf_op jit(solution)/shard_map/ppermute | solution.py:23
  4.6 43.5 %collective-permute-start = (bf16[1,192,4096]{2,1,0:T(8,128)(2,1)}, bf16[1,192,4096]{2,1,0:T(8,128)(2,1)}, u32[]{:S(2)}, u32[]{:S(2)}) collective-permute-start(bf16[1,192,4096]{2,1,0:T(8,128)(2,1)} %param.5), channel_id=1, source_target_pairs={{0,63},{1,0},{2,1},{3,2},{4,3},{5,4},{6,5},{7,6},{8,7},{9,8},{10,9... | collective-permute-start | bytes 4718600 | tf_op jit(solution)/shard_map/ppermute | solution.py:23
  12.5 33.7 %collective-permute-start.3 = (bf16[1,192,4096]{2,1,0:T(8,128)(2,1)}, bf16[1,192,4096]{2,1,0:T(8,128)(2,1)S(1)}, u32[]{:S(2)}, u32[]{:S(2)}) collective-permute-start(bf16[1,192,4096]{2,1,0:T(8,128)(2,1)} %param.5), channel_id=1, source_target_pairs={{0,64},{64,0},{1,65},{65,1},{2,66},{66,2},{3,67},{67,3},{4,68},{68... | collective-permute-start | bytes 4718600 | tf_op jit(solution)/shard_map/ppermute | solution.py:23
  18.8 1.4 %copy-start = (bf16[1,192,4096]{2,1,0:T(8,128)(2,1)S(1)}, bf16[1,192,4096]{2,1,0:T(8,128)(2,1)}, u32[]{:S(2)}) copy-start(bf16[1,192,4096]{2,1,0:T(8,128)(2,1)} %param.5) | copy-start | bytes 4718596
  37.9 14.0 %collective-permute-start.2 = (bf16[192,4096]{1,0:T(8,128)(2,1)S(1)}, bf16[192,4096]{1,0:T(8,128)(2,1)S(1)}, u32[]{:S(2)}, u32[]{:S(2)}) collective-permute-start(bf16[192,4096]{1,0:T(8,128)(2,1)S(1)} %bitcast.11), channel_id=1, source_target_pairs={{0,64},{64,0},{1,65},{65,1},{2,66},{66,2},{3,67},{67,3},{4,68},{68... | collective-permute-start | bytes 4718600 | tf_op jit(solution)/shard_map/ppermute | solution.py:23

commit v3 on v2

--- a/solution.py
+++ b/solution.py
@@ -35,20 +35,25 @@
     return nt_dot(head, head) + nt_dot(head, rest) + nt_dot(rest, head)
 
 
+def pair_amplitudes(pair, rows, cols, levels, virt_col, virt_rows, energy):
+    row, col, slot = pair
+    coupling = nt_dot(rows[row][...], cols[col][...])
+    half = col % 2
+    denominator = (
+        virt_col[...]
+        + virt_rows[half : half + 1, :]
+        - levels[row]
+        - levels[0 if col < 2 else 2]
+    )
+    amp = coupling / denominator
+    lane = lax.broadcasted_iota(jnp.int32, energy.shape, 1)
+    value = jnp.sum(amp * coupling, keepdims=True)
+    return amp, energy + jnp.where(lane == slot, value, 0.0)
+
+
 def add_pairs(pairs, rows, cols, levels, virt_col, virt_rows, density, energy):
-    lane = lax.broadcasted_iota(jnp.int32, energy.shape, 1)
-    for row, col, slot in pairs:
-        coupling = nt_dot(rows[row][...], cols[col][...])
-        half = col % 2
-        denominator = (
-            virt_col[...]
-            + virt_rows[half : half + 1, :]
-            - levels[row]
-            - levels[0 if col < 2 else 2]
-        )
-        amp = coupling / denominator
-        value = jnp.sum(amp * coupling, keepdims=True)
-        energy = energy + jnp.where(lane == slot, value, 0.0)
+    for pair in pairs:
+        amp, energy = pair_amplitudes(pair, rows, cols, levels, virt_col, virt_rows, energy)
         density = density + self_product(amp)
     return density, energy
 
@@ -96,49 +101,39 @@
     )
 
 
-def last_kernel(
-    levels,
-    block,
-    own,
-    near,
-    far_mirror,
-    virt_col,
-    virt_rows,
-    density_in,
-    energy_in,
-    spread,
-    held,
-):
-    density, energy = add_pairs(
-        LAST_PAIRS,
-        (own, near),
-        (None, None, None, far_mirror),
-        levels,
-        virt_col,
-        virt_rows,
-        density_in[...],
-        energy_in[...],
-    )
+def last_kernel(levels, own, near, far_mirror, virt_col, virt_rows, energy_in, amps, energy_out):
+    energy = energy_in[...]
+    for at, pair in enumerate(LAST_PAIRS):
+        amps[at], energy = pair_amplitudes(
+            pair,
+            (own, near),
+            (None, None, None, far_mirror),
+            levels,
+            virt_col,
+            virt_rows,
+            energy,
+        )
+    width = virt_col.shape[0]
+    energy_out[...] = energy * (-1.0 / (width * width))
+
+
+def spread_kernel(amps, density_in, spread, held):
+    density = density_in[...]
+    for at in range(amps.shape[0]):
+        density = density + self_product(amps[at])
     width = density.shape[0]
-    peers, rows, stride = spread.shape
+    peers, each, stride = spread.shape
     panels = stride // LANES
     for panel in range(panels):
         part = density[:, panel * LANES : min(width, (panel + 1) * LANES)]
         if part.shape[1] < LANES:
             held[panel] = jnp.zeros(held.shape[1:], jnp.float32)
         held[panel, :, : part.shape[1]] = part
-    each = width // peers
     for row in range(each):
         for panel in range(panels):
             spread[:, row, panel * LANES : (panel + 1) * LANES] = held[
                 panel, pl.Slice(row, peers, each), :
             ]
-    owner = lax.broadcasted_iota(jnp.int32, (peers, LANES), 0)
-    slot = lax.broadcasted_iota(jnp.int32, (peers, LANES), 1)
-    target = jnp.where(slot % 2 == 0, block[0], block[1])
-    scaled = energy * (-1.0 / (width * width))
-    spread[:, each, :LANES] = jnp.where(owner == target, scaled, 0.0)
-    spread[:, each, LANES:] = jnp.zeros((peers, stride - LANES), jnp.float32)
 
 
 def lookup_many(values_in, where_at):
@@ -202,19 +197,32 @@
     )
     each = width // peers
     panels = -(-width // LANES)
-    spread = call(
+    amps, energies = call(
         last_kernel,
-        jax.ShapeDtypeStruct((peers, each + 1, panels * LANES), jnp.float32),
-        (levels, wanted, own, near, far_mirror) + virt + tuple(state),
-        2,
+        (jax.ShapeDtypeStruct((len(LAST_PAIRS), width, width), jnp.float32), sums[1]),
+        (levels, own, near, far_mirror) + virt + (state[1],),
+        1,
         2,
         own,
+    )
+    energies = energies[:, :STEPS]
+    passed = shifted(energies, "blk", 1)
+    spread = call(
+        spread_kernel,
+        jax.ShapeDtypeStruct((peers, each, panels * LANES), jnp.float32),
+        (amps, state[0]),
+        0,
+        1,
+        own,
         scratch=(pltpu.VMEM((panels, width, LANES), jnp.float32),),
     )
+    odd = lax.broadcasted_iota(jnp.int32, energies.shape, 1) % 2 == 1
+    passed, spread = lax.optimization_barrier((passed, spread))
+    pair = lax.psum(jnp.where(odd, passed, energies), "core")
+    pair, spread = lax.optimization_barrier((pair, spread))
     arrived = lax.all_to_all(spread, "blk", 0, 0, tiled=True)
-    total = arrived.sum(axis=0)
-    pair = lax.psum(lax.psum(total[each:, :STEPS], "core"), "z_hi")
-    return total[:each, :width] * (1.0 / (occ_count * STEPS)), pair
+    pair = lax.psum(pair, "z_hi")
+    return arrived.sum(axis=0)[:, :width] * (1.0 / (occ_count * STEPS)), pair
 
 
 def solution(mesh):

time: 96.3 us -> 92.1 us (0.956); the launches traced: 95.9 us -> 90.6 us
  blocking collectives: 40.4 us -> 19.7 us
  starting transfers between devices: 23 us -> 34.2 us
  waiting for transfers between devices: 16.3 us -> 19.6 us
    all_to_all x1 -> x0, blocking collectives: 19.4 us -> none  [local(): arrived = lax.all_to_all(spread, 'blk', 0, 0, tiled=True)]
    all_to_all x0 -> x1, starting transfers between devices: none -> 7.21 us  [local(): arrived = lax.all_to_all(spread, 'blk', 0, 0, tiled=True)]
    ppermute x4 -> x5, starting transfers between devices: 23 us -> 27 us  [shifted(): lax.ppermute(shard, axis, [(i, (i + by) % peers) for i in range(peers)])]
    ppermute x4 -> x5, waiting for transfers between devices: 16.3 us -> 19.6 us  [shifted(): lax.ppermute(shard, axis, [(i, (i + by) % peers) for i in range(peers)])]
    psum x2, blocking collectives: 21 us -> 19.7 us  [the longest x1 16.4 us: local(): pair = lax.psum(pair, 'z_hi')]
    pallas_call x4 -> x5, Pallas kernels: 10 us -> 10.8 us  [call(): pl.pallas_call(kernel, out_shape=out_shape, in_specs=specs, out_specs=jax...]
  transfers between devices with their start and end apart: 4 -> 6, of which waited for: 1 -> 2; matrix products, arithmetic and copies ran while one was open for 3% -> 4% of each run, Pallas kernels for 7% -> 10%
where the time goes in v3:
time: 92.1 us; the launch traced here: 90.6 us
  starting transfers between devices  34.2 us (37%)
  blocking collectives  19.7 us (21%)
  waiting for transfers between devices  19.6 us (21%)
  Pallas kernels  10.8 us (12%)
  other arithmetic  3.07 us (3%)
  local copies, waits for them, and re-layouts  2.37 us (3%)
    ppermute x5, starting transfers between devices, shifted(): lax.ppermute(shard, axis, [(i, (i + by) % peers) for i in range(peers)])  27 us
    ppermute x5, waiting for transfers between devices, shifted(): lax.ppermute(shard, axis, [(i, (i + by) % peers) for i in range(peers)])  19.6 us
    psum x1, blocking collectives, local(): pair = lax.psum(pair, 'z_hi')  16.4 us
    pallas_call x5, Pallas kernels, call(): pl.pallas_call(kernel, out_shape=out_shape, in_specs=specs, out_specs=jax...  10.8 us
    all_to_all x1, starting transfers between devices, local(): arrived = lax.all_to_all(spread, 'blk', 0, 0, tiled=True)  7.21 us
    psum x1, blocking collectives, local(): pair = lax.psum(jnp.where(odd, passed, energies), 'core')  3.27 us
  transfers between devices with their start and end apart: 6, of which 2 were waited for; matrix products, arithmetic and copies ran while one was open for 4% of the time, Pallas kernels for 10%

profile of v3, /device:TPU:1, one launch (start us, length us, event | category | flops | bytes accessed | tf_op | source)
XLA Modules:
  0.0 90.6 jit_solution(18423014879172825951)
XLA Ops:
  0.6 4.0 %collective-permute-start.1 = (bf16[1,192,4096]{2,1,0:T(8,128)(2,1)}, bf16[1,192,4096]{2,1,0:T(8,128)(2,1)S(1)}, u32[]{:S(2)}, u32[]{:S(2)}) collective-permute-start(bf16[1,192,4096]{2,1,0:T(8,128)(2,1)} %param.5), channel_id=1, source_target_pairs={{0,2},{1,3},{2,4},{3,5},{4,6},{5,7},{6,8},{7,9},{8,10},{9,11},{10,... | collective-permute-start | bytes 4718600 | tf_op jit(solution)/shard_map/ppermute | solution.py:23
  4.6 7.9 %collective-permute-start = (bf16[1,192,4096]{2,1,0:T(8,128)(2,1)}, bf16[1,192,4096]{2,1,0:T(8,128)(2,1)S(1)}, u32[]{:S(2)}, u32[]{:S(2)}) collective-permute-start(bf16[1,192,4096]{2,1,0:T(8,128)(2,1)} %param.5), channel_id=1, source_target_pairs={{0,63},{1,0},{2,1},{3,2},{4,3},{5,4},{6,5},{7,6},{8,7},{9,8},{10,9... | collective-permute-start | bytes 4718600 | tf_op jit(solution)/shard_map/ppermute | solution.py:23
  12.5 2.9 %collective-permute-start.3 = (bf16[1,192,4096]{2,1,0:T(8,128)(2,1)}, bf16[1,192,4096]{2,1,0:T(8,128)(2,1)}, u32[]{:S(2)}, u32[]{:S(2)}) collective-permute-start(bf16[1,192,4096]{2,1,0:T(8,128)(2,1)} %param.5), channel_id=1, source_target_pairs={{0,64},{64,0},{1,65},{65,1},{2,66},{66,2},{3,67},{67,3},{4,68},{68... | collective-permute-start | bytes 4718600 | tf_op jit(solution)/shard_map/ppermute | solution.py:23
  15.4 0.7 and_select_fusion
  16.1 0.8 select_reduce_fusion.1
  16.9 0.9 select_reduce_fusion.levels
  17.8 0.8 fusion.1
  18.6 0.1 copy.11.virt_col
  18.8 0.0 copy-start
  18.8 1.4 %copy-done = bf16[1,192,4096]{2,1,0:T(8,128)(2,1)S(1)} copy-done((bf16[1,192,4096]{2,1,0:T(8,128)(2,1)S(1)}, bf16[1,192,4096]{2,1,0:T(8,128)(2,1)}, u32[]{:S(2)}) %copy-start) | copy-done | bytes 1572888
  20.2 1.5 %shard_map.68 = (f32[192,192]{1,0:T(8,128)S(1)}, f32[1,128]{1,0:T(1,128)S(1)}) custom-call(f32[3]{0:T(128)S(1)} %select_reduce_fusion.levels, bf16[192,4096]{1,0:T(8,128)(2,1)S(1)} %bitcast.8, f32[192,1]{1,0:T(8,128)S(1)} %copy.11.virt_col, f32[2,192]{1,0:T(2,128)S(1)} %pad_maximum_fusion.virt_rows), custom_call_target="tpu_custom_call" | custom-call | flops 301989888 | bytes 1572864 | tf_op jit(solution)/shard_map/pallas_call | solution.py:152
  21.7 16.3 %collective-permute-done.1 = bf16[1,192,4096]{2,1,0:T(8,128)(2,1)S(1)} collective-permute-done((bf16[1,192,4096]{2,1,0:T(8,128)(2,1)}, bf16[1,192,4096]{2,1,0:T(8,128)(2,1)S(1)}, u32[]{:S(2)}, u32[]{:S(2)}) %collective-permute-start.1) | collective-permute-done | bytes 1572896 | tf_op jit(solution)/shard_map/ppermute | solution.py:23
  37.9 8.3 %collective-permute-start.2 = (bf16[192,4096]{1,0:T(8,128)(2,1)S(1)}, bf16[192,4096]{1,0:T(8,128)(2,1)S(1)}, u32[]{:S(2)}, u32[]{:S(2)}) collective-permute-start(bf16[192,4096]{1,0:T(8,128)(2,1)S(1)} %bitcast.14), channel_id=1, source_target_pairs={{0,64},{64,0},{1,65},{65,1},{2,66},{66,2},{3,67},{67,3},{4,68},{68... | collective-permute-start | bytes 4718600 | tf_op jit(solution)/shard_map/ppermute | solution.py:23
  46.2 0.0 collective-permute-done.3
  46.2 2.8 %shard_map.69 = (f32[192,192]{1,0:T(8,128)S(1)}, f32[1,128]{1,0:T(1,128)S(1)}) custom-call(f32[3]{0:T(128)S(1)} %select_reduce_fusion.levels, bf16[192,4096]{1,0:T(8,128)(2,1)S(1)} %bitcast.9, bf16[192,4096]{1,0:T(8,128)(2,1)} %bitcast.6.own_mirror, bf16[192,4096]{1,0:T(8,128)(2,1)S(1)} %bitcast.15, f32[192,1]{1,0:T(8,128)S(1)} %copy.11.virt_col, ...), custom_call_target="tpu_custom_call" | custom-call | flops 603979776 | bytes 3145728 | tf_op jit(solution)/shard_map/pallas_call | solution.py:152
  49.0 0.0 collective-permute-done
  49.0 3.8 %shard_map.70 = (f32[192,192]{1,0:T(8,128)S(1)}, f32[1,128]{1,0:T(1,128)S(1)}) custom-call(f32[3]{0:T(128)S(1)} %select_reduce_fusion.levels, bf16[192,4096]{1,0:T(8,128)(2,1)S(1)} %bitcast.10, bf16[192,4096]{1,0:T(8,128)(2,1)} %bitcast.6.own_mirror, bf16[192,4096]{1,0:T(8,128)(2,1)S(1)} %bitcast.12, bf16[192,4096]{1,0:T(8,128)(2,1)S(1)} %bitcast.16, ...), custom_call_target="tpu_custom_call" | custom-call | flops 905969664 | bytes 4718592 | tf_op jit(solution)/shard_map/pallas_call | solution.py:152
  52.8 0.0 collective-permute-done.2.far_mirror
  52.8 1.7 %shard_map.71 = (f32[2,192,192]{2,1,0:T(8,128)S(1)}, f32[1,128]{1,0:T(1,128)S(1)}) custom-call(f32[3]{0:T(128)S(1)} %select_reduce_fusion.levels, bf16[192,4096]{1,0:T(8,128)(2,1)S(1)} %bitcast.11, bf16[192,4096]{1,0:T(8,128)(2,1)S(1)} %bitcast.13, bf16[192,4096]{1,0:T(8,128)(2,1)S(1)} %collective-permute-done.2.far_mirror, f32[192,1]{1,0:T(8,128)S(1)} %copy.11.virt_col, ...), custom_call_target="tpu_custom_call" | custom-call | flops 603979776 | bytes 3145728 | tf_op jit(solution)/shard_map/pallas_call | solution.py:152
  54.5 4.0 %collective-permute-start.4 = (f32[1,4]{1,0:T(1,128)S(1)}, f32[1,4]{1,0:T(1,128)S(1)}, u32[]{:S(2)}, u32[]{:S(2)}) collective-permute-start(f32[1,4]{1,0:T(1,128)S(1)} %bitcast.17), channel_id=1, source_target_pairs={{0,1},{1,2},{2,3},{3,4},{4,5},{5,6},{6,7},{7,8},{8,9},{9,10},{10,1... | collective-permute-start | bytes 56 | tf_op jit(solution)/shard_map/ppermute | solution.py:23
  58.5 1.1 %shard_map.72 = f32[64,3,256]{2,1,0:T(4,128)} custom-call(f32[2,192,192]{2,1,0:T(8,128)S(1)} %get-tuple-element.26.amps, f32[192,192]{1,0:T(8,128)S(1)} %get-tuple-element.27.density_in), custom_call_target="tpu_custom_call" | custom-call | flops 301989888 | bytes 1572864 | tf_op jit(solution)/shard_map/pallas_call | solution.py:152
  59.6 3.4 %collective-permute-done.4 = f32[1,4]{1,0:T(1,128)S(1)} collective-permute-done((f32[1,4]{1,0:T(1,128)S(1)}, f32[1,4]{1,0:T(1,128)S(1)}, u32[]{:S(2)}, u32[]{:S(2)}) %collective-permute-start.4) | collective-permute-done | bytes 48 | tf_op jit(solution)/shard_map/ppermute | solution.py:23
  63.0 3.3 %psum.14 = f32[1,4]{1,0:T(1,128)S(1)} all-reduce(f32[1,4]{1,0:T(1,128)S(1)} %compare_select_fusion.2), channel_id=1, replica_groups=mesh['z_hi'=4,'core'=2,'blk'=64] {'core'}, use_global_device_ids=true, to_apply=%region_2.3 | all-reduce | flops 4 | bytes 32 | tf_op jit(solution)/shard_map/psum | solution.py:221
  66.2 7.2 %all-to-all-start = ((f32[64,3,256]{2,1,0:T(4,128)}), f32[64,3,256]{2,1,0:T(4,128)S(1)}, u32[]{:S(2)}, u32[]{:S(2)}) async-start(f32[64,3,256]{2,1,0:T(4,128)} %shard_map.72), calls=%async_computation | async-start | bytes 524288 | tf_op jit(solution)/shard_map/all_to_all | solution.py:223
  73.5 16.4 %psum.15 = f32[1,4]{1,0:T(1,128)} all-reduce(f32[1,4]{1,0:T(1,128)S(1)} %psum.14), channel_id=1, replica_groups=mesh['z_hi'=4,'core'=2,'blk'=64] {'z_hi'}, use_global_device_ids=true, to_apply=%region_4.5 | all-reduce | flops 4 | bytes 32 | tf_op jit(solution)/shard_map/psum | solution.py:224
  89.9 0.0 all-to-all-done
  89.9 0.1 reduce_sum.29
  90.0 0.6 slice_multiply_fusion
  (2 shorter events, 0.0 us)
Async XLA Ops:
  0.6 37.3 %collective-permute-start.1 = (bf16[1,192,4096]{2,1,0:T(8,128)(2,1)}, bf16[1,192,4096]{2,1,0:T(8,128)(2,1)S(1)}, u32[]{:S(2)}, u32[]{:S(2)}) collective-permute-start(bf16[1,192,4096]{2,1,0:T(8,128)(2,1)} %param.5), channel_id=1, source_target_pairs={{0,2},{1,3},{2,4},{3,5},{4,6},{5,7},{6,8},{7,9},{8,10},{9,11},{10,... | collective-permute-start | bytes 4718600 | tf_op jit(solution)/shard_map/ppermute | solution.py:23
  4.6 44.4 %collective-permute-start = (bf16[1,192,4096]{2,1,0:T(8,128)(2,1)}, bf16[1,192,4096]{2,1,0:T(8,128)(2,1)S(1)}, u32[]{:S(2)}, u32[]{:S(2)}) collective-permute-start(bf16[1,192,4096]{2,1,0:T(8,128)(2,1)} %param.5), channel_id=1, source_target_pairs={{0,63},{1,0},{2,1},{3,2},{4,3},{5,4},{6,5},{7,6},{8,7},{9,8},{10,9... | collective-permute-start | bytes 4718600 | tf_op jit(solution)/shard_map/ppermute | solution.py:23
  12.5 33.7 %collective-permute-start.3 = (bf16[1,192,4096]{2,1,0:T(8,128)(2,1)}, bf16[1,192,4096]{2,1,0:T(8,128)(2,1)}, u32[]{:S(2)}, u32[]{:S(2)}) collective-permute-start(bf16[1,192,4096]{2,1,0:T(8,128)(2,1)} %param.5), channel_id=1, source_target_pairs={{0,64},{64,0},{1,65},{65,1},{2,66},{66,2},{3,67},{67,3},{4,68},{68... | collective-permute-start | bytes 4718600 | tf_op jit(solution)/shard_map/ppermute | solution.py:23
  18.8 1.4 %copy-start = (bf16[1,192,4096]{2,1,0:T(8,128)(2,1)S(1)}, bf16[1,192,4096]{2,1,0:T(8,128)(2,1)}, u32[]{:S(2)}) copy-start(bf16[1,192,4096]{2,1,0:T(8,128)(2,1)} %param.5) | copy-start | bytes 4718596
  37.9 14.8 %collective-permute-start.2 = (bf16[192,4096]{1,0:T(8,128)(2,1)S(1)}, bf16[192,4096]{1,0:T(8,128)(2,1)S(1)}, u32[]{:S(2)}, u32[]{:S(2)}) collective-permute-start(bf16[192,4096]{1,0:T(8,128)(2,1)S(1)} %bitcast.14), channel_id=1, source_target_pairs={{0,64},{64,0},{1,65},{65,1},{2,66},{66,2},{3,67},{67,3},{4,68},{68... | collective-permute-start | bytes 4718600 | tf_op jit(solution)/shard_map/ppermute | solution.py:23
  54.5 8.5 %collective-permute-start.4 = (f32[1,4]{1,0:T(1,128)S(1)}, f32[1,4]{1,0:T(1,128)S(1)}, u32[]{:S(2)}, u32[]{:S(2)}) collective-permute-start(f32[1,4]{1,0:T(1,128)S(1)} %bitcast.17), channel_id=1, source_target_pairs={{0,1},{1,2},{2,3},{3,4},{4,5},{5,6},{6,7},{7,8},{8,9},{9,10},{10,1... | collective-permute-start | bytes 56 | tf_op jit(solution)/shard_map/ppermute | solution.py:23
  66.2 23.7 %all-to-all-start = ((f32[64,3,256]{2,1,0:T(4,128)}), f32[64,3,256]{2,1,0:T(4,128)S(1)}, u32[]{:S(2)}, u32[]{:S(2)}) async-start(f32[64,3,256]{2,1,0:T(4,128)} %shard_map.72), calls=%async_computation | async-start | bytes 524288 | tf_op jit(solution)/shard_map/all_to_all | solution.py:223

commit v4 on v3

v4 whole, which is shorter than its diff:
```python
import jax
import jax.numpy as jnp
from jax import lax
from jax.experimental import pallas as pl
from jax.experimental.pallas import tpu as pltpu
from jax.sharding import Mesh
from jax.sharding import PartitionSpec as P

STEPS = 4
LANES = 128
GRP = ("z_hi", "core")
VMEM_BYTES = 8 * 1024 * 1024
FAR_PAIRS = ((0, 2),)
NEAR_PAIRS = ((0, 1), (1, 0), (1, 1), (1, 2))
LAST_PAIRS = ((0, 3), (1, 3))


def shifted(shard, axis, by):
    peers = lax.axis_size(axis)
    return lax.ppermute(shard, axis, [(i, (i + by) % peers) for i in range(peers)])


def nt_dot(left, right):
    return lax.dot_general(
        left, right, (((1,), (1,)), ((), ())), preferred_element_type=jnp.float32
    )


def slot_of(row, col):
    return row + 2 * (col // 2)


def amplitude_of(row, col, rows, cols, inverse):
    coupling = nt_dot(rows[row][...], cols[col][...])
    amp = coupling * inverse[4 * row + col]
    return amp, amp * coupling


def add_energies(line, products):
    lane = lax.broadcasted_iota(jnp.int32, line.shape, 1)
    for slot in sorted({slot for slot, _ in products}):
        value = sum(array for at, array in products if at == slot)
        line = line + jnp.where(lane == slot, jnp.sum(value, keepdims=True), 0.0)
    return line


def add_squares(heads, cross, amps):
    for amp in amps:
        head = amp.astype(jnp.bfloat16)
        rest = (amp - head.astype(jnp.float32)).astype(jnp.bfloat16)
        heads = heads + nt_dot(head, head)
        cross = cross + nt_dot(head, rest)
    return heads, cross


def own_kernel(window, occ, virt, own, inverse, squares, energy):
    width = own.shape[0]
    orbitals = window.shape[0]
    group = 2 * lax.axis_index("z_hi") + lax.axis_index("core")
    block = lax.axis_index("blk")
    mirror = group + 1 - 2 * lax.rem(group, 2)
    row_own = jnp.zeros((1, width), jnp.float32)
    row_mirror = jnp.zeros((1, width), jnp.float32)
    for at in range(virt.shape[1] // width):
        row = virt[:, at * width : (at + 1) * width]
        row_own = jnp.where(group == at, row, row_own)
        row_mirror = jnp.where(mirror == at, row, row_mirror)
    down = lax.broadcasted_iota(jnp.int32, (width, width), 0)
    across = lax.broadcasted_iota(jnp.int32, (width, width), 1)
    col_own = jnp.sum(jnp.where(down == across, row_own, 0.0), axis=1, keepdims=True)
    level_own = occ[window[block]]
    level_next = occ[window[lax.rem(block + 1, orbitals)]]
    level_far = occ[window[lax.rem(block + orbitals - 2, orbitals)]]
    for row, level_row in enumerate((level_own, level_next)):
        for col in range(4):
            denominator = (
                col_own
                + (row_own if col % 2 == 0 else row_mirror)
                - level_row
                - (level_own if col < 2 else level_far)
            )
            inverse[4 * row + col] = 1.0 / denominator
    amp, product = amplitude_of(0, 0, (own,), (own,), inverse)
    energy[...] = add_energies(jnp.zeros(energy.shape, jnp.float32), [(0, product)])
    zero = jnp.zeros((width, width), jnp.float32)
    squares[0], squares[1] = add_squares(zero, zero, [amp])


def far_kernel(own, far, inverse, squares_in, energy_in, squares, energy):
    amps, products = [], []
    for row, col in FAR_PAIRS:
        amp, product = amplitude_of(row, col, (own,), (None, None, far), inverse)
        amps.append(amp)
        products.append((slot_of(row, col), product))
    energy[...] = add_energies(energy_in[...], products)
    squares[0], squares[1] = add_squares(squares_in[0], squares_in[1], amps)


def near_kernel(near, own, far, own_mirror, inverse, squares_in, energy_in, squares, energy):
    amps, products = [], []
    for row, col in NEAR_PAIRS:
        amp, product = amplitude_of(row, col, (own, near), (own, own_mirror, far), inverse)
        amps.append(amp)
        products.append((slot_of(row, col), product))
    energy[...] = add_energies(energy_in[...], products)
    squares[0], squares[1] = add_squares(squares_in[0], squares_in[1], amps)


def last_kernel(near, far_mirror, own, inverse, energy_in, amps, energy):
    products = []
    for at, (row, col) in enumerate(LAST_PAIRS):
        amp, product = amplitude_of(row, col, (own, near), (None, None, None, far_mirror), inverse)
        amps[at] = amp
        products.append((slot_of(row, col), product))
    width = own.shape[0]
    energy[...] = add_energies(energy_in[...], products) * (-1.0 / (width * width))


def spread_kernel(scale, amps, squares, spread, held):
    heads, cross = add_squares(
        squares[0], squares[1], [amps[at] for at in range(amps.shape[0])]
    )
    density = (heads + cross + cross.T) * scale
    width = density.shape[0]
    peers, each, stride = spread.shape
    panels = stride // LANES
    for panel in range(panels):
        part = density[:, panel * LANES : min(width, (panel + 1) * LANES)]
        if part.shape[1] < LANES:
            held[panel] = jnp.zeros(held.shape[1:], jnp.float32)
        held[panel, :, : part.shape[1]] = part
    for row in range(each):
        for panel in range(panels):
            spread[:, row, panel * LANES : (panel + 1) * LANES] = held[
                panel, pl.Slice(row, peers, each), :
            ]


def call(kernel, out_shape, operands, pairs, block, smem=0, scratch=()):
    vmem = pl.BlockSpec(memory_space=pltpu.VMEM)
    specs = [pl.BlockSpec(memory_space=pltpu.SMEM)] * smem
    specs += [vmem] * (len(operands) - smem)
    width, depth = block.shape
    return pl.pallas_call(
        kernel,
        out_shape=out_shape,
        in_specs=specs,
        out_specs=jax.tree.map(lambda _: vmem, out_shape),
        scratch_shapes=list(scratch),
        compiler_params=pltpu.CompilerParams(vmem_limit_bytes=VMEM_BYTES),
        cost_estimate=pl.CostEstimate(
            flops=2 * pairs * width * width * depth,
            bytes_accessed=2 * pairs * width * depth,
            transcendentals=0,
        ),
    )(*operands)


def local(ints, occ_energy, occ_window, virt_energy):
    far = shifted(ints, "blk", 2)[0]
    near = shifted(ints, "blk", -1)[0]
    own = ints[0]
    width = own.shape[0]
    occ_count = occ_window.shape[0]
    peers = lax.axis_size("blk")

    def squares_of(count):
        return jax.ShapeDtypeStruct((count, width, width), jnp.float32)

    line = jax.ShapeDtypeStruct((1, LANES), jnp.float32)
    inverse, squares, energy = call(
        own_kernel,
        (squares_of(8), squares_of(2), line),
        (occ_window, occ_energy, virt_energy[None, :], own),
        1,
        own,
        smem=2,
    )
    far, inverse, squares, energy = lax.optimization_barrier((far, inverse, squares, energy))
    far_mirror = shifted(far, "core", 1)
    own_mirror = shifted(ints, "core", 1)[0]
    squares, energy = call(
        far_kernel,
        (squares_of(2), line),
        (own, far, inverse, squares, energy),
        len(FAR_PAIRS),
        own,
    )
    squares, energy = call(
        near_kernel,
        (squares_of(2), line),
        (near, own, far, own_mirror, inverse, squares, energy),
        len(NEAR_PAIRS),
        own,
    )
    amps, energy = call(
        last_kernel,
        (squares_of(len(LAST_PAIRS)), line),
        (near, far_mirror, own, inverse, energy),
        len(LAST_PAIRS),
        own,
    )
    energy = energy[:, :STEPS]
    passed = shifted(energy, "blk", 1)
    each = width // peers
    panels = -(-width // LANES)
    scale = 1.0 / (occ_count * STEPS)
    spread = call(
        lambda *refs: spread_kernel(scale, *refs),
        jax.ShapeDtypeStruct((peers, each, panels * LANES), jnp.float32),
        (amps, squares),
        1,
        own,
        scratch=(pltpu.VMEM((panels, width, LANES), jnp.float32),),
    )
    odd = lax.broadcasted_iota(jnp.int32, energy.shape, 1) % 2 == 1
    passed, spread = lax.optimization_barrier((passed, spread))
    pair = lax.psum(jnp.where(odd, passed, energy), "core")
    pair, spread = lax.optimization_barrier((pair, spread))
    arrived = lax.all_to_all(spread, "blk", 0, 0, tiled=True)
    pair = lax.all_gather(pair, "z_hi", axis=0, tiled=True).sum(axis=0, keepdims=True)
    return arrived[:, :, :width].sum(axis=0), pair


def solution(mesh):
    peers = mesh.shape["blk"]
    finer = Mesh(mesh.devices.reshape(-1, 2, peers), ("z_hi", "core", "blk"))
    placed = (P("blk", GRP, None), P(), P(), P())
    return jax.shard_map(
        local,
        mesh=finer,
        in_specs=placed,
        out_specs=(P(GRP + ("blk",), None), P("blk", None)),
        check_vma=False,
    )
```

time: 92.1 us -> 87.4 us (0.949)
  Pallas kernels: 10.8 us -> 7.22 us
  other arithmetic: 3.07 us -> 1.21 us
  local copies, waits for them, and re-layouts: 2.37 us -> 3.45 us
    psum x2 -> x1, blocking collectives: 19.7 us -> 3.89 us  [local(): pair = lax.psum(jnp.where(odd, passed, energy), 'core')]
    all_gather x0 -> x1, blocking collectives: none -> 14.9 us  [local(): lax.all_gather(pair, 'z_hi', axis=0, tiled=True).sum(axis=0, keepdims=True)]
    pallas_call x5, Pallas kernels: 10.8 us -> 7.22 us  [call(): pl.pallas_call(kernel, out_shape=out_shape, in_specs=specs, out_specs=jax...]
    unnamed x2 -> x8, local copies, waits for them, and re-layouts: 1.4 us -> 2.75 us
  transfers between devices with their start and end apart: 6 -> 6, of which waited for: 2 -> 2; matrix products, arithmetic and copies ran while one was open for 4% -> 1% of each run, Pallas kernels for 10% -> 7%
where the time goes in v4:
time: 87.4 us; the launch traced here: 86.1 us
  starting transfers between devices  34.2 us (39%)
  waiting for transfers between devices  20.5 us (23%)
  blocking collectives  18.8 us (22%)
  Pallas kernels  7.22 us (8%)
  local copies, waits for them, and re-layouts  3.45 us (4%)
  other arithmetic  1.21 us (1%)
    ppermute x5, starting transfers between devices, shifted(): lax.ppermute(shard, axis, [(i, (i + by) % peers) for i in range(peers)])  27 us
    ppermute x5, waiting for transfers between devices, shifted(): lax.ppermute(shard, axis, [(i, (i + by) % peers) for i in range(peers)])  20.5 us
    all_gather x1, blocking collectives, local(): lax.all_gather(pair, 'z_hi', axis=0, tiled=True).sum(axis=0, keepdims=True)  14.9 us
    all_to_all x1, starting transfers between devices, local(): arrived = lax.all_to_all(spread, 'blk', 0, 0, tiled=True)  7.22 us
    pallas_call x5, Pallas kernels, call(): pl.pallas_call(kernel, out_shape=out_shape, in_specs=specs, out_specs=jax...  7.22 us
    psum x1, blocking collectives, local(): pair = lax.psum(jnp.where(odd, passed, energy), 'core')  3.89 us
    unnamed x8, local copies, waits for them, and re-layouts  2.75 us
  transfers between devices with their start and end apart: 6, of which 2 were waited for; matrix products, arithmetic and copies ran while one was open for 1% of the time, Pallas kernels for 7%

profile of v4, /device:TPU:1, one launch (start us, length us, event | category | flops | bytes accessed | tf_op | source)
XLA Modules:
  0.0 86.1 jit_solution(16875507013506818348)
XLA Ops:
  0.6 4.0 %collective-permute-start.1 = (bf16[1,192,4096]{2,1,0:T(8,128)(2,1)}, bf16[1,192,4096]{2,1,0:T(8,128)(2,1)S(1)}, u32[]{:S(2)}, u32[]{:S(2)}) collective-permute-start(bf16[1,192,4096]{2,1,0:T(8,128)(2,1)} %param.4), channel_id=1, source_target_pairs={{0,2},{1,3},{2,4},{3,5},{4,6},{5,7},{6,8},{7,9},{8,10},{9,11},{10,... | collective-permute-start | bytes 4718600 | tf_op jit(solution)/shard_map/ppermute | solution.py:20
  4.6 7.9 %collective-permute-start = (bf16[1,192,4096]{2,1,0:T(8,128)(2,1)}, bf16[1,192,4096]{2,1,0:T(8,128)(2,1)S(1)}, u32[]{:S(2)}, u32[]{:S(2)}) collective-permute-start(bf16[1,192,4096]{2,1,0:T(8,128)(2,1)} %param.4), channel_id=1, source_target_pairs={{0,63},{1,0},{2,1},{3,2},{4,3},{5,4},{6,5},{7,6},{8,7},{9,8},{10,9... | collective-permute-start | bytes 4718600 | tf_op jit(solution)/shard_map/ppermute | solution.py:20
  12.5 2.9 %collective-permute-start.3 = (bf16[1,192,4096]{2,1,0:T(8,128)(2,1)}, bf16[1,192,4096]{2,1,0:T(8,128)(2,1)S(1)}, u32[]{:S(2)}, u32[]{:S(2)}) collective-permute-start(bf16[1,192,4096]{2,1,0:T(8,128)(2,1)} %param.4), channel_id=1, source_target_pairs={{0,64},{64,0},{1,65},{65,1},{2,66},{66,2},{3,67},{67,3},{4,68},{68... | collective-permute-start | bytes 4718600 | tf_op jit(solution)/shard_map/ppermute | solution.py:20
  15.4 0.7 broadcast_in_dim.6.virt
  16.1 0.0 copy-start
  16.1 1.4 %copy-done = bf16[1,192,4096]{2,1,0:T(8,128)(2,1)S(1)} copy-done((bf16[1,192,4096]{2,1,0:T(8,128)(2,1)S(1)}, bf16[1,192,4096]{2,1,0:T(8,128)(2,1)}, u32[]{:S(2)}) %copy-start) | copy-done | bytes 1572888
  17.5 0.0 copy-start.2
  17.5 0.7 copy-done.2
  18.2 0.0 copy-start.3
  18.2 0.7 copy-done.3
  18.8 0.0 copy-start.1
  18.8 2.0 %shard_map.59 = (f32[8,192,192]{2,1,0:T(8,128)S(1)}, f32[2,192,192]{2,1,0:T(8,128)S(1)}, f32[1,128]{1,0:T(1,128)S(1)}) custom-call(s32[64]{0:T(128)S(1)} %copy-done.3, f32[400]{0:T(512)S(1)} %copy-done.2, f32[1,1536]{1,0:T(1,128)S(1)} %broadcast_in_dim.6.virt, bf16[192,4096]{1,0:T(8,128)(2,1)S(1)} %bitcast.7), custom_call_target="tpu_custom_call" | custom-call | flops 301989888 | bytes 1572864 | tf_op jit(solution)/shard_map/pallas_call | solution.py:144
  20.8 17.1 %collective-permute-done.1 = bf16[1,192,4096]{2,1,0:T(8,128)(2,1)S(1)} collective-permute-done((bf16[1,192,4096]{2,1,0:T(8,128)(2,1)}, bf16[1,192,4096]{2,1,0:T(8,128)(2,1)S(1)}, u32[]{:S(2)}, u32[]{:S(2)}) %collective-permute-start.1) | collective-permute-done | bytes 1572896 | tf_op jit(solution)/shard_map/ppermute | solution.py:20
  37.9 8.3 %collective-permute-start.2 = (bf16[192,4096]{1,0:T(8,128)(2,1)S(1)}, bf16[192,4096]{1,0:T(8,128)(2,1)S(1)}, u32[]{:S(2)}, u32[]{:S(2)}) collective-permute-start(bf16[192,4096]{1,0:T(8,128)(2,1)S(1)} %bitcast.13), channel_id=1, source_target_pairs={{0,64},{64,0},{1,65},{65,1},{2,66},{66,2},{3,67},{67,3},{4,68},{68... | collective-permute-start | bytes 4718600 | tf_op jit(solution)/shard_map/ppermute | solution.py:20
  46.2 0.0 copy-done.1
  46.2 0.9 %shard_map.60 = (f32[2,192,192]{2,1,0:T(8,128)S(1)}, f32[1,128]{1,0:T(1,128)S(1)}) custom-call(bf16[192,4096]{1,0:T(8,128)(2,1)S(1)} %bitcast.8, bf16[192,4096]{1,0:T(8,128)(2,1)S(1)} %bitcast.14, f32[8,192,192]{2,1,0:T(8,128)S(1)} %get-tuple-element.23.inverse, f32[2,192,192]{2,1,0:T(8,128)S(1)} %get-tuple-element.24.squares_in, ...), custom_call_target="tpu_custom_call" | custom-call | flops 301989888 | bytes 1572864 | tf_op jit(solution)/shard_map/pallas_call | solution.py:144
  47.1 0.0 collective-permute-done
  47.1 0.0 collective-permute-done.3
  47.1 2.1 %shard_map.61 = (f32[2,192,192]{2,1,0:T(8,128)S(1)}, f32[1,128]{1,0:T(1,128)S(1)}) custom-call(bf16[192,4096]{1,0:T(8,128)(2,1)S(1)} %bitcast.11, bf16[192,4096]{1,0:T(8,128)(2,1)S(1)} %bitcast.9, bf16[192,4096]{1,0:T(8,128)(2,1)S(1)} %bitcast.15, bf16[192,4096]{1,0:T(8,128)(2,1)S(1)} %bitcast.16, f32[8,192,192]{2,1,0:T(8,128)S(1)} %get-tuple-element.23.inverse, ...), custom_call_target="tpu_custom_call" | custom-call | flops 1207959552 | bytes 6291456 | tf_op jit(solution)/shard_map/pallas_call | solution.py:144
  49.2 0.0 collective-permute-done.2.far_mirror
  49.2 1.1 %shard_map.62 = (f32[2,192,192]{2,1,0:T(8,128)S(1)}, f32[1,128]{1,0:T(1,128)S(1)}) custom-call(bf16[192,4096]{1,0:T(8,128)(2,1)S(1)} %bitcast.12, bf16[192,4096]{1,0:T(8,128)(2,1)S(1)} %collective-permute-done.2.far_mirror, bf16[192,4096]{1,0:T(8,128)(2,1)S(1)} %bitcast.10, f32[8,192,192]{2,1,0:T(8,128)S(1)} %get-tuple-element.23.inverse, ...), custom_call_target="tpu_custom_call" | custom-call | flops 603979776 | bytes 3145728 | tf_op jit(solution)/shard_map/pallas_call | solution.py:144
  50.4 4.0 %collective-permute-start.4 = (f32[1,4]{1,0:T(1,128)S(1)}, f32[1,4]{1,0:T(1,128)S(1)}, u32[]{:S(2)}, u32[]{:S(2)}) collective-permute-start(f32[1,4]{1,0:T(1,128)S(1)} %bitcast.17), channel_id=1, source_target_pairs={{0,1},{1,2},{2,3},{3,4},{4,5},{5,6},{6,7},{7,8},{8,9},{9,10},{10,1... | collective-permute-start | bytes 56 | tf_op jit(solution)/shard_map/ppermute | solution.py:20
  54.4 1.2 %shard_map.63 = f32[64,3,256]{2,1,0:T(4,128)} custom-call(f32[2,192,192]{2,1,0:T(8,128)S(1)} %get-tuple-element.30.refs_0_, f32[2,192,192]{2,1,0:T(8,128)S(1)} %get-tuple-element.31.refs_1_), custom_call_target="tpu_custom_call" | custom-call | flops 301989888 | bytes 1572864 | tf_op jit(solution)/shard_map/pallas_call | solution.py:144
  55.5 3.3 %collective-permute-done.4 = f32[1,4]{1,0:T(1,128)S(1)} collective-permute-done((f32[1,4]{1,0:T(1,128)S(1)}, f32[1,4]{1,0:T(1,128)S(1)}, u32[]{:S(2)}, u32[]{:S(2)}) %collective-permute-start.4) | collective-permute-done | bytes 48 | tf_op jit(solution)/shard_map/ppermute | solution.py:20
  58.9 3.9 %psum.7 = f32[1,4]{1,0:T(1,128)S(1)} all-reduce(f32[1,4]{1,0:T(1,128)S(1)} %compare_select_fusion), channel_id=1, replica_groups=mesh['z_hi'=4,'core'=2,'blk'=64] {'core'}, use_global_device_ids=true, to_apply=%region_0.1 | all-reduce | flops 4 | bytes 32 | tf_op jit(solution)/shard_map/psum | solution.py:218
  62.8 7.2 %all-to-all-start = ((f32[64,3,256]{2,1,0:T(4,128)}), f32[64,3,256]{2,1,0:T(4,128)S(1)}, u32[]{:S(2)}, u32[]{:S(2)}) async-start(f32[64,3,256]{2,1,0:T(4,128)} %shard_map.63), calls=%async_computation | async-start | bytes 524288 | tf_op jit(solution)/shard_map/all_to_all | solution.py:220
  70.0 14.9 %all-gather = f32[4,1,4]{2,1,0:T(1,128)S(1)} all-gather(f32[1,1,4]{2,1,0:T(1,128)S(1)} %bitcast.18), channel_id=1, replica_groups=mesh['z_hi'=4,'core'=2,'blk'=64] {'z_hi'}, dimensions={0}, use_global_device_ids=true | all-gather | bytes 80 | tf_op jit(solution)/shard_map/all_gather | solution.py:221
  84.9 0.5 reduce_sum.19
  85.4 0.0 all-to-all-done
  85.4 0.7 slice_reduce_fusion
  (1 shorter events, 0.0 us)
Async XLA Ops:
  0.6 37.3 %collective-permute-start.1 = (bf16[1,192,4096]{2,1,0:T(8,128)(2,1)}, bf16[1,192,4096]{2,1,0:T(8,128)(2,1)S(1)}, u32[]{:S(2)}, u32[]{:S(2)}) collective-permute-start(bf16[1,192,4096]{2,1,0:T(8,128)(2,1)} %param.4), channel_id=1, source_target_pairs={{0,2},{1,3},{2,4},{3,5},{4,6},{5,7},{6,8},{7,9},{8,10},{9,11},{10,... | collective-permute-start | bytes 4718600 | tf_op jit(solution)/shard_map/ppermute | solution.py:20
  4.6 42.5 %collective-permute-start = (bf16[1,192,4096]{2,1,0:T(8,128)(2,1)}, bf16[1,192,4096]{2,1,0:T(8,128)(2,1)S(1)}, u32[]{:S(2)}, u32[]{:S(2)}) collective-permute-start(bf16[1,192,4096]{2,1,0:T(8,128)(2,1)} %param.4), channel_id=1, source_target_pairs={{0,63},{1,0},{2,1},{3,2},{4,3},{5,4},{6,5},{7,6},{8,7},{9,8},{10,9... | collective-permute-start | bytes 4718600 | tf_op jit(solution)/shard_map/ppermute | solution.py:20
  12.5 34.6 %collective-permute-start.3 = (bf16[1,192,4096]{2,1,0:T(8,128)(2,1)}, bf16[1,192,4096]{2,1,0:T(8,128)(2,1)S(1)}, u32[]{:S(2)}, u32[]{:S(2)}) collective-permute-start(bf16[1,192,4096]{2,1,0:T(8,128)(2,1)} %param.4), channel_id=1, source_target_pairs={{0,64},{64,0},{1,65},{65,1},{2,66},{66,2},{3,67},{67,3},{4,68},{68... | collective-permute-start | bytes 4718600 | tf_op jit(solution)/shard_map/ppermute | solution.py:20
  16.1 1.4 %copy-start = (bf16[1,192,4096]{2,1,0:T(8,128)(2,1)S(1)}, bf16[1,192,4096]{2,1,0:T(8,128)(2,1)}, u32[]{:S(2)}) copy-start(bf16[1,192,4096]{2,1,0:T(8,128)(2,1)} %param.4) | copy-start | bytes 4718596
  17.5 0.7 copy-start.2
  18.2 0.7 copy-start.3
  18.8 27.4 %copy-start.1 = (bf16[1,192,4096]{2,1,0:T(8,128)(2,1)S(1)}, bf16[1,192,4096]{2,1,0:T(8,128)(2,1)}, u32[]{:S(2)}) copy-start(bf16[1,192,4096]{2,1,0:T(8,128)(2,1)} %param.4) | copy-start | bytes 4718596
  37.9 11.3 %collective-permute-start.2 = (bf16[192,4096]{1,0:T(8,128)(2,1)S(1)}, bf16[192,4096]{1,0:T(8,128)(2,1)S(1)}, u32[]{:S(2)}, u32[]{:S(2)}) collective-permute-start(bf16[192,4096]{1,0:T(8,128)(2,1)S(1)} %bitcast.13), channel_id=1, source_target_pairs={{0,64},{64,0},{1,65},{65,1},{2,66},{66,2},{3,67},{67,3},{4,68},{68... | collective-permute-start | bytes 4718600 | tf_op jit(solution)/shard_map/ppermute | solution.py:20
  50.4 8.5 %collective-permute-start.4 = (f32[1,4]{1,0:T(1,128)S(1)}, f32[1,4]{1,0:T(1,128)S(1)}, u32[]{:S(2)}, u32[]{:S(2)}) collective-permute-start(f32[1,4]{1,0:T(1,128)S(1)} %bitcast.17), channel_id=1, source_target_pairs={{0,1},{1,2},{2,3},{3,4},{4,5},{5,6},{6,7},{7,8},{8,9},{9,10},{10,1... | collective-permute-start | bytes 56 | tf_op jit(solution)/shard_map/ppermute | solution.py:20
  62.8 22.7 %all-to-all-start = ((f32[64,3,256]{2,1,0:T(4,128)}), f32[64,3,256]{2,1,0:T(4,128)S(1)}, u32[]{:S(2)}, u32[]{:S(2)}) async-start(f32[64,3,256]{2,1,0:T(4,128)} %shard_map.63), calls=%async_computation | async-start | bytes 524288 | tf_op jit(solution)/shard_map/all_to_all | solution.py:220

commit v5 on v4

--- a/solution.py
+++ b/solution.py
@@ -8,6 +8,7 @@
 
 STEPS = 4
 LANES = 128
+ROWS = 512
 GRP = ("z_hi", "core")
 VMEM_BYTES = 8 * 1024 * 1024
 FAR_PAIRS = ((0, 2),)
@@ -122,18 +123,29 @@
     )
     density = (heads + cross + cross.T) * scale
     width = density.shape[0]
-    peers, each, stride = spread.shape
-    panels = stride // LANES
-    for panel in range(panels):
-        part = density[:, panel * LANES : min(width, (panel + 1) * LANES)]
-        if part.shape[1] < LANES:
-            held[panel] = jnp.zeros(held.shape[1:], jnp.float32)
-        held[panel, :, : part.shape[1]] = part
+    held[0] = density[:, :LANES]
+    held[1, :, : width - LANES] = density[:, LANES:]
+    peers = spread.shape[0]
+    each = width // peers
+    tails = []
     for row in range(each):
-        for panel in range(panels):
-            spread[:, row, panel * LANES : (panel + 1) * LANES] = held[
-                panel, pl.Slice(row, peers, each), :
-            ]
+        spread[:, 0, row * LANES : (row + 1) * LANES] = held[0, pl.Slice(row, peers, each), :]
+        tails.append(held[1, pl.Slice(row, peers, each), :][:, : width - LANES])
+    tails.append(jnp.zeros_like(tails[0]))
+    for at in range(0, each, 2):
+        start = each * LANES + at * (width - LANES)
+        spread[:, 0, start : start + LANES] = jnp.concatenate(tails[at : at + 2], axis=1)
+
+
+def final_kernel(arrived, gathered, density, pair):
+    total = jnp.sum(arrived[...], axis=0)
+    each, width = density.shape
+    rest = width - LANES
+    for row in range(each):
+        density[row : row + 1, :LANES] = total[:, row * LANES : (row + 1) * LANES]
+        start = each * LANES + row * rest
+        density[row : row + 1, LANES:] = total[:, start : start + rest]
+    pair[...] = jnp.sum(gathered[...], axis=0, keepdims=True)
 
 
 def call(kernel, out_shape, operands, pairs, block, smem=0, scratch=()):
@@ -200,26 +212,31 @@
         len(LAST_PAIRS),
         own,
     )
+    energy = lax.psum(energy, "core")
+    passed = shifted(jnp.broadcast_to(energy, (ROWS, LANES)), "blk", 1)[:1, :STEPS]
+    energy, amps = lax.optimization_barrier((energy, amps))
     energy = energy[:, :STEPS]
-    passed = shifted(energy, "blk", 1)
     each = width // peers
-    panels = -(-width // LANES)
+    rest = width - LANES
     scale = 1.0 / (occ_count * STEPS)
     spread = call(
         lambda *refs: spread_kernel(scale, *refs),
-        jax.ShapeDtypeStruct((peers, each, panels * LANES), jnp.float32),
+        jax.ShapeDtypeStruct((peers, 1, each * LANES + (each + 1) * rest), jnp.float32),
         (amps, squares),
         1,
         own,
-        scratch=(pltpu.VMEM((panels, width, LANES), jnp.float32),),
+        scratch=(pltpu.VMEM((2, width, LANES), jnp.float32),),
     )
     odd = lax.broadcasted_iota(jnp.int32, energy.shape, 1) % 2 == 1
-    passed, spread = lax.optimization_barrier((passed, spread))
-    pair = lax.psum(jnp.where(odd, passed, energy), "core")
-    pair, spread = lax.optimization_barrier((pair, spread))
+    pair = jnp.where(odd, passed, energy)
     arrived = lax.all_to_all(spread, "blk", 0, 0, tiled=True)
-    pair = lax.all_gather(pair, "z_hi", axis=0, tiled=True).sum(axis=0, keepdims=True)
-    return arrived[:, :, :width].sum(axis=0), pair
+    gathered = lax.all_gather(pair, "z_hi", axis=0, tiled=True)
+    shapes = (
+        jax.ShapeDtypeStruct((each, width), jnp.float32),
+        jax.ShapeDtypeStruct((1, STEPS), jnp.float32),
+    )
+    density, pair = call(final_kernel, shapes, (arrived, gathered), 0, own)
+    return density, pair
 
 
 def solution(mesh):

time: 87.4 us -> 84 us (0.961)
  waiting for transfers between devices: 20.5 us -> 17.3 us
  blocking collectives: 18.8 us -> 16.7 us
  starting transfers between devices: 34.2 us -> 36.2 us
  other arithmetic: 1.21 us -> 0.01 us
    ppermute x5, waiting for transfers between devices: 20.5 us -> 17.2 us  [shifted(): lax.ppermute(shard, axis, [(i, (i + by) % peers) for i in range(peers)])]
    all_to_all x1, starting transfers between devices: 7.22 us -> 9.24 us  [local(): arrived = lax.all_to_all(spread, 'blk', 0, 0, tiled=True)]
    psum x1, blocking collectives: 3.89 us -> 2.5 us  [local(): energy = lax.psum(energy, 'core')]
    reduce_sum x2 -> x0, other arithmetic: 1.21 us -> none  [the longest x1 0.68 us: local(): return (arrived[:, :, :width].sum(axis=0), pair)]
    pallas_call x5 -> x6, Pallas kernels: 7.22 us -> 8.01 us  [call(): pl.pallas_call(kernel, out_shape=out_shape, in_specs=specs, out_specs=jax...]
where the time goes in v5:
time: 84 us; the launch traced here: 82.4 us
  starting transfers between devices  36.2 us (43%)
  waiting for transfers between devices  17.3 us (21%)
  blocking collectives  16.7 us (20%)
  Pallas kernels  8.01 us (10%)
  local copies, waits for them, and re-layouts  3.47 us (4%)
    ppermute x5, starting transfers between devices, shifted(): lax.ppermute(shard, axis, [(i, (i + by) % peers) for i in range(peers)])  27 us
    ppermute x5, waiting for transfers between devices, shifted(): lax.ppermute(shard, axis, [(i, (i + by) % peers) for i in range(peers)])  17.2 us
    all_gather x1, blocking collectives, local(): gathered = lax.all_gather(pair, 'z_hi', axis=0, tiled=True)  14.2 us
    all_to_all x1, starting transfers between devices, local(): arrived = lax.all_to_all(spread, 'blk', 0, 0, tiled=True)  9.24 us
    pallas_call x6, Pallas kernels, call(): pl.pallas_call(kernel, out_shape=out_shape, in_specs=specs, out_specs=jax...  8.01 us
    unnamed x8, local copies, waits for them, and re-layouts  2.75 us
    psum x1, blocking collectives, local(): energy = lax.psum(energy, 'core')  2.5 us
  transfers between devices with their start and end apart: 6, of which 2 were waited for; matrix products, arithmetic and copies ran while one was open for 1% of the time, Pallas kernels for 7%

profile of v5, /device:TPU:1, one launch (start us, length us, event | category | flops | bytes accessed | tf_op | source)
XLA Modules:
  0.0 82.4 jit_solution(12767171505035354862)
XLA Ops:
  0.6 4.0 %collective-permute-start.1 = (bf16[1,192,4096]{2,1,0:T(8,128)(2,1)}, bf16[1,192,4096]{2,1,0:T(8,128)(2,1)S(1)}, u32[]{:S(2)}, u32[]{:S(2)}) collective-permute-start(bf16[1,192,4096]{2,1,0:T(8,128)(2,1)} %param.4), channel_id=1, source_target_pairs={{0,2},{1,3},{2,4},{3,5},{4,6},{5,7},{6,8},{7,9},{8,10},{9,11},{10,... | collective-permute-start | bytes 4718600 | tf_op jit(solution)/shard_map/ppermute | solution.py:21
  4.6 7.9 %collective-permute-start = (bf16[1,192,4096]{2,1,0:T(8,128)(2,1)}, bf16[1,192,4096]{2,1,0:T(8,128)(2,1)S(1)}, u32[]{:S(2)}, u32[]{:S(2)}) collective-permute-start(bf16[1,192,4096]{2,1,0:T(8,128)(2,1)} %param.4), channel_id=1, source_target_pairs={{0,63},{1,0},{2,1},{3,2},{4,3},{5,4},{6,5},{7,6},{8,7},{9,8},{10,9... | collective-permute-start | bytes 4718600 | tf_op jit(solution)/shard_map/ppermute | solution.py:21
  12.5 2.9 %collective-permute-start.3 = (bf16[1,192,4096]{2,1,0:T(8,128)(2,1)}, bf16[1,192,4096]{2,1,0:T(8,128)(2,1)S(1)}, u32[]{:S(2)}, u32[]{:S(2)}) collective-permute-start(bf16[1,192,4096]{2,1,0:T(8,128)(2,1)} %param.4), channel_id=1, source_target_pairs={{0,64},{64,0},{1,65},{65,1},{2,66},{66,2},{3,67},{67,3},{4,68},{68... | collective-permute-start | bytes 4718600 | tf_op jit(solution)/shard_map/ppermute | solution.py:21
  15.4 0.7 broadcast_in_dim.10.virt
  16.1 0.0 copy-start
  16.1 1.4 %copy-done = bf16[1,192,4096]{2,1,0:T(8,128)(2,1)S(1)} copy-done((bf16[1,192,4096]{2,1,0:T(8,128)(2,1)S(1)}, bf16[1,192,4096]{2,1,0:T(8,128)(2,1)}, u32[]{:S(2)}) %copy-start) | copy-done | bytes 1572888
  17.5 0.0 copy-start.2
  17.5 0.7 copy-done.2
  18.2 0.0 copy-start.3
  18.2 0.7 copy-done.3
  18.8 0.0 copy-start.1
  18.8 2.0 %shard_map.59 = (f32[8,192,192]{2,1,0:T(8,128)S(1)}, f32[2,192,192]{2,1,0:T(8,128)S(1)}, f32[1,128]{1,0:T(1,128)S(1)}) custom-call(s32[64]{0:T(128)S(1)} %copy-done.3, f32[400]{0:T(512)S(1)} %copy-done.2, f32[1,1536]{1,0:T(1,128)S(1)} %broadcast_in_dim.10.virt, bf16[192,4096]{1,0:T(8,128)(2,1)S(1)} %bitcast.8), custom_call_target="tpu_custom_call" | custom-call | flops 301989888 | bytes 1572864 | tf_op jit(solution)/shard_map/pallas_call | solution.py:156
  20.8 17.1 %collective-permute-done.1 = bf16[1,192,4096]{2,1,0:T(8,128)(2,1)S(1)} collective-permute-done((bf16[1,192,4096]{2,1,0:T(8,128)(2,1)}, bf16[1,192,4096]{2,1,0:T(8,128)(2,1)S(1)}, u32[]{:S(2)}, u32[]{:S(2)}) %collective-permute-start.1) | collective-permute-done | bytes 1572896 | tf_op jit(solution)/shard_map/ppermute | solution.py:21
  37.9 8.3 %collective-permute-start.2 = (bf16[192,4096]{1,0:T(8,128)(2,1)S(1)}, bf16[192,4096]{1,0:T(8,128)(2,1)S(1)}, u32[]{:S(2)}, u32[]{:S(2)}) collective-permute-start(bf16[192,4096]{1,0:T(8,128)(2,1)S(1)} %bitcast.14), channel_id=1, source_target_pairs={{0,64},{64,0},{1,65},{65,1},{2,66},{66,2},{3,67},{67,3},{4,68},{68... | collective-permute-start | bytes 4718600 | tf_op jit(solution)/shard_map/ppermute | solution.py:21
  46.2 0.0 copy-done.1
  46.2 0.9 %shard_map.60 = (f32[2,192,192]{2,1,0:T(8,128)S(1)}, f32[1,128]{1,0:T(1,128)S(1)}) custom-call(bf16[192,4096]{1,0:T(8,128)(2,1)S(1)} %bitcast.9, bf16[192,4096]{1,0:T(8,128)(2,1)S(1)} %bitcast.15, f32[8,192,192]{2,1,0:T(8,128)S(1)} %get-tuple-element.21.inverse, f32[2,192,192]{2,1,0:T(8,128)S(1)} %get-tuple-element.22.squares_in, ...), custom_call_target="tpu_custom_call" | custom-call | flops 301989888 | bytes 1572864 | tf_op jit(solution)/shard_map/pallas_call | solution.py:156
  47.1 0.0 collective-permute-done
  47.1 0.0 collective-permute-done.3
  47.1 2.1 %shard_map.61 = (f32[2,192,192]{2,1,0:T(8,128)S(1)}, f32[1,128]{1,0:T(1,128)S(1)}) custom-call(bf16[192,4096]{1,0:T(8,128)(2,1)S(1)} %bitcast.12, bf16[192,4096]{1,0:T(8,128)(2,1)S(1)} %bitcast.10, bf16[192,4096]{1,0:T(8,128)(2,1)S(1)} %bitcast.16, bf16[192,4096]{1,0:T(8,128)(2,1)S(1)} %bitcast.17, f32[8,192,192]{2,1,0:T(8,128)S(1)} %get-tuple-element.21.inverse, ...), custom_call_target="tpu_custom_call" | custom-call | flops 1207959552 | bytes 6291456 | tf_op jit(solution)/shard_map/pallas_call | solution.py:156
  49.2 0.0 collective-permute-done.2.far_mirror
  49.2 1.1 %shard_map.62 = (f32[2,192,192]{2,1,0:T(8,128)S(1)}, f32[1,128]{1,0:T(1,128)S(1)}) custom-call(bf16[192,4096]{1,0:T(8,128)(2,1)S(1)} %bitcast.13, bf16[192,4096]{1,0:T(8,128)(2,1)S(1)} %collective-permute-done.2.far_mirror, bf16[192,4096]{1,0:T(8,128)(2,1)S(1)} %bitcast.11, f32[8,192,192]{2,1,0:T(8,128)S(1)} %get-tuple-element.21.inverse, ...), custom_call_target="tpu_custom_call" | custom-call | flops 603979776 | bytes 3145728 | tf_op jit(solution)/shard_map/pallas_call | solution.py:156
  50.4 2.5 %psum.7 = f32[1,128]{1,0:T(1,128)S(1)} all-reduce(f32[1,128]{1,0:T(1,128)S(1)} %get-tuple-element.27), channel_id=1, replica_groups=mesh['z_hi'=4,'core'=2,'blk'=64] {'core'}, use_global_device_ids=true, to_apply=%region_0.0 | all-reduce | flops 128 | bytes 1024 | tf_op jit(solution)/shard_map/psum | solution.py:215
  52.9 4.0 %collective-permute-start.4 = (f32[512,128]{1,0:T(8,128)S(1)}, f32[512,128]{1,0:T(8,128)S(1)}, u32[]{:S(2)}, u32[]{:S(2)}) collective-permute-start(f32[512,128]{1,0:T(8,128)S(1)} %broadcast_in_dim.12), channel_id=1, source_target_pairs={{0,1},{1,2},{2,3},{3,4},{4,5},{5,6},{6,7},{7,8},{8,9},{9,10},{10,1... | collective-permute-start | bytes 786440 | tf_op jit(solution)/shard_map/ppermute | solution.py:21
  56.9 1.2 %shard_map.63 = f32[64,1,640]{2,1,0:T(1,128)} custom-call(f32[2,192,192]{2,1,0:T(8,128)S(1)} %get-tuple-element.29.refs_0_, f32[2,192,192]{2,1,0:T(8,128)S(1)} %get-tuple-element.30.refs_1_), custom_call_target="tpu_custom_call" | custom-call | flops 301989888 | bytes 1572864 | tf_op jit(solution)/shard_map/pallas_call | solution.py:156
  58.1 9.2 %all-to-all-start = ((f32[64,1,640]{2,1,0:T(1,128)}), f32[64,1,640]{2,1,0:T(1,128)S(1)}, u32[]{:S(2)}, u32[]{:S(2)}) async-start(f32[64,1,640]{2,1,0:T(1,128)} %shard_map.63), calls=%async_computation | async-start | bytes 327680 | tf_op jit(solution)/shard_map/all_to_all | solution.py:232
  67.3 0.1 collective-permute-done.4
  67.4 14.2 %all-gather = f32[4,1,4]{2,1,0:T(1,128)S(1)} all-gather(f32[1,1,4]{2,1,0:T(1,128)S(1)} %fusion), channel_id=1, replica_groups=mesh['z_hi'=4,'core'=2,'blk'=64] {'z_hi'}, dimensions={0}, use_global_device_ids=true | all-gather | bytes 80 | tf_op jit(solution)/shard_map/all_gather | solution.py:233
  81.7 0.0 all-to-all-done.arrived
  81.7 0.8 shard_map.64
  (2 shorter events, 0.0 us)
Async XLA Ops:
  0.6 37.3 %collective-permute-start.1 = (bf16[1,192,4096]{2,1,0:T(8,128)(2,1)}, bf16[1,192,4096]{2,1,0:T(8,128)(2,1)S(1)}, u32[]{:S(2)}, u32[]{:S(2)}) collective-permute-start(bf16[1,192,4096]{2,1,0:T(8,128)(2,1)} %param.4), channel_id=1, source_target_pairs={{0,2},{1,3},{2,4},{3,5},{4,6},{5,7},{6,8},{7,9},{8,10},{9,11},{10,... | collective-permute-start | bytes 4718600 | tf_op jit(solution)/shard_map/ppermute | solution.py:21
  4.6 42.5 %collective-permute-start = (bf16[1,192,4096]{2,1,0:T(8,128)(2,1)}, bf16[1,192,4096]{2,1,0:T(8,128)(2,1)S(1)}, u32[]{:S(2)}, u32[]{:S(2)}) collective-permute-start(bf16[1,192,4096]{2,1,0:T(8,128)(2,1)} %param.4), channel_id=1, source_target_pairs={{0,63},{1,0},{2,1},{3,2},{4,3},{5,4},{6,5},{7,6},{8,7},{9,8},{10,9... | collective-permute-start | bytes 4718600 | tf_op jit(solution)/shard_map/ppermute | solution.py:21
  12.5 34.6 %collective-permute-start.3 = (bf16[1,192,4096]{2,1,0:T(8,128)(2,1)}, bf16[1,192,4096]{2,1,0:T(8,128)(2,1)S(1)}, u32[]{:S(2)}, u32[]{:S(2)}) collective-permute-start(bf16[1,192,4096]{2,1,0:T(8,128)(2,1)} %param.4), channel_id=1, source_target_pairs={{0,64},{64,0},{1,65},{65,1},{2,66},{66,2},{3,67},{67,3},{4,68},{68... | collective-permute-start | bytes 4718600 | tf_op jit(solution)/shard_map/ppermute | solution.py:21
  16.1 1.4 %copy-start = (bf16[1,192,4096]{2,1,0:T(8,128)(2,1)S(1)}, bf16[1,192,4096]{2,1,0:T(8,128)(2,1)}, u32[]{:S(2)}) copy-start(bf16[1,192,4096]{2,1,0:T(8,128)(2,1)} %param.4) | copy-start | bytes 4718596
  17.5 0.7 copy-start.2
  18.2 0.7 copy-start.3
  18.8 27.4 %copy-start.1 = (bf16[1,192,4096]{2,1,0:T(8,128)(2,1)S(1)}, bf16[1,192,4096]{2,1,0:T(8,128)(2,1)}, u32[]{:S(2)}) copy-start(bf16[1,192,4096]{2,1,0:T(8,128)(2,1)} %param.4) | copy-start | bytes 4718596
  37.9 11.3 %collective-permute-start.2 = (bf16[192,4096]{1,0:T(8,128)(2,1)S(1)}, bf16[192,4096]{1,0:T(8,128)(2,1)S(1)}, u32[]{:S(2)}, u32[]{:S(2)}) collective-permute-start(bf16[192,4096]{1,0:T(8,128)(2,1)S(1)} %bitcast.14), channel_id=1, source_target_pairs={{0,64},{64,0},{1,65},{65,1},{2,66},{66,2},{3,67},{67,3},{4,68},{68... | collective-permute-start | bytes 4718600 | tf_op jit(solution)/shard_map/ppermute | solution.py:21
  52.9 14.5 %collective-permute-start.4 = (f32[512,128]{1,0:T(8,128)S(1)}, f32[512,128]{1,0:T(8,128)S(1)}, u32[]{:S(2)}, u32[]{:S(2)}) collective-permute-start(f32[512,128]{1,0:T(8,128)S(1)} %broadcast_in_dim.12), channel_id=1, source_target_pairs={{0,1},{1,2},{2,3},{3,4},{4,5},{5,6},{6,7},{7,8},{8,9},{9,10},{10,1... | collective-permute-start | bytes 786440 | tf_op jit(solution)/shard_map/ppermute | solution.py:21
  58.1 23.6 %all-to-all-start = ((f32[64,1,640]{2,1,0:T(1,128)}), f32[64,1,640]{2,1,0:T(1,128)S(1)}, u32[]{:S(2)}, u32[]{:S(2)}) async-start(f32[64,1,640]{2,1,0:T(1,128)} %shard_map.63), calls=%async_computation | async-start | bytes 327680 | tf_op jit(solution)/shard_map/all_to_all | solution.py:232

commit v6 on v5

--- a/solution.py
+++ b/solution.py
@@ -8,7 +8,7 @@
 
 STEPS = 4
 LANES = 128
-ROWS = 512
+ROWS = 384
 GRP = ("z_hi", "core")
 VMEM_BYTES = 8 * 1024 * 1024
 FAR_PAIRS = ((0, 2),)
@@ -212,10 +212,7 @@
         len(LAST_PAIRS),
         own,
     )
-    energy = lax.psum(energy, "core")
-    passed = shifted(jnp.broadcast_to(energy, (ROWS, LANES)), "blk", 1)[:1, :STEPS]
-    energy, amps = lax.optimization_barrier((energy, amps))
-    energy = energy[:, :STEPS]
+    swapped = shifted(energy, "core", 1)
     each = width // peers
     rest = width - LANES
     scale = 1.0 / (occ_count * STEPS)
@@ -227,6 +224,10 @@
         own,
         scratch=(pltpu.VMEM((2, width, LANES), jnp.float32),),
     )
+    swapped, spread = lax.optimization_barrier((swapped, spread))
+    energy = energy + swapped
+    passed = shifted(jnp.broadcast_to(energy, (ROWS, LANES)), "blk", 1)[:1, :STEPS]
+    energy = energy[:, :STEPS]
     odd = lax.broadcasted_iota(jnp.int32, energy.shape, 1) % 2 == 1
     pair = jnp.where(odd, passed, energy)
     arrived = lax.all_to_all(spread, "blk", 0, 0, tiled=True)

time: 84 us -> 83.7 us (level)
  blocking collectives: 16.7 us -> 14.2 us
  starting transfers between devices: 36.2 us -> 38.5 us
    psum x1 -> x0, blocking collectives: 2.5 us -> none  [local(): energy = lax.psum(energy, 'core')]
    ppermute x5 -> x6, starting transfers between devices: 27 us -> 29.3 us  [shifted(): lax.ppermute(shard, axis, [(i, (i + by) % peers) for i in range(peers)])]
    ppermute x5 -> x6, waiting for transfers between devices: 17.2 us -> 17.3 us  [shifted(): lax.ppermute(shard, axis, [(i, (i + by) % peers) for i in range(peers)])]
  transfers between devices with their start and end apart: 6 -> 7, of which waited for: 2 -> 2; matrix products, arithmetic and copies ran while one was open for 1% -> 1% of each run, Pallas kernels for 7% -> 7%
where the time goes in v6:
time: 83.7 us; the launch traced here: 82.2 us
  starting transfers between devices  38.5 us (46%)
  waiting for transfers between devices  17.3 us (21%)
  blocking collectives  14.2 us (17%)
  Pallas kernels  8.01 us (10%)
  local copies, waits for them, and re-layouts  3.47 us (4%)
    ppermute x6, starting transfers between devices, shifted(): lax.ppermute(shard, axis, [(i, (i + by) % peers) for i in range(peers)])  29.3 us
    ppermute x6, waiting for transfers between devices, shifted(): lax.ppermute(shard, axis, [(i, (i + by) % peers) for i in range(peers)])  17.3 us
    all_gather x1, blocking collectives, local(): gathered = lax.all_gather(pair, 'z_hi', axis=0, tiled=True)  14.2 us
    all_to_all x1, starting transfers between devices, local(): arrived = lax.all_to_all(spread, 'blk', 0, 0, tiled=True)  9.25 us
    pallas_call x6, Pallas kernels, call(): pl.pallas_call(kernel, out_shape=out_shape, in_specs=specs, out_specs=jax...  8.01 us
    unnamed x8, local copies, waits for them, and re-layouts  2.75 us
  transfers between devices with their start and end apart: 7, of which 2 were waited for; matrix products, arithmetic and copies ran while one was open for 1% of the time, Pallas kernels for 7%

profile of v6, /device:TPU:1, one launch (start us, length us, event | category | flops | bytes accessed | tf_op | source)
XLA Modules:
  0.0 82.2 jit_solution(1795683525988337634)
XLA Ops:
  0.6 4.0 %collective-permute-start.1 = (bf16[1,192,4096]{2,1,0:T(8,128)(2,1)}, bf16[1,192,4096]{2,1,0:T(8,128)(2,1)S(1)}, u32[]{:S(2)}, u32[]{:S(2)}) collective-permute-start(bf16[1,192,4096]{2,1,0:T(8,128)(2,1)} %param.4), channel_id=1, source_target_pairs={{0,2},{1,3},{2,4},{3,5},{4,6},{5,7},{6,8},{7,9},{8,10},{9,11},{10,... | collective-permute-start | bytes 4718600 | tf_op jit(solution)/shard_map/ppermute | solution.py:21
  4.6 7.9 %collective-permute-start = (bf16[1,192,4096]{2,1,0:T(8,128)(2,1)}, bf16[1,192,4096]{2,1,0:T(8,128)(2,1)S(1)}, u32[]{:S(2)}, u32[]{:S(2)}) collective-permute-start(bf16[1,192,4096]{2,1,0:T(8,128)(2,1)} %param.4), channel_id=1, source_target_pairs={{0,63},{1,0},{2,1},{3,2},{4,3},{5,4},{6,5},{7,6},{8,7},{9,8},{10,9... | collective-permute-start | bytes 4718600 | tf_op jit(solution)/shard_map/ppermute | solution.py:21
  12.5 2.9 %collective-permute-start.3 = (bf16[1,192,4096]{2,1,0:T(8,128)(2,1)}, bf16[1,192,4096]{2,1,0:T(8,128)(2,1)S(1)}, u32[]{:S(2)}, u32[]{:S(2)}) collective-permute-start(bf16[1,192,4096]{2,1,0:T(8,128)(2,1)} %param.4), channel_id=1, source_target_pairs={{0,64},{64,0},{1,65},{65,1},{2,66},{66,2},{3,67},{67,3},{4,68},{68... | collective-permute-start | bytes 4718600 | tf_op jit(solution)/shard_map/ppermute | solution.py:21
  15.4 0.7 broadcast_in_dim.10.virt
  16.1 0.0 copy-start
  16.1 1.4 %copy-done = bf16[1,192,4096]{2,1,0:T(8,128)(2,1)S(1)} copy-done((bf16[1,192,4096]{2,1,0:T(8,128)(2,1)S(1)}, bf16[1,192,4096]{2,1,0:T(8,128)(2,1)}, u32[]{:S(2)}) %copy-start) | copy-done | bytes 1572888
  17.5 0.0 copy-start.2
  17.5 0.7 copy-done.2
  18.2 0.0 copy-start.3
  18.2 0.7 copy-done.3
  18.8 0.0 copy-start.1
  18.8 2.0 %shard_map.59 = (f32[8,192,192]{2,1,0:T(8,128)S(1)}, f32[2,192,192]{2,1,0:T(8,128)S(1)}, f32[1,128]{1,0:T(1,128)S(1)}) custom-call(s32[64]{0:T(128)S(1)} %copy-done.3, f32[400]{0:T(512)S(1)} %copy-done.2, f32[1,1536]{1,0:T(1,128)S(1)} %broadcast_in_dim.10.virt, bf16[192,4096]{1,0:T(8,128)(2,1)S(1)} %bitcast.8), custom_call_target="tpu_custom_call" | custom-call | flops 301989888 | bytes 1572864 | tf_op jit(solution)/shard_map/pallas_call | solution.py:156
  20.8 17.1 %collective-permute-done.1 = bf16[1,192,4096]{2,1,0:T(8,128)(2,1)S(1)} collective-permute-done((bf16[1,192,4096]{2,1,0:T(8,128)(2,1)}, bf16[1,192,4096]{2,1,0:T(8,128)(2,1)S(1)}, u32[]{:S(2)}, u32[]{:S(2)}) %collective-permute-start.1) | collective-permute-done | bytes 1572896 | tf_op jit(solution)/shard_map/ppermute | solution.py:21
  37.9 8.3 %collective-permute-start.2 = (bf16[192,4096]{1,0:T(8,128)(2,1)S(1)}, bf16[192,4096]{1,0:T(8,128)(2,1)S(1)}, u32[]{:S(2)}, u32[]{:S(2)}) collective-permute-start(bf16[192,4096]{1,0:T(8,128)(2,1)S(1)} %bitcast.14), channel_id=1, source_target_pairs={{0,64},{64,0},{1,65},{65,1},{2,66},{66,2},{3,67},{67,3},{4,68},{68... | collective-permute-start | bytes 4718600 | tf_op jit(solution)/shard_map/ppermute | solution.py:21
  46.2 0.0 copy-done.1
  46.2 0.9 %shard_map.60 = (f32[2,192,192]{2,1,0:T(8,128)S(1)}, f32[1,128]{1,0:T(1,128)S(1)}) custom-call(bf16[192,4096]{1,0:T(8,128)(2,1)S(1)} %bitcast.9, bf16[192,4096]{1,0:T(8,128)(2,1)S(1)} %bitcast.15, f32[8,192,192]{2,1,0:T(8,128)S(1)} %get-tuple-element.21.inverse, f32[2,192,192]{2,1,0:T(8,128)S(1)} %get-tuple-element.22.squares_in, ...), custom_call_target="tpu_custom_call" | custom-call | flops 301989888 | bytes 1572864 | tf_op jit(solution)/shard_map/pallas_call | solution.py:156
  47.1 0.0 collective-permute-done
  47.1 0.0 collective-permute-done.3
  47.1 2.1 %shard_map.61 = (f32[2,192,192]{2,1,0:T(8,128)S(1)}, f32[1,128]{1,0:T(1,128)S(1)}) custom-call(bf16[192,4096]{1,0:T(8,128)(2,1)S(1)} %bitcast.12, bf16[192,4096]{1,0:T(8,128)(2,1)S(1)} %bitcast.10, bf16[192,4096]{1,0:T(8,128)(2,1)S(1)} %bitcast.16, bf16[192,4096]{1,0:T(8,128)(2,1)S(1)} %bitcast.17, f32[8,192,192]{2,1,0:T(8,128)S(1)} %get-tuple-element.21.inverse, ...), custom_call_target="tpu_custom_call" | custom-call | flops 1207959552 | bytes 6291456 | tf_op jit(solution)/shard_map/pallas_call | solution.py:156
  49.2 0.0 collective-permute-done.2.far_mirror
  49.2 1.1 %shard_map.62 = (f32[2,192,192]{2,1,0:T(8,128)S(1)}, f32[1,128]{1,0:T(1,128)S(1)}) custom-call(bf16[192,4096]{1,0:T(8,128)(2,1)S(1)} %bitcast.13, bf16[192,4096]{1,0:T(8,128)(2,1)S(1)} %collective-permute-done.2.far_mirror, bf16[192,4096]{1,0:T(8,128)(2,1)S(1)} %bitcast.11, f32[8,192,192]{2,1,0:T(8,128)S(1)} %get-tuple-element.21.inverse, ...), custom_call_target="tpu_custom_call" | custom-call | flops 603979776 | bytes 3145728 | tf_op jit(solution)/shard_map/pallas_call | solution.py:156
  50.4 2.3 %collective-permute-start.4 = (f32[1,128]{1,0:T(1,128)S(1)}, f32[1,128]{1,0:T(1,128)S(1)}, u32[]{:S(2)}, u32[]{:S(2)}) collective-permute-start(f32[1,128]{1,0:T(1,128)S(1)} %get-tuple-element.27), channel_id=1, source_target_pairs={{0,64},{64,0},{1,65},{65,1},{2,66},{66,2},{3,67},{67,3},{4,68},{68... | collective-permute-start | bytes 1544 | tf_op jit(solution)/shard_map/ppermute | solution.py:21
  52.6 1.2 %shard_map.63 = f32[64,1,640]{2,1,0:T(1,128)} custom-call(f32[2,192,192]{2,1,0:T(8,128)S(1)} %get-tuple-element.28.refs_0_, f32[2,192,192]{2,1,0:T(8,128)S(1)} %get-tuple-element.29.refs_1_), custom_call_target="tpu_custom_call" | custom-call | flops 301989888 | bytes 1572864 | tf_op jit(solution)/shard_map/pallas_call | solution.py:156
  53.8 0.0 collective-permute-done.4
  53.9 4.0 %collective-permute-start.5 = (f32[384,128]{1,0:T(8,128)S(1)}, f32[384,128]{1,0:T(8,128)S(1)}, u32[]{:S(2)}, u32[]{:S(2)}) collective-permute-start(f32[384,128]{1,0:T(8,128)S(1)} %broadcast_in_dim.12), channel_id=1, source_target_pairs={{0,1},{1,2},{2,3},{3,4},{4,5},{5,6},{6,7},{7,8},{8,9},{9,10},{10,1... | collective-permute-start | bytes 589832 | tf_op jit(solution)/shard_map/ppermute | solution.py:21
  57.9 9.2 %all-to-all-start = ((f32[64,1,640]{2,1,0:T(1,128)}), f32[64,1,640]{2,1,0:T(1,128)S(1)}, u32[]{:S(2)}, u32[]{:S(2)}) async-start(f32[64,1,640]{2,1,0:T(1,128)} %shard_map.63), calls=%async_computation | async-start | bytes 327680 | tf_op jit(solution)/shard_map/all_to_all | solution.py:233
  67.1 0.1 collective-permute-done.5
  67.3 14.2 %all-gather = f32[4,1,4]{2,1,0:T(1,128)S(1)} all-gather(f32[1,1,4]{2,1,0:T(1,128)S(1)} %fusion), channel_id=1, replica_groups=mesh['z_hi'=4,'core'=2,'blk'=64] {'z_hi'}, dimensions={0}, use_global_device_ids=true | all-gather | bytes 80 | tf_op jit(solution)/shard_map/all_gather | solution.py:234
  81.5 0.0 all-to-all-done.arrived
  81.5 0.8 shard_map.64
  (3 shorter events, 0.0 us)
Async XLA Ops:
  0.6 37.3 %collective-permute-start.1 = (bf16[1,192,4096]{2,1,0:T(8,128)(2,1)}, bf16[1,192,4096]{2,1,0:T(8,128)(2,1)S(1)}, u32[]{:S(2)}, u32[]{:S(2)}) collective-permute-start(bf16[1,192,4096]{2,1,0:T(8,128)(2,1)} %param.4), channel_id=1, source_target_pairs={{0,2},{1,3},{2,4},{3,5},{4,6},{5,7},{6,8},{7,9},{8,10},{9,11},{10,... | collective-permute-start | bytes 4718600 | tf_op jit(solution)/shard_map/ppermute | solution.py:21
  4.6 42.5 %collective-permute-start = (bf16[1,192,4096]{2,1,0:T(8,128)(2,1)}, bf16[1,192,4096]{2,1,0:T(8,128)(2,1)S(1)}, u32[]{:S(2)}, u32[]{:S(2)}) collective-permute-start(bf16[1,192,4096]{2,1,0:T(8,128)(2,1)} %param.4), channel_id=1, source_target_pairs={{0,63},{1,0},{2,1},{3,2},{4,3},{5,4},{6,5},{7,6},{8,7},{9,8},{10,9... | collective-permute-start | bytes 4718600 | tf_op jit(solution)/shard_map/ppermute | solution.py:21
  12.5 34.6 %collective-permute-start.3 = (bf16[1,192,4096]{2,1,0:T(8,128)(2,1)}, bf16[1,192,4096]{2,1,0:T(8,128)(2,1)S(1)}, u32[]{:S(2)}, u32[]{:S(2)}) collective-permute-start(bf16[1,192,4096]{2,1,0:T(8,128)(2,1)} %param.4), channel_id=1, source_target_pairs={{0,64},{64,0},{1,65},{65,1},{2,66},{66,2},{3,67},{67,3},{4,68},{68... | collective-permute-start | bytes 4718600 | tf_op jit(solution)/shard_map/ppermute | solution.py:21
  16.1 1.4 %copy-start = (bf16[1,192,4096]{2,1,0:T(8,128)(2,1)S(1)}, bf16[1,192,4096]{2,1,0:T(8,128)(2,1)}, u32[]{:S(2)}) copy-start(bf16[1,192,4096]{2,1,0:T(8,128)(2,1)} %param.4) | copy-start | bytes 4718596
  17.5 0.7 copy-start.2
  18.2 0.7 copy-start.3
  18.8 27.4 %copy-start.1 = (bf16[1,192,4096]{2,1,0:T(8,128)(2,1)S(1)}, bf16[1,192,4096]{2,1,0:T(8,128)(2,1)}, u32[]{:S(2)}) copy-start(bf16[1,192,4096]{2,1,0:T(8,128)(2,1)} %param.4) | copy-start | bytes 4718596
  37.9 11.3 %collective-permute-start.2 = (bf16[192,4096]{1,0:T(8,128)(2,1)S(1)}, bf16[192,4096]{1,0:T(8,128)(2,1)S(1)}, u32[]{:S(2)}, u32[]{:S(2)}) collective-permute-start(bf16[192,4096]{1,0:T(8,128)(2,1)S(1)} %bitcast.14), channel_id=1, source_target_pairs={{0,64},{64,0},{1,65},{65,1},{2,66},{66,2},{3,67},{67,3},{4,68},{68... | collective-permute-start | bytes 4718600 | tf_op jit(solution)/shard_map/ppermute | solution.py:21
  50.4 3.5 %collective-permute-start.4 = (f32[1,128]{1,0:T(1,128)S(1)}, f32[1,128]{1,0:T(1,128)S(1)}, u32[]{:S(2)}, u32[]{:S(2)}) collective-permute-start(f32[1,128]{1,0:T(1,128)S(1)} %get-tuple-element.27), channel_id=1, source_target_pairs={{0,64},{64,0},{1,65},{65,1},{2,66},{66,2},{3,67},{67,3},{4,68},{68... | collective-permute-start | bytes 1544 | tf_op jit(solution)/shard_map/ppermute | solution.py:21
  53.9 13.4 %collective-permute-start.5 = (f32[384,128]{1,0:T(8,128)S(1)}, f32[384,128]{1,0:T(8,128)S(1)}, u32[]{:S(2)}, u32[]{:S(2)}) collective-permute-start(f32[384,128]{1,0:T(8,128)S(1)} %broadcast_in_dim.12), channel_id=1, source_target_pairs={{0,1},{1,2},{2,3},{3,4},{4,5},{5,6},{6,7},{7,8},{8,9},{9,10},{10,1... | collective-permute-start | bytes 589832 | tf_op jit(solution)/shard_map/ppermute | solution.py:21
  57.9 23.6 %all-to-all-start = ((f32[64,1,640]{2,1,0:T(1,128)}), f32[64,1,640]{2,1,0:T(1,128)S(1)}, u32[]{:S(2)}, u32[]{:S(2)}) async-start(f32[64,1,640]{2,1,0:T(1,128)} %shard_map.63), calls=%async_computation | async-start | bytes 327680 | tf_op jit(solution)/shard_map/all_to_all | solution.py:233

commit v7 on v6

--- a/solution.py
+++ b/solution.py
@@ -28,7 +28,7 @@
 
 
 def slot_of(row, col):
-    return row + 2 * (col // 2)
+    return 2 * row + col // 2
 
 
 def amplitude_of(row, col, rows, cols, inverse):
@@ -70,8 +70,8 @@
     across = lax.broadcasted_iota(jnp.int32, (width, width), 1)
     col_own = jnp.sum(jnp.where(down == across, row_own, 0.0), axis=1, keepdims=True)
     level_own = occ[window[block]]
-    level_next = occ[window[lax.rem(block + 1, orbitals)]]
-    level_far = occ[window[lax.rem(block + orbitals - 2, orbitals)]]
+    level_next = occ[window[lax.rem(block + 2, orbitals)]]
+    level_far = occ[window[lax.rem(block + orbitals - 1, orbitals)]]
     for row, level_row in enumerate((level_own, level_next)):
         for col in range(4):
             denominator = (
@@ -169,8 +169,8 @@
 
 
 def local(ints, occ_energy, occ_window, virt_energy):
-    far = shifted(ints, "blk", 2)[0]
-    near = shifted(ints, "blk", -1)[0]
+    far = shifted(ints, "blk", 1)[0]
+    near = shifted(ints, "blk", -2)[0]
     own = ints[0]
     width = own.shape[0]
     occ_count = occ_window.shape[0]
@@ -226,10 +226,10 @@
     )
     swapped, spread = lax.optimization_barrier((swapped, spread))
     energy = energy + swapped
-    passed = shifted(jnp.broadcast_to(energy, (ROWS, LANES)), "blk", 1)[:1, :STEPS]
+    passed = shifted(jnp.broadcast_to(energy, (ROWS, LANES)), "blk", 2)[:1, :STEPS]
     energy = energy[:, :STEPS]
-    odd = lax.broadcasted_iota(jnp.int32, energy.shape, 1) % 2 == 1
-    pair = jnp.where(odd, passed, energy)
+    later = lax.broadcasted_iota(jnp.int32, energy.shape, 1) >= 2
+    pair = jnp.where(later, passed, energy)
     arrived = lax.all_to_all(spread, "blk", 0, 0, tiled=True)
     gathered = lax.all_gather(pair, "z_hi", axis=0, tiled=True)
     shapes = (

time: 83.7 us -> 83.7 us (level)
  starting transfers between devices: 38.5 us -> 35.5 us
  waiting for transfers between devices: 17.3 us -> 20.3 us
    ppermute x6, waiting for transfers between devices: 17.3 us -> 20.3 us  [shifted(): lax.ppermute(shard, axis, [(i, (i + by) % peers) for i in range(peers)])]
    ppermute x6, starting transfers between devices: 29.3 us -> 26.8 us  [shifted(): lax.ppermute(shard, axis, [(i, (i + by) % peers) for i in range(peers)])]
where the time goes in v7:
time: 83.7 us; the launch traced here: 82.2 us
  starting transfers between devices  35.5 us (42%)
  waiting for transfers between devices  20.3 us (24%)
  blocking collectives  14.2 us (17%)
  Pallas kernels  8 us (10%)
  local copies, waits for them, and re-layouts  3.47 us (4%)
    ppermute x6, starting transfers between devices, shifted(): lax.ppermute(shard, axis, [(i, (i + by) % peers) for i in range(peers)])  26.8 us
    ppermute x6, waiting for transfers between devices, shifted(): lax.ppermute(shard, axis, [(i, (i + by) % peers) for i in range(peers)])  20.3 us
    all_gather x1, blocking collectives, local(): gathered = lax.all_gather(pair, 'z_hi', axis=0, tiled=True)  14.2 us
    all_to_all x1, starting transfers between devices, local(): arrived = lax.all_to_all(spread, 'blk', 0, 0, tiled=True)  8.7 us
    pallas_call x6, Pallas kernels, call(): pl.pallas_call(kernel, out_shape=out_shape, in_specs=specs, out_specs=jax...  8 us
    unnamed x8, local copies, waits for them, and re-layouts  2.75 us
  transfers between devices with their start and end apart: 7, of which 2 were waited for; matrix products, arithmetic and copies ran while one was open for 1% of the time, Pallas kernels for 7%

profile of v7, /device:TPU:1, one launch (start us, length us, event | category | flops | bytes accessed | tf_op | source)
XLA Modules:
  0.0 82.2 jit_solution(11785159088223047679)
XLA Ops:
  0.6 4.8 %collective-permute-start.1 = (bf16[1,192,4096]{2,1,0:T(8,128)(2,1)}, bf16[1,192,4096]{2,1,0:T(8,128)(2,1)S(1)}, u32[]{:S(2)}, u32[]{:S(2)}) collective-permute-start(bf16[1,192,4096]{2,1,0:T(8,128)(2,1)} %param.4), channel_id=1, source_target_pairs={{0,1},{1,2},{2,3},{3,4},{4,5},{5,6},{6,7},{7,8},{8,9},{9,10},{10,1... | collective-permute-start | bytes 4718600 | tf_op jit(solution)/shard_map/ppermute | solution.py:21
  5.5 7.3 %collective-permute-start = (bf16[1,192,4096]{2,1,0:T(8,128)(2,1)}, bf16[1,192,4096]{2,1,0:T(8,128)(2,1)S(1)}, u32[]{:S(2)}, u32[]{:S(2)}) collective-permute-start(bf16[1,192,4096]{2,1,0:T(8,128)(2,1)} %param.4), channel_id=1, source_target_pairs={{0,62},{1,63},{2,0},{3,1},{4,2},{5,3},{6,4},{7,5},{8,6},{9,7},{10,... | collective-permute-start | bytes 4718600 | tf_op jit(solution)/shard_map/ppermute | solution.py:21
  12.8 3.1 %collective-permute-start.3 = (bf16[1,192,4096]{2,1,0:T(8,128)(2,1)}, bf16[1,192,4096]{2,1,0:T(8,128)(2,1)S(1)}, u32[]{:S(2)}, u32[]{:S(2)}) collective-permute-start(bf16[1,192,4096]{2,1,0:T(8,128)(2,1)} %param.4), channel_id=1, source_target_pairs={{0,64},{64,0},{1,65},{65,1},{2,66},{66,2},{3,67},{67,3},{4,68},{68... | collective-permute-start | bytes 4718600 | tf_op jit(solution)/shard_map/ppermute | solution.py:21
  15.9 0.7 broadcast_in_dim.10.virt
  16.6 0.0 copy-start
  16.6 1.4 %copy-done = bf16[1,192,4096]{2,1,0:T(8,128)(2,1)S(1)} copy-done((bf16[1,192,4096]{2,1,0:T(8,128)(2,1)S(1)}, bf16[1,192,4096]{2,1,0:T(8,128)(2,1)}, u32[]{:S(2)}) %copy-start) | copy-done | bytes 1572888
  18.0 0.0 copy-start.2
  18.0 0.7 copy-done.2
  18.7 0.0 copy-start.3
  18.7 0.7 copy-done.3
  19.4 0.0 copy-start.1
  19.4 2.0 %shard_map.59 = (f32[8,192,192]{2,1,0:T(8,128)S(1)}, f32[2,192,192]{2,1,0:T(8,128)S(1)}, f32[1,128]{1,0:T(1,128)S(1)}) custom-call(s32[64]{0:T(128)S(1)} %copy-done.3, f32[400]{0:T(512)S(1)} %copy-done.2, f32[1,1536]{1,0:T(1,128)S(1)} %broadcast_in_dim.10.virt, bf16[192,4096]{1,0:T(8,128)(2,1)S(1)} %bitcast.8), custom_call_target="tpu_custom_call" | custom-call | flops 301989888 | bytes 1572864 | tf_op jit(solution)/shard_map/pallas_call | solution.py:156
  21.4 19.3 %collective-permute-done.1 = bf16[1,192,4096]{2,1,0:T(8,128)(2,1)S(1)} collective-permute-done((bf16[1,192,4096]{2,1,0:T(8,128)(2,1)}, bf16[1,192,4096]{2,1,0:T(8,128)(2,1)S(1)}, u32[]{:S(2)}, u32[]{:S(2)}) %collective-permute-start.1) | collective-permute-done | bytes 1572896 | tf_op jit(solution)/shard_map/ppermute | solution.py:21
  40.7 7.3 %collective-permute-start.2 = (bf16[192,4096]{1,0:T(8,128)(2,1)S(1)}, bf16[192,4096]{1,0:T(8,128)(2,1)S(1)}, u32[]{:S(2)}, u32[]{:S(2)}) collective-permute-start(bf16[192,4096]{1,0:T(8,128)(2,1)S(1)} %bitcast.14), channel_id=1, source_target_pairs={{0,64},{64,0},{1,65},{65,1},{2,66},{66,2},{3,67},{67,3},{4,68},{68... | collective-permute-start | bytes 4718600 | tf_op jit(solution)/shard_map/ppermute | solution.py:21
  48.0 0.0 copy-done.1
  48.0 0.9 %shard_map.60 = (f32[2,192,192]{2,1,0:T(8,128)S(1)}, f32[1,128]{1,0:T(1,128)S(1)}) custom-call(bf16[192,4096]{1,0:T(8,128)(2,1)S(1)} %bitcast.9, bf16[192,4096]{1,0:T(8,128)(2,1)S(1)} %bitcast.15, f32[8,192,192]{2,1,0:T(8,128)S(1)} %get-tuple-element.21.inverse, f32[2,192,192]{2,1,0:T(8,128)S(1)} %get-tuple-element.22.squares_in, ...), custom_call_target="tpu_custom_call" | custom-call | flops 301989888 | bytes 1572864 | tf_op jit(solution)/shard_map/pallas_call | solution.py:156
  48.9 0.0 collective-permute-done
  48.9 0.0 collective-permute-done.3
  48.9 2.1 %shard_map.61 = (f32[2,192,192]{2,1,0:T(8,128)S(1)}, f32[1,128]{1,0:T(1,128)S(1)}) custom-call(bf16[192,4096]{1,0:T(8,128)(2,1)S(1)} %bitcast.12, bf16[192,4096]{1,0:T(8,128)(2,1)S(1)} %bitcast.10, bf16[192,4096]{1,0:T(8,128)(2,1)S(1)} %bitcast.16, bf16[192,4096]{1,0:T(8,128)(2,1)S(1)} %bitcast.17, f32[8,192,192]{2,1,0:T(8,128)S(1)} %get-tuple-element.21.inverse, ...), custom_call_target="tpu_custom_call" | custom-call | flops 1207959552 | bytes 6291456 | tf_op jit(solution)/shard_map/pallas_call | solution.py:156
  51.0 0.0 collective-permute-done.2.far_mirror
  51.0 1.1 %shard_map.62 = (f32[2,192,192]{2,1,0:T(8,128)S(1)}, f32[1,128]{1,0:T(1,128)S(1)}) custom-call(bf16[192,4096]{1,0:T(8,128)(2,1)S(1)} %bitcast.13, bf16[192,4096]{1,0:T(8,128)(2,1)S(1)} %collective-permute-done.2.far_mirror, bf16[192,4096]{1,0:T(8,128)(2,1)S(1)} %bitcast.11, f32[8,192,192]{2,1,0:T(8,128)S(1)} %get-tuple-element.21.inverse, ...), custom_call_target="tpu_custom_call" | custom-call | flops 603979776 | bytes 3145728 | tf_op jit(solution)/shard_map/pallas_call | solution.py:156
  52.2 2.3 %collective-permute-start.4 = (f32[1,128]{1,0:T(1,128)S(1)}, f32[1,128]{1,0:T(1,128)S(1)}, u32[]{:S(2)}, u32[]{:S(2)}) collective-permute-start(f32[1,128]{1,0:T(1,128)S(1)} %get-tuple-element.27), channel_id=1, source_target_pairs={{0,64},{64,0},{1,65},{65,1},{2,66},{66,2},{3,67},{67,3},{4,68},{68... | collective-permute-start | bytes 1544 | tf_op jit(solution)/shard_map/ppermute | solution.py:21
  54.5 1.2 %shard_map.63 = f32[64,1,640]{2,1,0:T(1,128)} custom-call(f32[2,192,192]{2,1,0:T(8,128)S(1)} %get-tuple-element.28.refs_0_, f32[2,192,192]{2,1,0:T(8,128)S(1)} %get-tuple-element.29.refs_1_), custom_call_target="tpu_custom_call" | custom-call | flops 301989888 | bytes 1572864 | tf_op jit(solution)/shard_map/pallas_call | solution.py:156
  55.7 0.0 collective-permute-done.4
  55.7 1.9 %collective-permute-start.5 = (f32[384,128]{1,0:T(8,128)S(1)}, f32[384,128]{1,0:T(8,128)S(1)}, u32[]{:S(2)}, u32[]{:S(2)}) collective-permute-start(f32[384,128]{1,0:T(8,128)S(1)} %broadcast_in_dim.12), channel_id=1, source_target_pairs={{0,2},{1,3},{2,4},{3,5},{4,6},{5,7},{6,8},{7,9},{8,10},{9,11},{10,... | collective-permute-start | bytes 589832 | tf_op jit(solution)/shard_map/ppermute | solution.py:21
  57.6 8.7 %all-to-all-start = ((f32[64,1,640]{2,1,0:T(1,128)}), f32[64,1,640]{2,1,0:T(1,128)S(1)}, u32[]{:S(2)}, u32[]{:S(2)}) async-start(f32[64,1,640]{2,1,0:T(1,128)} %shard_map.63), calls=%async_computation | async-start | bytes 327680 | tf_op jit(solution)/shard_map/all_to_all | solution.py:233
  66.3 0.9 %collective-permute-done.5 = f32[384,128]{1,0:T(8,128)S(1)} collective-permute-done((f32[384,128]{1,0:T(8,128)S(1)}, f32[384,128]{1,0:T(8,128)S(1)}, u32[]{:S(2)}, u32[]{:S(2)}) %collective-permute-start.5) | collective-permute-done | bytes 196640 | tf_op jit(solution)/shard_map/ppermute | solution.py:21
  67.3 14.2 %all-gather = f32[4,1,4]{2,1,0:T(1,128)S(1)} all-gather(f32[1,1,4]{2,1,0:T(1,128)S(1)} %fusion), channel_id=1, replica_groups=mesh['z_hi'=4,'core'=2,'blk'=64] {'z_hi'}, dimensions={0}, use_global_device_ids=true | all-gather | bytes 80 | tf_op jit(solution)/shard_map/all_gather | solution.py:234
  81.5 0.0 all-to-all-done.arrived
  81.5 0.8 shard_map.64
  (3 shorter events, 0.0 us)
Async XLA Ops:
  0.6 40.0 %collective-permute-start.1 = (bf16[1,192,4096]{2,1,0:T(8,128)(2,1)}, bf16[1,192,4096]{2,1,0:T(8,128)(2,1)S(1)}, u32[]{:S(2)}, u32[]{:S(2)}) collective-permute-start(bf16[1,192,4096]{2,1,0:T(8,128)(2,1)} %param.4), channel_id=1, source_target_pairs={{0,1},{1,2},{2,3},{3,4},{4,5},{5,6},{6,7},{7,8},{8,9},{9,10},{10,1... | collective-permute-start | bytes 4718600 | tf_op jit(solution)/shard_map/ppermute | solution.py:21
  5.5 43.4 %collective-permute-start = (bf16[1,192,4096]{2,1,0:T(8,128)(2,1)}, bf16[1,192,4096]{2,1,0:T(8,128)(2,1)S(1)}, u32[]{:S(2)}, u32[]{:S(2)}) collective-permute-start(bf16[1,192,4096]{2,1,0:T(8,128)(2,1)} %param.4), channel_id=1, source_target_pairs={{0,62},{1,63},{2,0},{3,1},{4,2},{5,3},{6,4},{7,5},{8,6},{9,7},{10,... | collective-permute-start | bytes 4718600 | tf_op jit(solution)/shard_map/ppermute | solution.py:21
  12.8 36.1 %collective-permute-start.3 = (bf16[1,192,4096]{2,1,0:T(8,128)(2,1)}, bf16[1,192,4096]{2,1,0:T(8,128)(2,1)S(1)}, u32[]{:S(2)}, u32[]{:S(2)}) collective-permute-start(bf16[1,192,4096]{2,1,0:T(8,128)(2,1)} %param.4), channel_id=1, source_target_pairs={{0,64},{64,0},{1,65},{65,1},{2,66},{66,2},{3,67},{67,3},{4,68},{68... | collective-permute-start | bytes 4718600 | tf_op jit(solution)/shard_map/ppermute | solution.py:21
  16.6 1.4 %copy-start = (bf16[1,192,4096]{2,1,0:T(8,128)(2,1)S(1)}, bf16[1,192,4096]{2,1,0:T(8,128)(2,1)}, u32[]{:S(2)}) copy-start(bf16[1,192,4096]{2,1,0:T(8,128)(2,1)} %param.4) | copy-start | bytes 4718596
  18.0 0.7 copy-start.2
  18.7 0.7 copy-start.3
  19.4 28.6 %copy-start.1 = (bf16[1,192,4096]{2,1,0:T(8,128)(2,1)S(1)}, bf16[1,192,4096]{2,1,0:T(8,128)(2,1)}, u32[]{:S(2)}) copy-start(bf16[1,192,4096]{2,1,0:T(8,128)(2,1)} %param.4) | copy-start | bytes 4718596
  40.7 10.4 %collective-permute-start.2 = (bf16[192,4096]{1,0:T(8,128)(2,1)S(1)}, bf16[192,4096]{1,0:T(8,128)(2,1)S(1)}, u32[]{:S(2)}, u32[]{:S(2)}) collective-permute-start(bf16[192,4096]{1,0:T(8,128)(2,1)S(1)} %bitcast.14), channel_id=1, source_target_pairs={{0,64},{64,0},{1,65},{65,1},{2,66},{66,2},{3,67},{67,3},{4,68},{68... | collective-permute-start | bytes 4718600 | tf_op jit(solution)/shard_map/ppermute | solution.py:21
  52.2 3.5 %collective-permute-start.4 = (f32[1,128]{1,0:T(1,128)S(1)}, f32[1,128]{1,0:T(1,128)S(1)}, u32[]{:S(2)}, u32[]{:S(2)}) collective-permute-start(f32[1,128]{1,0:T(1,128)S(1)} %get-tuple-element.27), channel_id=1, source_target_pairs={{0,64},{64,0},{1,65},{65,1},{2,66},{66,2},{3,67},{67,3},{4,68},{68... | collective-permute-start | bytes 1544 | tf_op jit(solution)/shard_map/ppermute | solution.py:21
  55.7 11.6 %collective-permute-start.5 = (f32[384,128]{1,0:T(8,128)S(1)}, f32[384,128]{1,0:T(8,128)S(1)}, u32[]{:S(2)}, u32[]{:S(2)}) collective-permute-start(f32[384,128]{1,0:T(8,128)S(1)} %broadcast_in_dim.12), channel_id=1, source_target_pairs={{0,2},{1,3},{2,4},{3,5},{4,6},{5,7},{6,8},{7,9},{8,10},{9,11},{10,... | collective-permute-start | bytes 589832 | tf_op jit(solution)/shard_map/ppermute | solution.py:21
  57.6 23.9 %all-to-all-start = ((f32[64,1,640]{2,1,0:T(1,128)}), f32[64,1,640]{2,1,0:T(1,128)S(1)}, u32[]{:S(2)}, u32[]{:S(2)}) async-start(f32[64,1,640]{2,1,0:T(1,128)} %shard_map.63), calls=%async_computation | async-start | bytes 327680 | tf_op jit(solution)/shard_map/all_to_all | solution.py:233

commit v8 on v6

--- a/solution.py
+++ b/solution.py
@@ -97,14 +97,15 @@
     squares[0], squares[1] = add_squares(squares_in[0], squares_in[1], amps)
 
 
-def near_kernel(near, own, far, own_mirror, inverse, squares_in, energy_in, squares, energy):
+def near_kernel(near, own, far, own_mirror, inverse, squares_in, energy_in, density, energy):
     amps, products = [], []
     for row, col in NEAR_PAIRS:
         amp, product = amplitude_of(row, col, (own, near), (own, own_mirror, far), inverse)
         amps.append(amp)
         products.append((slot_of(row, col), product))
     energy[...] = add_energies(energy_in[...], products)
-    squares[0], squares[1] = add_squares(squares_in[0], squares_in[1], amps)
+    heads, cross = add_squares(squares_in[0], squares_in[1], amps)
+    density[...] = heads + cross + cross.T
 
 
 def last_kernel(near, far_mirror, own, inverse, energy_in, amps, energy):
@@ -117,11 +118,13 @@
     energy[...] = add_energies(energy_in[...], products) * (-1.0 / (width * width))
 
 
-def spread_kernel(scale, amps, squares, spread, held):
-    heads, cross = add_squares(
-        squares[0], squares[1], [amps[at] for at in range(amps.shape[0])]
-    )
-    density = (heads + cross + cross.T) * scale
+def spread_kernel(scale, amps, density_in, spread, held):
+    density = density_in[...]
+    for at in range(amps.shape[0]):
+        head = amps[at].astype(jnp.bfloat16)
+        rest = (amps[at] - head.astype(jnp.float32)).astype(jnp.bfloat16)
+        density = density + nt_dot(head, head) + nt_dot(head, rest) + nt_dot(rest, head)
+    density = density * scale
     width = density.shape[0]
     held[0] = density[:, :LANES]
     held[1, :, : width - LANES] = density[:, LANES:]
@@ -198,9 +201,9 @@
         len(FAR_PAIRS),
         own,
     )
-    squares, energy = call(
+    density, energy = call(
         near_kernel,
-        (squares_of(2), line),
+        (jax.ShapeDtypeStruct((width, width), jnp.float32), line),
         (near, own, far, own_mirror, inverse, squares, energy),
         len(NEAR_PAIRS),
         own,
@@ -219,7 +222,7 @@
     spread = call(
         lambda *refs: spread_kernel(scale, *refs),
         jax.ShapeDtypeStruct((peers, 1, each * LANES + (each + 1) * rest), jnp.float32),
-        (amps, squares),
+        (amps, density),
         1,
         own,
         scratch=(pltpu.VMEM((2, width, LANES), jnp.float32),),

time: 83.7 us -> 83.7 us (level)
  no operation moved by 1% of the time
where the time goes in v8:
time: 83.7 us; the launch traced here: 82.2 us
  starting transfers between devices  38.5 us (46%)
  waiting for transfers between devices  17.3 us (21%)
  blocking collectives  14.1 us (17%)
  Pallas kernels  8.06 us (10%)
  local copies, waits for them, and re-layouts  3.47 us (4%)
    ppermute x6, starting transfers between devices, shifted(): lax.ppermute(shard, axis, [(i, (i + by) % peers) for i in range(peers)])  29.2 us
    ppermute x6, waiting for transfers between devices, shifted(): lax.ppermute(shard, axis, [(i, (i + by) % peers) for i in range(peers)])  17.3 us
    all_gather x1, blocking collectives, local(): gathered = lax.all_gather(pair, 'z_hi', axis=0, tiled=True)  14.1 us
    all_to_all x1, starting transfers between devices, local(): arrived = lax.all_to_all(spread, 'blk', 0, 0, tiled=True)  9.35 us
    pallas_call x6, Pallas kernels, call(): pl.pallas_call(kernel, out_shape=out_shape, in_specs=specs, out_specs=jax...  8.06 us
    unnamed x8, local copies, waits for them, and re-layouts  2.75 us
  transfers between devices with their start and end apart: 7, of which 2 were waited for; matrix products, arithmetic and copies ran while one was open for 1% of the time, Pallas kernels for 7%

profile of v8, /device:TPU:1, one launch (start us, length us, event | category | flops | bytes accessed | tf_op | source)
XLA Modules:
  0.0 82.2 jit_solution(14521041345404954198)
XLA Ops:
  0.6 4.0 %collective-permute-start.1 = (bf16[1,192,4096]{2,1,0:T(8,128)(2,1)}, bf16[1,192,4096]{2,1,0:T(8,128)(2,1)S(1)}, u32[]{:S(2)}, u32[]{:S(2)}) collective-permute-start(bf16[1,192,4096]{2,1,0:T(8,128)(2,1)} %param.4), channel_id=1, source_target_pairs={{0,2},{1,3},{2,4},{3,5},{4,6},{5,7},{6,8},{7,9},{8,10},{9,11},{10,... | collective-permute-start | bytes 4718600 | tf_op jit(solution)/shard_map/ppermute | solution.py:21
  4.6 7.9 %collective-permute-start = (bf16[1,192,4096]{2,1,0:T(8,128)(2,1)}, bf16[1,192,4096]{2,1,0:T(8,128)(2,1)S(1)}, u32[]{:S(2)}, u32[]{:S(2)}) collective-permute-start(bf16[1,192,4096]{2,1,0:T(8,128)(2,1)} %param.4), channel_id=1, source_target_pairs={{0,63},{1,0},{2,1},{3,2},{4,3},{5,4},{6,5},{7,6},{8,7},{9,8},{10,9... | collective-permute-start | bytes 4718600 | tf_op jit(solution)/shard_map/ppermute | solution.py:21
  12.5 2.9 %collective-permute-start.3 = (bf16[1,192,4096]{2,1,0:T(8,128)(2,1)}, bf16[1,192,4096]{2,1,0:T(8,128)(2,1)S(1)}, u32[]{:S(2)}, u32[]{:S(2)}) collective-permute-start(bf16[1,192,4096]{2,1,0:T(8,128)(2,1)} %param.4), channel_id=1, source_target_pairs={{0,64},{64,0},{1,65},{65,1},{2,66},{66,2},{3,67},{67,3},{4,68},{68... | collective-permute-start | bytes 4718600 | tf_op jit(solution)/shard_map/ppermute | solution.py:21
  15.4 0.7 broadcast_in_dim.10.virt
  16.1 0.0 copy-start
  16.1 1.4 %copy-done = bf16[1,192,4096]{2,1,0:T(8,128)(2,1)S(1)} copy-done((bf16[1,192,4096]{2,1,0:T(8,128)(2,1)S(1)}, bf16[1,192,4096]{2,1,0:T(8,128)(2,1)}, u32[]{:S(2)}) %copy-start) | copy-done | bytes 1572888
  17.5 0.0 copy-start.2
  17.5 0.7 copy-done.2
  18.2 0.0 copy-start.3
  18.2 0.7 copy-done.3
  18.8 0.0 copy-start.1
  18.8 2.0 %shard_map.59 = (f32[8,192,192]{2,1,0:T(8,128)S(1)}, f32[2,192,192]{2,1,0:T(8,128)S(1)}, f32[1,128]{1,0:T(1,128)S(1)}) custom-call(s32[64]{0:T(128)S(1)} %copy-done.3, f32[400]{0:T(512)S(1)} %copy-done.2, f32[1,1536]{1,0:T(1,128)S(1)} %broadcast_in_dim.10.virt, bf16[192,4096]{1,0:T(8,128)(2,1)S(1)} %bitcast.8), custom_call_target="tpu_custom_call" | custom-call | flops 301989888 | bytes 1572864 | tf_op jit(solution)/shard_map/pallas_call | solution.py:159
  20.8 17.1 %collective-permute-done.1 = bf16[1,192,4096]{2,1,0:T(8,128)(2,1)S(1)} collective-permute-done((bf16[1,192,4096]{2,1,0:T(8,128)(2,1)}, bf16[1,192,4096]{2,1,0:T(8,128)(2,1)S(1)}, u32[]{:S(2)}, u32[]{:S(2)}) %collective-permute-start.1) | collective-permute-done | bytes 1572896 | tf_op jit(solution)/shard_map/ppermute | solution.py:21
  37.9 8.3 %collective-permute-start.2 = (bf16[192,4096]{1,0:T(8,128)(2,1)S(1)}, bf16[192,4096]{1,0:T(8,128)(2,1)S(1)}, u32[]{:S(2)}, u32[]{:S(2)}) collective-permute-start(bf16[192,4096]{1,0:T(8,128)(2,1)S(1)} %bitcast.14), channel_id=1, source_target_pairs={{0,64},{64,0},{1,65},{65,1},{2,66},{66,2},{3,67},{67,3},{4,68},{68... | collective-permute-start | bytes 4718600 | tf_op jit(solution)/shard_map/ppermute | solution.py:21
  46.2 0.0 copy-done.1
  46.2 0.9 %shard_map.60 = (f32[2,192,192]{2,1,0:T(8,128)S(1)}, f32[1,128]{1,0:T(1,128)S(1)}) custom-call(bf16[192,4096]{1,0:T(8,128)(2,1)S(1)} %bitcast.9, bf16[192,4096]{1,0:T(8,128)(2,1)S(1)} %bitcast.15, f32[8,192,192]{2,1,0:T(8,128)S(1)} %get-tuple-element.21.inverse, f32[2,192,192]{2,1,0:T(8,128)S(1)} %get-tuple-element.22.squares_in, ...), custom_call_target="tpu_custom_call" | custom-call | flops 301989888 | bytes 1572864 | tf_op jit(solution)/shard_map/pallas_call | solution.py:159
  47.1 0.0 collective-permute-done
  47.1 0.0 collective-permute-done.3
  47.1 2.2 %shard_map.61 = (f32[192,192]{1,0:T(8,128)S(1)}, f32[1,128]{1,0:T(1,128)S(1)}) custom-call(bf16[192,4096]{1,0:T(8,128)(2,1)S(1)} %bitcast.12, bf16[192,4096]{1,0:T(8,128)(2,1)S(1)} %bitcast.10, bf16[192,4096]{1,0:T(8,128)(2,1)S(1)} %bitcast.16, bf16[192,4096]{1,0:T(8,128)(2,1)S(1)} %bitcast.17, f32[8,192,192]{2,1,0:T(8,128)S(1)} %get-tuple-element.21.inverse, ...), custom_call_target="tpu_custom_call" | custom-call | flops 1207959552 | bytes 6291456 | tf_op jit(solution)/shard_map/pallas_call | solution.py:159
  49.3 0.0 collective-permute-done.2.far_mirror
  49.3 1.1 %shard_map.62 = (f32[2,192,192]{2,1,0:T(8,128)S(1)}, f32[1,128]{1,0:T(1,128)S(1)}) custom-call(bf16[192,4096]{1,0:T(8,128)(2,1)S(1)} %bitcast.13, bf16[192,4096]{1,0:T(8,128)(2,1)S(1)} %collective-permute-done.2.far_mirror, bf16[192,4096]{1,0:T(8,128)(2,1)S(1)} %bitcast.11, f32[8,192,192]{2,1,0:T(8,128)S(1)} %get-tuple-element.21.inverse, ...), custom_call_target="tpu_custom_call" | custom-call | flops 603979776 | bytes 3145728 | tf_op jit(solution)/shard_map/pallas_call | solution.py:159
  50.4 2.2 %collective-permute-start.4 = (f32[1,128]{1,0:T(1,128)S(1)}, f32[1,128]{1,0:T(1,128)S(1)}, u32[]{:S(2)}, u32[]{:S(2)}) collective-permute-start(f32[1,128]{1,0:T(1,128)S(1)} %get-tuple-element.27), channel_id=1, source_target_pairs={{0,64},{64,0},{1,65},{65,1},{2,66},{66,2},{3,67},{67,3},{4,68},{68... | collective-permute-start | bytes 1544 | tf_op jit(solution)/shard_map/ppermute | solution.py:21
  52.6 1.1 %shard_map.63 = f32[64,1,640]{2,1,0:T(1,128)} custom-call(f32[2,192,192]{2,1,0:T(8,128)S(1)} %get-tuple-element.28.refs_0_, f32[192,192]{1,0:T(8,128)S(1)} %get-tuple-element.29.refs_1_), custom_call_target="tpu_custom_call" | custom-call | flops 301989888 | bytes 1572864 | tf_op jit(solution)/shard_map/pallas_call | solution.py:159
  53.8 0.0 collective-permute-done.4
  53.8 4.0 %collective-permute-start.5 = (f32[384,128]{1,0:T(8,128)S(1)}, f32[384,128]{1,0:T(8,128)S(1)}, u32[]{:S(2)}, u32[]{:S(2)}) collective-permute-start(f32[384,128]{1,0:T(8,128)S(1)} %broadcast_in_dim.12), channel_id=1, source_target_pairs={{0,1},{1,2},{2,3},{3,4},{4,5},{5,6},{6,7},{7,8},{8,9},{9,10},{10,1... | collective-permute-start | bytes 589832 | tf_op jit(solution)/shard_map/ppermute | solution.py:21
  57.8 9.3 %all-to-all-start = ((f32[64,1,640]{2,1,0:T(1,128)}), f32[64,1,640]{2,1,0:T(1,128)S(1)}, u32[]{:S(2)}, u32[]{:S(2)}) async-start(f32[64,1,640]{2,1,0:T(1,128)} %shard_map.63), calls=%async_computation | async-start | bytes 327680 | tf_op jit(solution)/shard_map/all_to_all | solution.py:236
  67.2 0.1 collective-permute-done.5
  67.3 14.1 %all-gather = f32[4,1,4]{2,1,0:T(1,128)S(1)} all-gather(f32[1,1,4]{2,1,0:T(1,128)S(1)} %fusion), channel_id=1, replica_groups=mesh['z_hi'=4,'core'=2,'blk'=64] {'z_hi'}, dimensions={0}, use_global_device_ids=true | all-gather | bytes 80 | tf_op jit(solution)/shard_map/all_gather | solution.py:237
  81.4 0.0 all-to-all-done.arrived
  81.4 0.8 shard_map.64
  (3 shorter events, 0.0 us)
Async XLA Ops:
  0.6 37.3 %collective-permute-start.1 = (bf16[1,192,4096]{2,1,0:T(8,128)(2,1)}, bf16[1,192,4096]{2,1,0:T(8,128)(2,1)S(1)}, u32[]{:S(2)}, u32[]{:S(2)}) collective-permute-start(bf16[1,192,4096]{2,1,0:T(8,128)(2,1)} %param.4), channel_id=1, source_target_pairs={{0,2},{1,3},{2,4},{3,5},{4,6},{5,7},{6,8},{7,9},{8,10},{9,11},{10,... | collective-permute-start | bytes 4718600 | tf_op jit(solution)/shard_map/ppermute | solution.py:21
  4.6 42.5 %collective-permute-start = (bf16[1,192,4096]{2,1,0:T(8,128)(2,1)}, bf16[1,192,4096]{2,1,0:T(8,128)(2,1)S(1)}, u32[]{:S(2)}, u32[]{:S(2)}) collective-permute-start(bf16[1,192,4096]{2,1,0:T(8,128)(2,1)} %param.4), channel_id=1, source_target_pairs={{0,63},{1,0},{2,1},{3,2},{4,3},{5,4},{6,5},{7,6},{8,7},{9,8},{10,9... | collective-permute-start | bytes 4718600 | tf_op jit(solution)/shard_map/ppermute | solution.py:21
  12.5 34.6 %collective-permute-start.3 = (bf16[1,192,4096]{2,1,0:T(8,128)(2,1)}, bf16[1,192,4096]{2,1,0:T(8,128)(2,1)S(1)}, u32[]{:S(2)}, u32[]{:S(2)}) collective-permute-start(bf16[1,192,4096]{2,1,0:T(8,128)(2,1)} %param.4), channel_id=1, source_target_pairs={{0,64},{64,0},{1,65},{65,1},{2,66},{66,2},{3,67},{67,3},{4,68},{68... | collective-permute-start | bytes 4718600 | tf_op jit(solution)/shard_map/ppermute | solution.py:21
  16.1 1.4 %copy-start = (bf16[1,192,4096]{2,1,0:T(8,128)(2,1)S(1)}, bf16[1,192,4096]{2,1,0:T(8,128)(2,1)}, u32[]{:S(2)}) copy-start(bf16[1,192,4096]{2,1,0:T(8,128)(2,1)} %param.4) | copy-start | bytes 4718596
  17.5 0.7 copy-start.2
  18.2 0.7 copy-start.3
  18.8 27.4 %copy-start.1 = (bf16[1,192,4096]{2,1,0:T(8,128)(2,1)S(1)}, bf16[1,192,4096]{2,1,0:T(8,128)(2,1)}, u32[]{:S(2)}) copy-start(bf16[1,192,4096]{2,1,0:T(8,128)(2,1)} %param.4) | copy-start | bytes 4718596
  37.9 11.3 %collective-permute-start.2 = (bf16[192,4096]{1,0:T(8,128)(2,1)S(1)}, bf16[192,4096]{1,0:T(8,128)(2,1)S(1)}, u32[]{:S(2)}, u32[]{:S(2)}) collective-permute-start(bf16[192,4096]{1,0:T(8,128)(2,1)S(1)} %bitcast.14), channel_id=1, source_target_pairs={{0,64},{64,0},{1,65},{65,1},{2,66},{66,2},{3,67},{67,3},{4,68},{68... | collective-permute-start | bytes 4718600 | tf_op jit(solution)/shard_map/ppermute | solution.py:21
  50.4 3.4 %collective-permute-start.4 = (f32[1,128]{1,0:T(1,128)S(1)}, f32[1,128]{1,0:T(1,128)S(1)}, u32[]{:S(2)}, u32[]{:S(2)}) collective-permute-start(f32[1,128]{1,0:T(1,128)S(1)} %get-tuple-element.27), channel_id=1, source_target_pairs={{0,64},{64,0},{1,65},{65,1},{2,66},{66,2},{3,67},{67,3},{4,68},{68... | collective-permute-start | bytes 1544 | tf_op jit(solution)/shard_map/ppermute | solution.py:21
  53.8 13.5 %collective-permute-start.5 = (f32[384,128]{1,0:T(8,128)S(1)}, f32[384,128]{1,0:T(8,128)S(1)}, u32[]{:S(2)}, u32[]{:S(2)}) collective-permute-start(f32[384,128]{1,0:T(8,128)S(1)} %broadcast_in_dim.12), channel_id=1, source_target_pairs={{0,1},{1,2},{2,3},{3,4},{4,5},{5,6},{6,7},{7,8},{8,9},{9,10},{10,1... | collective-permute-start | bytes 589832 | tf_op jit(solution)/shard_map/ppermute | solution.py:21
  57.8 23.6 %all-to-all-start = ((f32[64,1,640]{2,1,0:T(1,128)}), f32[64,1,640]{2,1,0:T(1,128)S(1)}, u32[]{:S(2)}, u32[]{:S(2)}) async-start(f32[64,1,640]{2,1,0:T(1,128)} %shard_map.63), calls=%async_computation | async-start | bytes 327680 | tf_op jit(solution)/shard_map/all_to_all | solution.py:236
